TPU v7x, 256 devices: a whole 4x4x8 slice. The times are simulated.
256 devices in a mesh: slab: 32 (over x, z), rows: 8 (over y, core).
Axes of the slice: x: 4, y: 4, z: 8, core: 2. Of those that a mesh axis runs over, the one named last changes fastest.
Arguments:
- blocks: float32 [1536, 64, 4096], P(('slab', 'rows')), may hold values from -6 to 6
- coords: int32 [1536, 3], P(('slab', 'rows')), may hold values from 0 to 255, as said below
- counts: int32 [256], P(('slab', 'rows')), may hold values from 0 to 6, as said below
- factor_b: float32 [16384, 64], P('rows'), may hold values from -0.055242717 to 0.055242717
- factor_c: float32 [16384, 64], P(('slab', 'rows')), may hold values from -0.055242717 to 0.055242717
Outputs:
- factor_a_new: float32 [16384, 64], P('rows')
- factor_b_new: float32 [16384, 64], P('rows')
- scale_b: float32 [64], replicated
Inputs may be any that keep to these rules, and one draw needn't show every extreme that they name: Slot k of device d holds part of the tensor when k < counts[d]; the other slots hold data that is not part of it. In every draw some device has all 6 slots live. `coords`: every slot of the device with index g along rows (in the joined slab+rows order, slab slowest) has its first two coordinates in the range from g * 16384 // (64 * the number of devices along rows) up to the next such bound; the third coordinate is free.
All inputs are finite; a program needn't handle non-finite values.
Results may differ from a plain program's by a relative error of at most 0.00025.
Values sent between devices are 32-bit elements; how exact they have to be, the bound alone decides.
No kernel may reach another device: no remote copies, remote signals or barrier semaphores. Data moves between devices by JAX's collectives and lax.ppermute only.
A program may use at most 64 MiB of HBM per device.

v0:
```python
import jax
import jax.numpy as jnp
from jax import lax
from jax.sharding import PartitionSpec as P


def apply_inverse(rows, gram):
    chol = jnp.linalg.cholesky(gram)
    inner = lax.linalg.triangular_solve(chol, rows, left_side=False, lower=True, transpose_a=True)
    return lax.linalg.triangular_solve(chol, inner, left_side=False, lower=True, transpose_a=False)


def contract(ranges, first, third, mode, base):
    side = ranges[0][0].shape[1]
    rank = first.shape[1]
    partial_value = jnp.zeros((first.shape[0], rank), jnp.float32)
    for stored, places, lower, upper in ranges:

        def step(slot, acc):
            block = lax.dynamic_index_in_dim(stored, slot, 0, keepdims=False)
            place = lax.dynamic_index_in_dim(places, slot, 0, keepdims=False)
            third_rows = lax.dynamic_slice_in_dim(third, place[2] * side, side, 0)
            folded = jnp.dot(
                block.reshape(side * side, side),
                third_rows,
                precision=lax.Precision.HIGHEST,
                preferred_element_type=jnp.float32,
            ).reshape(side, side, rank)
            if mode == 1:
                second = lax.dynamic_slice_in_dim(first, place[1] * side - base, side, 0)
                term = jnp.einsum("ijr,jr->ir", folded, second, precision=lax.Precision.HIGHEST)
                target = place[0] * side - base
            else:
                second = lax.dynamic_slice_in_dim(first, place[0] * side - base, side, 0)
                term = jnp.einsum("ijr,ir->jr", folded, second, precision=lax.Precision.HIGHEST)
                target = place[1] * side - base
            current = lax.dynamic_slice_in_dim(acc, target, side, 0)
            return lax.dynamic_update_slice_in_dim(acc, current + term, target, 0)

        partial_value = lax.fori_loop(lower, upper, step, partial_value)
    return partial_value


def solve_update(partial_value, gram, total_rows, last):
    high = lax.Precision.HIGHEST
    owned = lax.psum_scatter(partial_value, "slab", scatter_dimension=0, tiled=True)
    solved = apply_inverse(owned, gram)
    squares = lax.psum(jnp.sum(solved * solved, axis=0), ("slab", "rows"))
    scale = jnp.sqrt(squares / total_rows + 1e-06)
    updated = solved / scale
    group = lax.all_gather(updated, "slab", axis=0, tiled=True)
    next_gram = None
    if not last:
        next_gram = lax.psum(
            jnp.dot(updated.T, updated, precision=high, preferred_element_type=jnp.float32),
            ("slab", "rows"),
        )
    return (group, next_gram, scale)


def shards(blocks, coords, counts, factor_b, factor_c):
    high = lax.Precision.HIGHEST
    group_rows = factor_b.shape[0]
    total_rows = group_rows * lax.axis_size("rows")
    base = lax.axis_index("rows") * group_rows
    gram_b = lax.psum(
        jnp.dot(factor_b.T, factor_b, precision=high, preferred_element_type=jnp.float32), "rows"
    )
    full_c = lax.all_gather(factor_c, ("slab", "rows"), axis=0, tiled=True)
    gram_c = jnp.dot(full_c.T, full_c, precision=high, preferred_element_type=jnp.float32)
    count_own = counts[0]
    ranges = [(blocks, coords, jnp.int32(0), count_own)]
    partial_a = contract(ranges, factor_b, full_c, 1, base)
    group_a, gram_a, scale_a = solve_update(partial_a, gram_b * gram_c, total_rows, False)
    partial_b = contract(ranges, group_a, full_c, 2, base)
    group_b, unused_gram, scale_b = solve_update(partial_b, gram_a * gram_c, total_rows, True)
    return (group_a, group_b, scale_b)


def solution(mesh):
    in_specs = (
        P(("slab", "rows"), None, None),
        P(("slab", "rows"), None),
        P(("slab", "rows")),
        P("rows", None),
        P(("slab", "rows"), None),
    )
    out_specs = (P("rows", None), P("rows", None), P())
    return jax.shard_map(shards, mesh=mesh, in_specs=in_specs, out_specs=out_specs, check_vma=False)
```

profile of v0, /device:TPU:1, one launch (start us, length us, event | category | flops | bytes accessed | tf_op | source)
XLA Modules:
  0.0 931.3 jit_solution(10876942208482262396)
XLA Ops:
  8.0 1.9 fusion.19
  9.9 23.8 %psum.28 = f32[64,64]{0,1:T(8,128)S(1)} all-reduce(f32[64,64]{0,1:T(8,128)S(1)} %fusion.19), channel_id=1, replica_groups=mesh['slab'=32,'rows'=8] {'rows'}, use_global_device_ids=true, to_apply=%region_0.0 | all-reduce | flops 4096 | bytes 32768 | tf_op jit(solution)/shard_map/psum | solution.py:66
  33.7 100.5 %all-gather.2.cloned.1.call-done = f32[16384,64]{1,0:T(8,128)} async-done(((f32[64,64]{1,0:T(8,128)}), f32[16384,64]{1,0:T(8,128)}) %all-gather.2.cloned.1.call-update) | async-done | bytes 4194320 | tf_op jit(solution)/shard_map/all_gather | solution.py:69
  134.3 1.1 broadcast.53.clone
  135.4 31.6 %while.20 = (s32[]{:T(128)}, f32[2048,64]{1,0:T(8,128)}, s32[]{:T(128)}, s32[6,3]{0,1:T(4,128)S(1)}, s32[]{:T(128)}, /*index=5*/f32[2048,64]{0,1:T(8,128)}, f32[...) while((s32[]{:T(128)}, f32[2048,64]{1,0:T(8,128)}, ...), condition=%wide.region_4.6_spmd, body=%wide.region_3.5_spmd.sunk | while | flops 201850896 | bytes 5456269 | solution.py:40
  137.4 0.8 dynamic-slice_bitcast_fusion.4
  139.0 1.3 constant_dynamic-slice_fusion.9
  140.3 0.8 dot_general.30
  141.1 2.6 multiply_reduce_fusion.6
  144.3 1.4 fusion.44
  147.7 0.8 dynamic-slice_bitcast_fusion.4
  149.3 1.3 constant_dynamic-slice_fusion.9
  150.6 0.8 dot_general.30
  151.4 2.6 multiply_reduce_fusion.6
  154.6 1.4 fusion.44
  158.0 0.8 dynamic-slice_bitcast_fusion.4
  159.6 1.3 constant_dynamic-slice_fusion.9
  160.9 0.8 dot_general.30
  161.8 2.6 multiply_reduce_fusion.6
  164.9 1.4 fusion.44
  167.2 19.5 %fusion.18 = (f32[64,64]{0,1:T(8,128)S(1)}, f32[64,64]{0,1:T(8,128)S(1)}) fusion(f32[64,64]{0,1:T(8,128)S(1)} %psum.28, f32[16384,64]{1,0:T(8,128)} %get-tuple-element.341), kind=kOutput, calls=%fused_computation.48 | convolution fusion | flops 805310464 | bytes 4243456 | tf_op jit(solution)/shard_map/dot_general | solution.py:70
  186.8 5.8 cholesky.44
  194.0 4.9 custom-call.11
  198.9 204.6 %reduce-scatter.3.cloned.1.call-done = f32[64,64]{1,0:T(8,128)} async-done(((f32[2048,64]{1,0:T(8,128)}), f32[64,64]{1,0:T(8,128)}) %reduce-scatter.3.cloned.1.call-update) | async-done | bytes 16400 | tf_op jit(solution)/shard_map/reduce_scatter | solution.py:46
  403.5 1.0 convolution_bitcast_fusion.3
  404.7 79.7 %psum.29 = f32[64]{0:T(128)S(1)} all-reduce(f32[64]{0:T(128)S(1)} %get-tuple-element.137), channel_id=1, replica_groups=mesh['slab'=32,'rows'=8] {'slab','rows'}, use_global_device_ids=true, to_apply=%region_7.0 | all-reduce | flops 64 | bytes 512 | tf_op jit(solution)/shard_map/psum | solution.py:48
  484.5 41.6 %all_gather.10 = f32[2048,64]{1,0:T(8,128)} all-gather(f32[64,64]{1,0:T(8,128)S(1)} %broadcast_divide_fusion.1), channel_id=1, replica_groups=mesh['slab'=32,'rows'=8] {'slab'}, dimensions={0}, use_global_device_ids=true | all-gather | bytes 540672 | tf_op jit(solution)/shard_map/all_gather | solution.py:51
  526.1 1.0 broadcast.53
  527.1 31.0 %while.21 = (s32[]{:T(128)}, f32[2048,64]{1,0:T(8,128)}, s32[]{:T(128)}, s32[6,3]{0,1:T(4,128)S(1)}, s32[]{:T(128)}, /*index=5*/f32[2048,64]{1,0:T(8,128)}, f32[...) while((s32[]{:T(128)}, f32[2048,64]{1,0:T(8,128)}, ...), condition=%wide.region_10.0_spmd, body=%wide.region_9.0_spmd.sunk | while | flops 201850896 | bytes 5423501 | solution.py:40
  530.7 1.3 constant_dynamic-slice_fusion.11
  532.0 0.8 dot_general.31
  532.8 2.5 multiply_reduce_fusion.7
  536.1 1.4 fusion.48
  540.7 1.3 constant_dynamic-slice_fusion.11
  542.9 2.5 multiply_reduce_fusion.7
  546.1 1.4 fusion.48
  550.8 1.3 constant_dynamic-slice_fusion.11
  552.9 2.5 multiply_reduce_fusion.7
  556.2 1.4 fusion.48
  558.2 2.3 copy.14
  560.8 115.8 %psum.30 = f32[64,64]{0,1:T(8,128)S(1)} all-reduce(f32[64,64]{0,1:T(8,128)S(1)} %fusion.20), channel_id=1, replica_groups=mesh['slab'=32,'rows'=8] {'slab','rows'}, use_global_device_ids=true, to_apply=%region_8.0 | all-reduce | flops 4096 | bytes 32768 | tf_op jit(solution)/shard_map/psum | solution.py:54
  676.7 5.8 cholesky.55
  683.9 4.9 custom-call.13
  688.8 116.1 %reduce-scatter.5.cloned.1.call-done = f32[64,64]{1,0:T(8,128)} async-done(((f32[2048,64]{1,0:T(8,128)}), f32[64,64]{1,0:T(8,128)}) %reduce-scatter.5.cloned.1.call-update) | async-done | bytes 16400 | tf_op jit(solution)/shard_map/reduce_scatter | solution.py:46
  804.9 1.0 convolution_bitcast_fusion.1
  806.1 79.7 %psum.31 = f32[64]{0:T(128)S(1)} all-reduce(f32[64]{0:T(128)S(1)} %get-tuple-element.139), channel_id=1, replica_groups=mesh['slab'=32,'rows'=8] {'slab','rows'}, use_global_device_ids=true, to_apply=%region_13.17 | all-reduce | flops 64 | bytes 512 | tf_op jit(solution)/shard_map/psum | solution.py:48
  885.8 37.8 %all_gather.11 = f32[2048,64]{1,0:T(8,128)S(1)} all-gather(f32[64,64]{1,0:T(8,128)S(1)} %broadcast_divide_fusion), channel_id=1, replica_groups=mesh['slab'=32,'rows'=8] {'slab'}, dimensions={0}, use_global_device_ids=true | all-gather | bytes 540672 | tf_op jit(solution)/shard_map/all_gather | solution.py:51
  923.7 1.1 copy.15
  (48 shorter events, 12.8 us)
Async XLA Ops:
  7.2 128.2 %copy-start = (s32[6,3]{0,1:T(4,128)S(1)}, s32[6,3]{0,1:T(4,128)}, u32[]{:S(2)}) copy-start(s32[6,3]{0,1:T(4,128)} %param.15) | copy-start | bytes 220
  7.2 127.1 %all-gather.2.cloned.1.call-start = ((), (), s32[]{:S(2)}) async-start(), calls=%async_computation.2 | async-start | bytes 8421376 | tf_op jit(solution)/shard_map/all_gather | solution.py:69
  7.9 395.6 %reduce-scatter.3.cloned.1.call-start = ((), (), s32[]{:S(2)}) async-start(), calls=%async_computation.3 | async-start | bytes 1081344 | tf_op jit(solution)/shard_map/reduce_scatter | solution.py:46
  167.0 637.9 %reduce-scatter.5.cloned.1.call-start = ((), (), s32[]{:S(2)}) async-start(), calls=%async_computation.4 | async-start | bytes 1081344 | tf_op jit(solution)/shard_map/reduce_scatter | solution.py:46
  885.8 39.0 %copy-start.1 = (f32[64]{0:T(128)}, f32[64]{0:T(128)S(1)}, u32[]{:S(2)}) copy-start(f32[64]{0:T(128)S(1)} %add_sqrt_fusion) | copy-start | bytes 772
Sparse Core Ops, SparseCore 0:
  11.7 122.4 all-gather.1
  167.1 236.3 reduce-scatter.2
  558.3 246.4 reduce-scatter.4
where the time goes:
time: 944 us; the launch traced here: 931 us
  waiting for transfers between devices  422 us (45%)
  blocking collectives  379 us (40%)
  matrix products  39.4 us (4%)
  other arithmetic  32.4 us (3%)
  local copies, waits for them, and re-layouts  27.6 us (3%)
  loops' own time  17.3 us (2%)
  between operations  13.9 us (1%)
    reduce_scatter x2, waiting for transfers between devices, solve_update(): lax.psum_scatter(partial_value, 'slab', scatter_dimension=0, tiled=True)  321 us
    psum x2, blocking collectives, solve_update(): squares = lax.psum(jnp.sum(solved * solved, axis=0), ('slab', 'rows'))  159 us
    psum x1, blocking collectives, solve_update(): lax.psum(jnp.dot(updated.T, updated, precision=high, preferred_element_ty...  116 us
    all_gather x1, waiting for transfers between devices, shards(): full_c = lax.all_gather(factor_c, ('slab', 'rows'), axis=0, tiled=True)  101 us
    all_gather x2, blocking collectives, solve_update(): group = lax.all_gather(updated, 'slab', axis=0, tiled=True)  79.5 us
    psum x1, blocking collectives, shards(): lax.psum(jnp.dot(factor_b.T, factor_b, precision=high, preferred_element_...  23.8 us
    dot_general x1, matrix products, shards(): jnp.dot(full_c.T, full_c, precision=high, preferred_element_type=jnp.floa...  19.5 us
  transfers between devices with their start and end apart: 3, of which 3 were waited for; matrix products, arithmetic and copies ran while one was open for 5% of the time, Pallas kernels for 0%

commit v1 on v0

v1 whole, which is shorter than its diff:
```python
import jax
import jax.numpy as jnp
from jax import lax
from jax.experimental import pallas as pl
from jax.experimental.pallas import tpu as pltpu
from jax.sharding import PartitionSpec as P

SIDE = 64
HALF = 32
WIDE = 128
SLOTS = 6
PEERS = 8
OWNERS = 32
GROUP = 2048
ROWS = 16384
HIGH = lax.Precision.HIGHEST
LIMIT = pltpu.CompilerParams(vmem_limit_bytes=48 * 1024 * 1024)


def low(shape):
    return lax.broadcasted_iota(jnp.int32, shape, 1) < SIDE


def swap(x):
    return pltpu.roll(x, SIDE, 1)


def unfold_halves(packed):
    mask, other = low(packed.shape), swap(packed)
    return jnp.concatenate([jnp.where(mask, packed, other), jnp.where(mask, other, packed)], axis=0)


def fold_halves(rows):
    return jnp.where(low((HALF, WIDE)), rows[:HALF], rows[HALF:])


def gram_packed(packed):
    both = lax.dot_general(
        packed, packed, (((0,), (0,)), ((), ())), precision=HIGH, preferred_element_type=jnp.float32
    )
    total = both[:SIDE] + swap(both[SIDE:])
    return jnp.where(low(total.shape), total, swap(total))


def inverse(gram):
    shape = gram.shape
    row = lax.broadcasted_iota(jnp.int32, shape, 0)
    lane = lax.broadcasted_iota(jnp.int32, shape, 1)
    work = jnp.where(lane < SIDE, gram, jnp.where(lane - SIDE == row, 1.0, 0.0))
    for k in range(SIDE):
        line = work[k : k + 1, :] / work[k : k + 1, k : k + 1]
        column = work[:, k : k + 1]
        work = jnp.where(row == k, line, work - column * line)
    return work


def prepare(second_ref, third_ref, spread_ref, gram_ref):
    second = second_ref[...]
    twice = jnp.concatenate([second, second], axis=0)
    gram_ref[...] = lax.dot_general(
        second, twice, (((1,), (1,)), ((), ())), precision=HIGH, preferred_element_type=jnp.float32
    )
    third = third_ref[...]
    packed = jnp.concatenate([third[:HALF], third[HALF:]], axis=1)
    spread_ref[...] = jnp.broadcast_to(packed[None], spread_ref.shape)


def answer(asked_ref, third_ref, gram_ref, out_ref):
    for peer in range(PEERS):
        for slot in range(SLOTS):
            block = asked_ref[peer, slot] // PEERS
            out_ref[peer, slot * HALF : (slot + 1) * HALF, :] = third_ref[block]
    third = third_ref[...].reshape(OWNERS * HALF, WIDE)
    grams = jnp.where(low((SIDE, WIDE)), gram_ref[...], gram_packed(third))
    out_ref[:, SLOTS * HALF :, :] = jnp.broadcast_to(grams[None], (PEERS, SIDE, WIDE))


def split(x):
    high = x.astype(jnp.bfloat16)
    return high, (x - high.astype(jnp.float32)).astype(jnp.bfloat16)


def fold(
    place_ref, count_ref, block_ref, third_ref, second_ref, folded_ref, part_ref, inverse_ref, gram_ref, turned
):
    slot = pl.program_id(0)

    @pl.when(slot == 0)
    def _():
        part_ref[...] = jnp.zeros_like(part_ref)
        grams = jnp.sum(third_ref[:, SLOTS * HALF :, :], axis=0)
        mask = low(grams.shape)
        other = swap(grams)
        gram_ref[...] = jnp.where(mask, other, grams)
        solved = inverse(grams * other)
        inverse_ref[:SIDE, :] = jnp.where(mask, swap(solved), 0.0)
        inverse_ref[SIDE:, :] = jnp.where(mask, 0.0, solved)

    @pl.when(slot < count_ref[0])
    def _():
        which = place_ref[slot, 2]
        packed = third_ref[which % PEERS, pl.ds(slot * HALF, HALF), :]
        mask, other = low(packed.shape), swap(packed)
        zero = jnp.zeros_like(packed)
        twin = jnp.concatenate(
            [
                jnp.where(mask, packed, zero),
                jnp.where(mask, other, zero),
                jnp.where(mask, zero, other),
                jnp.where(mask, zero, packed),
            ],
            axis=0,
        )
        high, rest = split(twin)
        weights = jnp.concatenate([high, rest], axis=1)
        weights = jnp.concatenate([weights, weights], axis=0)
        place = place_ref[slot, 1] % OWNERS
        tile = second_ref[:, pl.ds(pl.multiple_of(place // 2 * WIDE, WIDE), WIDE)]
        turned[...] = jnp.concatenate([tile, tile], axis=0).T
        start = place % 2 * SIDE
        pairs = jnp.where(
            mask, turned[pl.ds(start, HALF, stride=2), :], turned[pl.ds(start + 1, HALF, stride=2), :]
        )
        total = jnp.zeros((SIDE, WIDE), jnp.float32)
        step = 8
        for at in range(0, HALF, step):
            lines = jnp.concatenate(
                [block_ref[0, :, (at + n) * WIDE : (at + n + 1) * WIDE] for n in range(step)], axis=0
            )
            high, rest = split(lines)
            lines = jnp.concatenate([high, rest], axis=1)
            product = jnp.dot(lines, weights, preferred_element_type=jnp.float32)
            product = product[:, :WIDE] + product[:, WIDE:]
            for n in range(step):
                piece = product[n * SIDE : (n + 1) * SIDE]
                folded_ref[0, at + n] = piece
                total += piece * pairs[at + n : at + n + 1, :]
        total = total + swap(total)
        part_ref[place_ref[slot, 0] % OWNERS] += fold_halves(total)


def solve_first(part_ref, inverse_ref, out_ref):
    total = jnp.sum(part_ref[...], axis=0)
    solved = jnp.dot(total, inverse_ref[...], precision=HIGH, preferred_element_type=jnp.float32)
    out_ref[...] = jnp.broadcast_to(solved[None], out_ref.shape)


def contract(place_ref, count_ref, folded_ref, first_ref, part_ref, square_ref):
    slot = pl.program_id(0)

    @pl.when(slot == 0)
    def _():
        part_ref[...] = jnp.zeros_like(part_ref)
        square = fold_halves(gram_packed(first_ref[...].reshape(OWNERS * HALF, WIDE)))
        square_ref[...] = jnp.broadcast_to(square[None], square_ref.shape)

    @pl.when(slot < count_ref[0])
    def _():
        first = unfold_halves(first_ref[place_ref[slot, 0] % OWNERS])
        term = jnp.sum(folded_ref[0] * first[None], axis=1)
        part_ref[place_ref[slot, 1] % OWNERS] += term


def solve_second(part_ref, square_ref, gram_ref, first_ref, out_ref, new_ref, spread):
    square = unfold_halves(jnp.sum(square_ref[...], axis=0))
    shape = square.shape
    row = lax.broadcasted_iota(jnp.int32, shape, 0)
    lane = lax.broadcasted_iota(jnp.int32, shape, 1)
    means = jnp.where(row == lane % SIDE, square, 0.0) / ROWS
    along = jnp.sqrt(jnp.sum(means, axis=0, keepdims=True) + 1e-06)
    down = jnp.sqrt(jnp.sum(jnp.where(lane < SIDE, means, 0.0), axis=1, keepdims=True) + 1e-06)
    gram = square / along / down * gram_ref[...]
    inverted = swap(inverse(gram))[:, :SIDE]
    total = jnp.sum(part_ref[...], axis=0) / along
    spread[pl.ds(0, HALF, stride=2), :] = total
    spread[pl.ds(1, HALF, stride=2), :] = swap(total)
    rows = spread[:, :SIDE]
    rows = jnp.concatenate([rows, rows], axis=0)
    solved = lax.dot_general(
        inverted, rows, (((1,), (1,)), ((), ())), precision=HIGH, preferred_element_type=jnp.float32
    )
    out_ref[...] = jnp.broadcast_to(fold_halves(solved)[None], out_ref.shape)
    for pair in range(OWNERS // 2):
        left, right = unfold_halves(first_ref[2 * pair]), unfold_halves(first_ref[2 * pair + 1])
        both = jnp.concatenate([left, right], axis=0).T[:SIDE]
        new_ref[:, pair * WIDE : (pair + 1) * WIDE] = both / down


def squares(solved_ref, out_ref):
    solved = solved_ref[...]
    out_ref[...] = jnp.broadcast_to(jnp.sum(solved * solved, axis=0)[None], out_ref.shape)


def finish(solved_ref, square_ref, new_ref, scale_ref):
    total = jnp.sum(square_ref[...], axis=0)
    mask = low(total.shape)
    left = jnp.sum(jnp.where(mask, total, 0.0), axis=1, keepdims=True)
    right = jnp.sum(jnp.where(mask, 0.0, total), axis=1, keepdims=True)
    down = jnp.sqrt(jnp.concatenate([left, right], axis=0) / ROWS + 1e-06)
    shape = (SIDE, SIDE)
    eye = lax.broadcasted_iota(jnp.int32, shape, 0) == lax.broadcasted_iota(jnp.int32, shape, 1)
    scale_ref[...] = jnp.sum(jnp.where(eye, jnp.broadcast_to(down, shape), 0.0), axis=0, keepdims=True)
    for pair in range(OWNERS // 2):
        left, right = solved_ref[2 * pair], solved_ref[2 * pair + 1]
        upper = jnp.where(mask, left, swap(right))
        lower = jnp.where(mask, swap(left), right)
        both = jnp.concatenate([upper, lower], axis=0)
        new_ref[:, pair * WIDE : (pair + 1) * WIDE] = both / down


def struct(*shape):
    return jax.ShapeDtypeStruct(shape, jnp.float32)


def exchange(x, axis):
    return lax.all_to_all(x, axis, 0, 0, tiled=True)


def whole(*shape):
    return pl.BlockSpec(shape, lambda slot, *_: (0,) * len(shape))


def shards(blocks, coords, counts, factor_b, factor_c):
    second = factor_b.T
    spread, gram_b = pl.pallas_call(
        prepare, out_shape=(struct(OWNERS, HALF, WIDE), struct(SIDE, WIDE)), compiler_params=LIMIT
    )(second, factor_c)
    asked = exchange(jnp.broadcast_to(coords[None, :, 2], (PEERS, SLOTS)), "rows")
    held = exchange(spread, "slab")
    answers = pl.pallas_call(
        answer,
        grid_spec=pltpu.PrefetchScalarGridSpec(
            num_scalar_prefetch=1,
            grid=(1,),
            in_specs=[whole(OWNERS, HALF, WIDE), whole(SIDE, WIDE)],
            out_specs=whole(PEERS, SLOTS * HALF + SIDE, WIDE),
        ),
        out_shape=struct(PEERS, SLOTS * HALF + SIDE, WIDE),
        compiler_params=LIMIT,
    )(asked, held, gram_b)
    third = exchange(answers, "rows")
    folded, part_a, inverse_a, gram_c = pl.pallas_call(
        fold,
        grid_spec=pltpu.PrefetchScalarGridSpec(
            num_scalar_prefetch=2,
            grid=(SLOTS,),
            in_specs=[
                pl.BlockSpec((1, SIDE, SIDE * SIDE), lambda slot, *_: (slot, 0, 0)),
                whole(PEERS, SLOTS * HALF + SIDE, WIDE),
                whole(SIDE, GROUP),
            ],
            out_specs=[
                pl.BlockSpec((1, HALF, SIDE, WIDE), lambda slot, *_: (slot, 0, 0, 0)),
                whole(OWNERS, HALF, WIDE),
                whole(WIDE, WIDE),
                whole(SIDE, WIDE),
            ],
            scratch_shapes=[pltpu.VMEM((WIDE, WIDE), jnp.float32)],
        ),
        out_shape=(
            struct(SLOTS, HALF, SIDE, WIDE),
            struct(OWNERS, HALF, WIDE),
            struct(WIDE, WIDE),
            struct(SIDE, WIDE),
        ),
        compiler_params=LIMIT,
    )(coords, counts, blocks, third, second)
    solved_a = pl.pallas_call(solve_first, out_shape=struct(OWNERS, HALF, WIDE), compiler_params=LIMIT)(
        exchange(part_a, "slab"), inverse_a
    )
    group_a = exchange(solved_a, "slab")
    part_b, square_a = pl.pallas_call(
        contract,
        grid_spec=pltpu.PrefetchScalarGridSpec(
            num_scalar_prefetch=2,
            grid=(SLOTS,),
            in_specs=[
                pl.BlockSpec((1, HALF, SIDE, WIDE), lambda slot, *_: (slot, 0, 0, 0)),
                whole(OWNERS, HALF, WIDE),
            ],
            out_specs=[whole(OWNERS, HALF, WIDE), whole(PEERS, HALF, WIDE)],
        ),
        out_shape=(struct(OWNERS, HALF, WIDE), struct(PEERS, HALF, WIDE)),
        compiler_params=LIMIT,
    )(coords, counts, folded, group_a)
    square_a = exchange(square_a, "rows")
    solved_b, new_a = pl.pallas_call(
        solve_second,
        out_shape=(struct(OWNERS, HALF, WIDE), struct(SIDE, GROUP)),
        scratch_shapes=[pltpu.VMEM((SIDE, WIDE), jnp.float32)],
        compiler_params=LIMIT,
    )(exchange(part_b, "slab"), square_a, gram_c, group_a)
    group_b = exchange(solved_b, "slab")
    square_b = pl.pallas_call(squares, out_shape=struct(PEERS, HALF, WIDE), compiler_params=LIMIT)(group_b)
    new_b, scale_b = pl.pallas_call(
        finish, out_shape=(struct(SIDE, GROUP), struct(1, SIDE)), compiler_params=LIMIT
    )(group_b, exchange(square_b, "rows"))
    return (new_a.T, new_b.T, scale_b.reshape(SIDE))


def solution(mesh):
    in_specs = (
        P(("slab", "rows"), None, None),
        P(("slab", "rows"), None),
        P(("slab", "rows")),
        P("rows", None),
        P(("slab", "rows"), None),
    )
    out_specs = (P("rows", None), P("rows", None), P())
    return jax.shard_map(shards, mesh=mesh, in_specs=in_specs, out_specs=out_specs, check_vma=False)
```

time: 944 us -> 197 us (0.21); the launches traced: 931 us -> 197 us
  waiting for transfers between devices: 422 us -> 15.2 us
  blocking collectives: 379 us -> 131 us
  matrix products: 39.4 us -> 0 us
  other arithmetic: 32.4 us -> 0 us
  Pallas kernels: 0 us -> 31.1 us
  local copies, waits for them, and re-layouts: 27.6 us -> 4.89 us
  loops' own time: 17.3 us -> 0 us
  starting transfers between devices: 0.3 us -> 13.5 us
  between operations: 13.9 us -> 1.31 us
    reduce_scatter x2 -> x0, waiting for transfers between devices: 321 us -> none  [solve_update(): lax.psum_scatter(partial_value, 'slab', scatter_dimension=0, tiled=True)]
    psum x4 -> x0, blocking collectives: 299 us -> none  [the longest x2 159 us: solve_update(): squares = lax.psum(jnp.sum(solved * solved, axis=0), ('slab', 'rows'))]
    all_to_all x0 -> x7, blocking collectives: none -> 131 us  [exchange(): return lax.all_to_all(x, axis, 0, 0, tiled=True)]
    all_gather x1 -> x0, waiting for transfers between devices: 101 us -> none  [shards(): full_c = lax.all_gather(factor_c, ('slab', 'rows'), axis=0, tiled=True)]
    all_gather x2 -> x0, blocking collectives: 79.5 us -> none  [solve_update(): group = lax.all_gather(updated, 'slab', axis=0, tiled=True)]
    dot_general x9 -> x0, matrix products: 36.9 us -> none  [the longest x1 19.5 us: shards(): jnp.dot(full_c.T, full_c, precision=high, preferred_element_type=jnp.floa...]
    pallas_call x0 -> x8, Pallas kernels: none -> 31.1 us  [the longest x1 13.4 us: shards(): pl.pallas_call(fold, grid_spec=pltpu.PrefetchScalarGridSpec(num_scalar_pr...]
    another operation x10 -> x0, other arithmetic: 24.1 us -> none  [the longest x6 13 us: apply_inverse(): chol = jnp.linalg.cholesky(gram)]
  transfers between devices with their start and end apart: 3 -> 2, of which waited for: 3 -> 2; matrix products, arithmetic and copies ran while one was open for 5% -> 0% of each run, Pallas kernels for 0% -> 1%
where the time goes in v1:
time: 197 us
  blocking collectives  131 us (66%)
  Pallas kernels  31.1 us (16%)
  waiting for transfers between devices  15.2 us (8%)
  starting transfers between devices  13.5 us (7%)
  local copies, waits for them, and re-layouts  4.89 us (2%)
    all_to_all x7, blocking collectives, exchange(): return lax.all_to_all(x, axis, 0, 0, tiled=True)  131 us
    all_to_all x2, waiting for transfers between devices, exchange(): return lax.all_to_all(x, axis, 0, 0, tiled=True)  15.2 us
    all_to_all x2, starting transfers between devices, exchange(): return lax.all_to_all(x, axis, 0, 0, tiled=True)  13.5 us
    pallas_call x1, Pallas kernels, shards(): pl.pallas_call(fold, grid_spec=pltpu.PrefetchScalarGridSpec(num_scalar_pr...  13.4 us
    pallas_call x1, Pallas kernels, shards(): pl.pallas_call(solve_second, out_shape=(struct(OWNERS, HALF, WIDE), struc...  6.96 us
    pallas_call x1, Pallas kernels, shards(): pl.pallas_call(contract, grid_spec=pltpu.PrefetchScalarGridSpec(num_scala...  5.68 us
  transfers between devices with their start and end apart: 2, of which 2 were waited for; matrix products, arithmetic and copies ran while one was open for 0% of the time, Pallas kernels for 1%

profile of v1, /device:TPU:1, one launch (start us, length us, event | category | flops | bytes accessed | tf_op | source)
XLA Modules:
  0.0 196.5 jit_solution(15884147706440503123)
XLA Ops:
  0.6 0.7 slice_bitcast_fusion
  1.3 0.6 broadcast_in_dim.8
  1.9 6.5 %all-to-all-start = ((s32[8,1,6]{2,1,0:T(1,128)}), s32[8,1,6]{2,1,0:T(1,128)S(1)}, u32[]{:S(2)}, u32[]{:S(2)}) async-start(s32[8,1,6]{2,1,0:T(1,128)} %broadcast_in_dim.8), calls=%async_computation | async-start | bytes 8192 | tf_op jit(solution)/shard_map/all_to_all | solution.py:216
  8.4 0.0 copy-start
  8.4 1.0 copy-done
  9.4 0.0 copy-start.2
  9.4 0.8 copy-done.2
  10.2 1.2 shard_map.76
  11.4 1.5 all-to-all-done
  12.9 24.6 %all_to_all.48.third_ref = f32[32,32,128]{2,1,0:T(8,128)S(1)} all-to-all(f32[32,32,128]{2,1,0:T(8,128)S(1)} %get-tuple-element.15), channel_id=1, replica_groups=mesh['slab'=32,'rows'=8] {'slab'}, dimensions={0} | all-to-all | bytes 1048576 | tf_op jit(solution)/shard_map/all_to_all | solution.py:216
  37.5 2.5 %shard_map.77 = f32[8,256,128]{2,1,0:T(8,128)} custom-call(s32[8,6]{1,0:T(8,128)S(1)} %bitcast.9, f32[32,32,128]{2,1,0:T(8,128)S(1)} %all_to_all.48.third_ref, f32[64,128]{1,0:T(8,128)S(1)} %get-tuple-element.16.gram_ref), custom_call_target="tpu_custom_call" | custom-call | tf_op jit(solution)/shard_map/pallas_call | solution.py:230
  40.0 7.0 %all-to-all-start.2 = ((f32[8,256,128]{2,1,0:T(8,128)}), f32[8,256,128]{2,1,0:T(8,128)S(1)}, u32[]{:S(2)}, u32[]{:S(2)}) async-start(f32[8,256,128]{2,1,0:T(8,128)} %shard_map.77), calls=%async_computation.2 | async-start | bytes 2097152 | tf_op jit(solution)/shard_map/all_to_all | solution.py:216
  47.0 0.8 copy.11.place_ref
  48.4 13.7 %all-to-all-done.2.third_ref = f32[8,256,128]{2,1,0:T(8,128)S(1)} async-done(((f32[8,256,128]{2,1,0:T(8,128)}), f32[8,256,128]{2,1,0:T(8,128)S(1)}, u32[]{:S(2)}, u32[]{:S(2)}) %all-to-all-start.2) | async-done | bytes 1048608 | tf_op jit(solution)/shard_map/all_to_all | solution.py:216
  62.1 0.0 copy-start.1
  62.1 1.0 copy-done.1
  63.2 13.4 %shard_map.78 = (f32[6,32,64,128]{3,2,1,0:T(8,128)}, f32[32,32,128]{2,1,0:T(8,128)S(1)}, f32[128,128]{1,0:T(8,128)S(1)}, f32[64,128]{1,0:T(8,128)S(1)}) custom-call(s32[6,3]{1,0:T(8,128)S(1)} %copy.11.place_ref, s32[1]{0:T(128)S(6)} %copy.12.count_ref, f32[6,64,4096]{2,1,0:T(8,128)} %block_ref.1, f32[8,256,128]{2,1,0:T(8,128)S(1)} %all-to-all-done.2.third_ref, ...), custom_call_target="tpu_custom_call" | custom-call | tf_op jit(solution)/shard_map/pallas_call | solution.py:242
  76.6 19.9 %all_to_all.49.part_ref = f32[32,32,128]{2,1,0:T(8,128)S(1)} all-to-all(f32[32,32,128]{2,1,0:T(8,128)S(1)} %get-tuple-element.18), channel_id=1, replica_groups=mesh['slab'=32,'rows'=8] {'slab'}, dimensions={0} | all-to-all | bytes 1048576 | tf_op jit(solution)/shard_map/all_to_all | solution.py:216
  96.5 0.2 shard_map.79
  96.8 22.0 %all_to_all.50.first_ref = f32[32,32,128]{2,1,0:T(8,128)S(1)} all-to-all(f32[32,32,128]{2,1,0:T(8,128)S(1)} %shard_map.79), channel_id=1, replica_groups=mesh['slab'=32,'rows'=8] {'slab'}, dimensions={0} | all-to-all | bytes 1048576 | tf_op jit(solution)/shard_map/all_to_all | solution.py:216
  118.8 5.7 %shard_map.80 = (f32[32,32,128]{2,1,0:T(8,128)S(1)}, f32[8,32,128]{2,1,0:T(8,128)S(1)}) custom-call(s32[6,3]{1,0:T(8,128)S(1)} %copy.11.place_ref, s32[1]{0:T(128)S(6)} %copy.12.count_ref, f32[6,32,64,128]{3,2,1,0:T(8,128)} %get-tuple-element.17.folded_ref, f32[32,32,128]{2,1,0:T(8,128)S(1)} %all_to_all.50.first_ref), custom_call_target="tpu_custom_call" | custom-call | tf_op jit(solution)/shard_map/pallas_call | solution.py:272
  124.5 12.0 %all_to_all.51.square_ref = f32[8,32,128]{2,1,0:T(8,128)S(1)} all-to-all(f32[8,32,128]{2,1,0:T(8,128)S(1)} %get-tuple-element.21), channel_id=1, replica_groups=mesh['slab'=32,'rows'=8] {'rows'}, dimensions={0} | all-to-all | bytes 262144 | tf_op jit(solution)/shard_map/all_to_all | solution.py:216
  136.5 18.6 %all_to_all.52.part_ref = f32[32,32,128]{2,1,0:T(8,128)S(1)} all-to-all(f32[32,32,128]{2,1,0:T(8,128)S(1)} %get-tuple-element.20), channel_id=1, replica_groups=mesh['slab'=32,'rows'=8] {'slab'}, dimensions={0} | all-to-all | bytes 1048576 | tf_op jit(solution)/shard_map/all_to_all | solution.py:216
  155.1 7.0 %shard_map.81 = (f32[32,32,128]{2,1,0:T(8,128)S(1)}, f32[64,2048]{1,0:T(8,128)}) custom-call(f32[32,32,128]{2,1,0:T(8,128)S(1)} %all_to_all.52.part_ref, f32[8,32,128]{2,1,0:T(8,128)S(1)} %all_to_all.51.square_ref, f32[64,128]{1,0:T(8,128)S(1)} %get-tuple-element.22.gram_ref, f32[32,32,128]{2,1,0:T(8,128)S(1)} %all_to_all.50.first_ref), custom_call_target="tpu_custom_call" | custom-call | tf_op jit(solution)/shard_map/pallas_call | solution.py:287
  162.0 21.2 %all_to_all.53.solved_ref = f32[32,32,128]{2,1,0:T(8,128)S(1)} all-to-all(f32[32,32,128]{2,1,0:T(8,128)S(1)} %get-tuple-element.24), channel_id=1, replica_groups=mesh['slab'=32,'rows'=8] {'slab'}, dimensions={0} | all-to-all | bytes 1048576 | tf_op jit(solution)/shard_map/all_to_all | solution.py:216
  183.2 0.1 shard_map.82
  183.3 12.2 %all_to_all.54.square_ref = f32[8,32,128]{2,1,0:T(8,128)S(1)} all-to-all(f32[8,32,128]{2,1,0:T(8,128)S(1)} %shard_map.82), channel_id=1, replica_groups=mesh['slab'=32,'rows'=8] {'rows'}, dimensions={0} | all-to-all | bytes 262144 | tf_op jit(solution)/shard_map/all_to_all | solution.py:216
  195.5 1.1 shard_map.83
Async XLA Ops:
  1.9 11.0 %all-to-all-start = ((s32[8,1,6]{2,1,0:T(1,128)}), s32[8,1,6]{2,1,0:T(1,128)S(1)}, u32[]{:S(2)}, u32[]{:S(2)}) async-start(s32[8,1,6]{2,1,0:T(1,128)} %broadcast_in_dim.8), calls=%async_computation | async-start | bytes 8192 | tf_op jit(solution)/shard_map/all_to_all | solution.py:216
  8.4 1.0 copy-start
  9.4 0.8 copy-start.2
  40.0 22.2 %all-to-all-start.2 = ((f32[8,256,128]{2,1,0:T(8,128)}), f32[8,256,128]{2,1,0:T(8,128)S(1)}, u32[]{:S(2)}, u32[]{:S(2)}) async-start(f32[8,256,128]{2,1,0:T(8,128)} %shard_map.77), calls=%async_computation.2 | async-start | bytes 2097152 | tf_op jit(solution)/shard_map/all_to_all | solution.py:216
  62.1 1.0 copy-start.1

commit v2 on v0

v2 whole, which is shorter than its diff:
```python
import jax
import jax.numpy as jnp
from jax import lax
from jax.experimental import pallas as pl
from jax.experimental.pallas import tpu as pltpu
from jax.sharding import PartitionSpec as P

SIDE = 64
HALF = 32
WIDE = 128
TILE = 8
SLOTS = 6
PEERS = 8
OWNERS = 32
GROUP = 2048
ROWS = 16384
HIGH = lax.Precision.HIGHEST
LIMIT = pltpu.CompilerParams(vmem_limit_bytes=24 * 1024 * 1024)
LARGE = pltpu.CompilerParams(vmem_limit_bytes=48 * 1024 * 1024)


def low(shape):
    return lax.broadcasted_iota(jnp.int32, shape, len(shape) - 1) < SIDE


def swap(x):
    return pltpu.roll(x, SIDE, 1)


def unfold_halves(packed):
    mask, other = low(packed.shape), swap(packed)
    return jnp.concatenate([jnp.where(mask, packed, other), jnp.where(mask, other, packed)], axis=0)


def fold_halves(rows):
    return jnp.where(low((HALF, WIDE)), rows[:HALF], rows[HALF:])


def product(left, right, left_dim=1, right_dim=0):
    return lax.dot_general(
        left,
        right,
        (((left_dim,), (right_dim,)), ((), ())),
        precision=HIGH,
        preferred_element_type=jnp.float32,
    )


def gram_packed(packed):
    both = product(packed, packed, 0, 0)
    total = both[:SIDE] + swap(both[SIDE:])
    return fold_halves(jnp.where(low(total.shape), total, swap(total)))


def inverse(gram):
    shape = gram.shape
    row = lax.broadcasted_iota(jnp.int32, shape, 0)
    lane = lax.broadcasted_iota(jnp.int32, shape, 1)
    work = jnp.where(lane < SIDE, gram, jnp.where(lane - SIDE == row, 1.0, 0.0))
    for k in range(SIDE):
        line = work[k : k + 1, :] / work[k : k + 1, k : k + 1]
        column = work[:, k : k + 1]
        work = jnp.where(row == k, line, work - column * line)
    zero = jnp.zeros_like(work)
    mask = lane < SIDE
    return jnp.concatenate([jnp.where(mask, swap(work), zero), jnp.where(mask, zero, work)], axis=0)


def pick(meta, at):
    lane = lax.broadcasted_iota(jnp.int32, meta.shape, 1)
    hit = (meta == (lane - at).astype(jnp.float32)) & (lane >= at) & (lane < at + OWNERS)
    return jnp.where(hit, 1.0, 0.0)


def lines(ref):
    return ref[...].reshape(OWNERS * TILE, WIDE)


def places(ref):
    return ref[:, TILE:, :].reshape(OWNERS * TILE, WIDE)


def prepare(place_ref, count_ref, third_ref, second_ref, out_ref, tile, arrived):
    own = lax.axis_index("slab")
    copy = pltpu.make_async_copy(
        second_ref.at[:, pl.ds(pl.multiple_of(own // 2 * WIDE, WIDE), WIDE)], tile, arrived
    )
    copy.start()
    third = third_ref[...]
    twice = jnp.concatenate([third, third], axis=1)
    out_ref[:, 0, :] = fold_halves(twice)
    out_ref[:, 2, :] = fold_halves(product(third, twice, 0, 0))
    out_ref[:, 3:TILE, :] = jnp.zeros((OWNERS, TILE - 3, WIDE), jnp.float32)
    row = lax.broadcasted_iota(jnp.int32, (TILE, WIDE), 0)
    lane = lax.broadcasted_iota(jnp.int32, (TILE, WIDE), 1)
    meta = jnp.full((TILE, WIDE), -1, jnp.int32)
    for slot in range(SLOTS):
        which = place_ref[slot, 2]
        value = jnp.where(
            lane < OWNERS,
            place_ref[slot, 0] % OWNERS,
            jnp.where(lane < 2 * OWNERS, place_ref[slot, 1] % OWNERS, which % PEERS * OWNERS + which // PEERS),
        )
        meta = jnp.where((row == slot) & (slot < count_ref[0]), value, meta)
    out_ref[:, TILE:, :] = jnp.broadcast_to(meta.astype(jnp.float32)[None], (OWNERS, TILE, WIDE))
    copy.wait()
    second = tile[...]
    share = lax.broadcasted_iota(jnp.int32, second.shape, 1) // SIDE == own % 2
    out_ref[:, 1, :] = fold_halves(
        product(jnp.where(share, second, 0.0), jnp.concatenate([second, second], axis=0), 1, 1)
    )


def relay(first_ref, out_ref):
    out_ref[:, :HALF, :] = jnp.broadcast_to(first_ref[:, 0, :][None], (PEERS, HALF, WIDE))
    grams = jnp.sum(first_ref[:, :TILE, :], axis=0)
    out_ref[:, HALF:, :] = jnp.broadcast_to(grams[None], (PEERS, TILE, WIDE))


def answer(meta_ref, held_ref, out_ref):
    wanted = places(meta_ref)[:, 2 * OWNERS : 2 * OWNERS + 1]
    lane = lax.broadcasted_iota(jnp.int32, (OWNERS * TILE, PEERS * OWNERS), 1).astype(jnp.float32)
    held = held_ref[:, :HALF, :].reshape(PEERS * OWNERS, WIDE)
    found = product(jnp.where(wanted == lane, 1.0, 0.0), held)
    grams = jnp.sum(held_ref[:, HALF:, :], axis=0)
    out_ref[...] = found.reshape(OWNERS, TILE, WIDE)
    out_ref[:, SLOTS, :] = jnp.broadcast_to(grams[1:2], (OWNERS, WIDE))
    out_ref[:, SLOTS + 1, :] = jnp.broadcast_to(grams[2:3], (OWNERS, WIDE))


def split(x):
    high = x.astype(jnp.bfloat16)
    return high, (x - high.astype(jnp.float32)).astype(jnp.bfloat16)


def fold(
    place_ref,
    count_ref,
    blocks_ref,
    third_ref,
    second_ref,
    folded_ref,
    out_ref,
    held,
    made,
    tiles,
    third_rows,
    terms,
    turned,
    held_sem,
    made_sem,
    tile_sem,
):
    count = count_ref[0]

    def load(slot):
        return pltpu.make_async_copy(blocks_ref.at[slot], held.at[slot], held_sem.at[slot])

    def load_tile(slot):
        start = pl.multiple_of(place_ref[slot, 1] % OWNERS // 2 * WIDE, WIDE)
        return pltpu.make_async_copy(second_ref.at[:, pl.ds(start, WIDE)], tiles.at[slot], tile_sem.at[slot])

    def store(slot):
        return pltpu.make_async_copy(made.at[slot], folded_ref.at[slot], made_sem.at[slot])

    for slot in range(SLOTS):

        @pl.when(slot < count)
        def _():
            load_tile(slot).start()
            load(slot).start()

    for slot in range(SLOTS):
        third_rows[slot] = third_ref[:, slot, :]
    terms[...] = jnp.zeros_like(terms)

    @pl.loop(0, count)
    def _(slot):
        packed = third_rows[slot]
        mask, other = low(packed.shape), swap(packed)
        zero = jnp.zeros_like(packed)
        twin = jnp.concatenate(
            [
                jnp.where(mask, packed, zero),
                jnp.where(mask, other, zero),
                jnp.where(mask, zero, other),
                jnp.where(mask, zero, packed),
            ],
            axis=0,
        )
        high, rest = split(twin)
        weights = jnp.concatenate([high, rest], axis=1)
        weights = jnp.concatenate([weights, weights], axis=0)
        load_tile(slot).wait()
        tile = tiles[slot]
        turned[...] = jnp.concatenate([tile, tile], axis=0).T
        start = place_ref[slot, 1] % 2 * SIDE
        pairs = jnp.where(
            mask, turned[pl.ds(start, HALF, stride=2), :], turned[pl.ds(start + 1, HALF, stride=2), :]
        )
        load(slot).wait()
        total = jnp.zeros((SIDE, WIDE), jnp.float32)
        step = 8
        for at in range(0, HALF, step):
            rows = jnp.concatenate(
                [held[slot, :, (at + n) * WIDE : (at + n + 1) * WIDE] for n in range(step)], axis=0
            )
            high, rest = split(rows)
            rows = jnp.concatenate([high, rest], axis=1)
            both = jnp.dot(rows, weights, preferred_element_type=jnp.float32)
            both = both[:, :WIDE] + both[:, WIDE:]
            for n in range(step):
                piece = both[n * SIDE : (n + 1) * SIDE]
                made[slot, at + n] = piece
                total += piece * pairs[at + n : at + n + 1, :]
        store(slot).start()
        terms[slot] = fold_halves(total + swap(total))

    for k in range(TILE):
        out_ref[:, k, :] = terms[k]

    for slot in range(SLOTS):

        @pl.when(slot < count)
        def _():
            store(slot).wait()


def invert_first(third_ref, out_ref):
    out_ref[...] = inverse(unfold_halves(third_ref[:, SLOTS, :] * third_ref[:, SLOTS + 1, :]))


def solve_first(part_ref, meta_ref, inverse_ref, spread_ref):
    total = product(pick(places(meta_ref), 0), lines(part_ref), 0, 0)[:OWNERS]
    spread_ref[...] = jnp.broadcast_to(product(total, inverse_ref[...])[None], spread_ref.shape)


def gram_first(first_ref, out_ref):
    out_ref[...] = jnp.broadcast_to(gram_packed(first_ref[...])[None], out_ref.shape)


def contract(place_ref, count_ref, folded_ref, first_ref, out_ref, terms, spaced):
    slot = pl.program_id(0)

    @pl.when(slot == 0)
    def _():
        terms[...] = jnp.zeros_like(terms)

    @pl.when(slot < count_ref[0])
    def _():
        first = first_ref[pl.ds(place_ref[slot, 0] % OWNERS, HALF, stride=OWNERS), :]
        term = jnp.sum(folded_ref[0] * unfold_halves(first)[None], axis=1)
        spaced[pl.ds(0, HALF, stride=2), :] = term
        spaced[pl.ds(1, HALF, stride=2), :] = swap(term)
        terms[slot] = jnp.where(low(term.shape), spaced[:HALF, :], swap(spaced[HALF:, :]))

    @pl.when(slot == SLOTS - 1)
    def _():
        for k in range(TILE):
            out_ref[:, k, :] = terms[k]


def invert_second(square_ref, third_ref, out_ref, scale_ref):
    square = unfold_halves(jnp.sum(square_ref[...], axis=0))
    shape = square.shape
    row = lax.broadcasted_iota(jnp.int32, shape, 0)
    lane = lax.broadcasted_iota(jnp.int32, shape, 1)
    means = jnp.where(row == lane % SIDE, square, 0.0) / ROWS
    along = jnp.sqrt(jnp.sum(means, axis=0, keepdims=True) + 1e-06)
    down = jnp.sqrt(jnp.sum(jnp.where(lane < SIDE, means, 0.0), axis=1, keepdims=True) + 1e-06)
    scale_ref[...] = along
    out_ref[...] = inverse(square / along / down * unfold_halves(third_ref[:, SLOTS + 1, :]))


def solve_second(part_ref, meta_ref, inverse_ref, scale_ref, spread_ref):
    total = product(pick(places(meta_ref), OWNERS), lines(part_ref), 0, 0)[OWNERS : 2 * OWNERS]
    solved = product(total / scale_ref[...], inverse_ref[...])
    spread_ref[...] = jnp.broadcast_to(solved[None], spread_ref.shape)


def turn(solved_ref, scale, out_ref):
    mask = low((HALF, WIDE))
    half = OWNERS // 2
    for pair in range(half // 2):
        parts = []
        for block in (2 * pair, 2 * pair + 1):
            left = solved_ref[:, block, :] / scale
            right = solved_ref[:, block + half, :] / scale
            parts += [jnp.where(mask, left, swap(right)), jnp.where(mask, swap(left), right)]
        both = jnp.concatenate(parts, axis=0).T
        out_ref[:, pair * WIDE : (pair + 1) * WIDE] = both[:SIDE]
        out_ref[:, GROUP // 2 + pair * WIDE : GROUP // 2 + (pair + 1) * WIDE] = both[SIDE:]


def finish_first(solved_ref, scale_ref, new_ref):
    turn(solved_ref, scale_ref[...], new_ref)


def squares(solved_ref, out_ref):
    solved = solved_ref[...].reshape(OWNERS * HALF, WIDE)
    total = jnp.sum(solved * solved, axis=0, keepdims=True)
    out_ref[...] = jnp.broadcast_to(total[None], out_ref.shape)


def finish_second(solved_ref, square_ref, new_ref, scale_ref):
    total = jnp.sum(square_ref[:, 0, :], axis=0, keepdims=True)
    scale = jnp.sqrt((total + swap(total)) / ROWS + 1e-06)
    scale_ref[...] = scale[:, :SIDE]
    turn(solved_ref, scale, new_ref)


def struct(*shape):
    return jax.ShapeDtypeStruct(shape, jnp.float32)


def exchange(x, axis):
    return lax.all_to_all(x, axis, 0, 0, tiled=True)


def whole(*shape):
    return pl.BlockSpec(shape, lambda *_: (0,) * len(shape))


def call(body, *outs):
    return pl.pallas_call(body, out_shape=outs if len(outs) > 1 else outs[0], compiler_params=LIMIT)


def shards(blocks, coords, counts, factor_b, factor_c):
    second = factor_b.T
    scalars = pl.BlockSpec(memory_space=pltpu.SMEM)
    local = pl.BlockSpec(memory_space=pltpu.VMEM)
    apart = pl.BlockSpec(memory_space=pltpu.HBM)
    small = (OWNERS, TILE, WIDE)
    full = (OWNERS, HALF, WIDE)
    opening = pl.pallas_call(
        prepare,
        in_specs=[scalars, scalars, local, apart],
        out_specs=local,
        out_shape=struct(OWNERS, 2 * TILE, WIDE),
        scratch_shapes=[pltpu.VMEM((SIDE, WIDE), jnp.float32), pltpu.SemaphoreType.DMA],
        compiler_params=LIMIT,
    )(coords, counts, factor_c, second)
    meta = exchange(opening, "slab")
    held = exchange(call(relay, struct(PEERS, HALF + TILE, WIDE))(meta), "rows")
    third = exchange(call(answer, struct(*small))(meta, held), "slab")
    folded, part_a = pl.pallas_call(
        fold,
        in_specs=[scalars, scalars, apart, local, apart],
        out_specs=[apart, local],
        out_shape=(struct(SLOTS, HALF, SIDE, WIDE), struct(*small)),
        scratch_shapes=[
            pltpu.VMEM((SLOTS, SIDE, SIDE * SIDE), jnp.float32),
            pltpu.VMEM((SLOTS, HALF, SIDE, WIDE), jnp.float32),
            pltpu.VMEM((SLOTS, SIDE, WIDE), jnp.float32),
            pltpu.VMEM((SLOTS, HALF, WIDE), jnp.float32),
            pltpu.VMEM((TILE, HALF, WIDE), jnp.float32),
            pltpu.VMEM((WIDE, WIDE), jnp.float32),
            pltpu.SemaphoreType.DMA((SLOTS,)),
            pltpu.SemaphoreType.DMA((SLOTS,)),
            pltpu.SemaphoreType.DMA((SLOTS,)),
        ],
        compiler_params=LARGE,
    )(coords, counts, blocks, third, second)
    part_a = exchange(part_a, "slab")
    inverse_a = call(invert_first, struct(WIDE, WIDE))(third)
    whole_a = exchange(call(solve_first, struct(*full))(part_a, meta, inverse_a), "slab")
    first = whole_a.reshape(OWNERS * HALF, WIDE)
    square_a = exchange(call(gram_first, struct(PEERS, HALF, WIDE))(first), "rows")
    part_b = pl.pallas_call(
        contract,
        grid_spec=pltpu.PrefetchScalarGridSpec(
            num_scalar_prefetch=2,
            grid=(SLOTS,),
            in_specs=[
                pl.BlockSpec((1, HALF, SIDE, WIDE), lambda slot, *_: (slot, 0, 0, 0)),
                whole(OWNERS * HALF, WIDE),
            ],
            out_specs=whole(*small),
            scratch_shapes=[
                pltpu.VMEM((TILE, HALF, WIDE), jnp.float32),
                pltpu.VMEM((SIDE, WIDE), jnp.float32),
            ],
        ),
        out_shape=struct(*small),
        compiler_params=LARGE,
    )(coords, counts, folded, first)
    part_b = exchange(part_b, "slab")
    inverse_b, scale_a = call(invert_second, struct(WIDE, WIDE), struct(1, WIDE))(square_a, third)
    new_a = call(finish_first, struct(SIDE, GROUP))(whole_a, scale_a)
    inverse_b, new_a = lax.optimization_barrier((inverse_b, new_a))
    spread_b = call(solve_second, struct(*full))(part_b, meta, inverse_b, scale_a)
    whole_b = exchange(spread_b, "slab")
    square_b = exchange(call(squares, struct(PEERS, TILE, WIDE))(whole_b), "rows")
    new_b, scale_b = call(finish_second, struct(SIDE, GROUP), struct(1, SIDE))(whole_b, square_b)
    return (new_a.T, new_b.T, scale_b.reshape(SIDE))


def solution(mesh):
    in_specs = (
        P(("slab", "rows"), None, None),
        P(("slab", "rows"), None),
        P(("slab", "rows")),
        P("rows", None),
        P(("slab", "rows"), None),
    )
    out_specs = (P("rows", None), P("rows", None), P())
    return jax.shard_map(shards, mesh=mesh, in_specs=in_specs, out_specs=out_specs, check_vma=False)
```

time: 944 us -> 161 us (0.17); the launches traced: 931 us -> 160 us
  waiting for transfers between devices: 422 us -> 5.83 us
  blocking collectives: 379 us -> 99.1 us
  matrix products: 39.4 us -> 0 us
  other arithmetic: 32.4 us -> 0 us
  Pallas kernels: 0 us -> 28 us
  local copies, waits for them, and re-layouts: 27.6 us -> 3.61 us
  starting transfers between devices: 0.3 us -> 22.3 us
  loops' own time: 17.3 us -> 0 us
  between operations: 13.9 us -> 1.35 us
    reduce_scatter x2 -> x0, waiting for transfers between devices: 321 us -> none  [solve_update(): lax.psum_scatter(partial_value, 'slab', scatter_dimension=0, tiled=True)]
    psum x4 -> x0, blocking collectives: 299 us -> none  [the longest x2 159 us: solve_update(): squares = lax.psum(jnp.sum(solved * solved, axis=0), ('slab', 'rows'))]
    all_gather x1 -> x0, waiting for transfers between devices: 101 us -> none  [shards(): full_c = lax.all_gather(factor_c, ('slab', 'rows'), axis=0, tiled=True)]
    all_to_all x0 -> x6, blocking collectives: none -> 99.1 us  [exchange(): return lax.all_to_all(x, axis, 0, 0, tiled=True)]
    all_gather x2 -> x0, blocking collectives: 79.5 us -> none  [solve_update(): group = lax.all_gather(updated, 'slab', axis=0, tiled=True)]
    dot_general x9 -> x0, matrix products: 36.9 us -> none  [the longest x1 19.5 us: shards(): jnp.dot(full_c.T, full_c, precision=high, preferred_element_type=jnp.floa...]
    pallas_call x0 -> x13, Pallas kernels: none -> 28 us  [the longest x1 5.69 us: shards(): call(invert_second, struct(WIDE, WIDE), struct(1, WIDE))(square_a, third)]
    another operation x10 -> x0, other arithmetic: 24.1 us -> none  [the longest x6 13 us: apply_inverse(): chol = jnp.linalg.cholesky(gram)]
  transfers between devices with their start and end apart: 3 -> 3, of which waited for: 3 -> 2; matrix products, arithmetic and copies ran while one was open for 5% -> 0% of each run, Pallas kernels for 0% -> 11%
where the time goes in v2:
time: 161 us; the launch traced here: 160 us
  blocking collectives  99.1 us (62%)
  Pallas kernels  28 us (17%)
  starting transfers between devices  22.3 us (14%)
  waiting for transfers between devices  5.83 us (4%)
  local copies, waits for them, and re-layouts  3.61 us (2%)
    all_to_all x6, blocking collectives, exchange(): return lax.all_to_all(x, axis, 0, 0, tiled=True)  99.1 us
    all_to_all x3, starting transfers between devices, exchange(): return lax.all_to_all(x, axis, 0, 0, tiled=True)  22.3 us
    all_to_all x3, waiting for transfers between devices, exchange(): return lax.all_to_all(x, axis, 0, 0, tiled=True)  5.83 us
    pallas_call x1, Pallas kernels, shards(): call(invert_second, struct(WIDE, WIDE), struct(1, WIDE))(square_a, third)  5.69 us
    pallas_call x1, Pallas kernels, shards(): pl.pallas_call(contract, grid_spec=pltpu.PrefetchScalarGridSpec(num_scala...  5.67 us
    pallas_call x1, Pallas kernels, shards(): inverse_a = call(invert_first, struct(WIDE, WIDE))(third)  5.56 us
    pallas_call x1, Pallas kernels, shards(): pl.pallas_call(fold, in_specs=[scalars, scalars, apart, local, apart], ou...  4.08 us
    unnamed x7, local copies, waits for them, and re-layouts  3.61 us
  transfers between devices with their start and end apart: 3, of which 2 were waited for; matrix products, arithmetic and copies ran while one was open for 0% of the time, Pallas kernels for 11%

profile of v2, /device:TPU:1, one launch (start us, length us, event | category | flops | bytes accessed | tf_op | source)
XLA Modules:
  0.0 160.3 jit_solution(11758986596697060620)
XLA Ops:
  1.3 0.8 copy.9.place_ref
  2.0 0.0 copy-start
  2.0 1.0 copy-done
  3.1 0.0 copy-start.2
  3.1 0.8 copy-done.2
  3.8 1.2 shard_map.76
  5.0 21.4 %all_to_all.45.first_ref.meta_ref = f32[32,16,128]{2,1,0:T(8,128)S(1)} all-to-all(f32[32,16,128]{2,1,0:T(8,128)S(1)} %shard_map.76), channel_id=1, replica_groups=mesh['slab'=32,'rows'=8] {'slab'}, dimensions={0} | all-to-all | bytes 524288 | tf_op jit(solution)/shard_map/all_to_all | solution.py:317
  26.4 13.6 %all_to_all.46.held_ref = f32[8,40,128]{2,1,0:T(8,128)S(1)} all-to-all(f32[8,40,128]{2,1,0:T(8,128)S(1)} %shard_map.77), channel_id=1, replica_groups=mesh['slab'=32,'rows'=8] {'rows'}, dimensions={0} | all-to-all | bytes 327680 | tf_op jit(solution)/shard_map/all_to_all | solution.py:317
  40.0 0.4 shard_map.78
  40.4 13.1 %all_to_all.47.third_ref = f32[32,8,128]{2,1,0:T(8,128)S(1)} all-to-all(f32[32,8,128]{2,1,0:T(8,128)S(1)} %shard_map.78), channel_id=1, replica_groups=mesh['slab'=32,'rows'=8] {'slab'}, dimensions={0} | all-to-all | bytes 262144 | tf_op jit(solution)/shard_map/all_to_all | solution.py:317
  53.5 0.0 copy-start.1
  53.5 1.0 copy-done.1
  54.5 4.1 %shard_map.79 = (f32[6,32,64,128]{3,2,1,0:T(8,128)}, f32[32,8,128]{2,1,0:T(8,128)}) custom-call(s32[6,3]{1,0:T(8,128)S(1)} %copy.9.place_ref, s32[1]{0:T(128)S(6)} %copy.11.count_ref, f32[6,64,4096]{2,1,0:T(8,128)} %blocks_ref.1, f32[32,8,128]{2,1,0:T(8,128)S(1)} %all_to_all.47.third_ref, f32[64,2048]{1,0:T(8,128)S(1)} %bitcast.8), custom_call_target="tpu_custom_call" | custom-call | tf_op jit(solution)/shard_map/pallas_call | solution.py:346
  58.6 7.4 %all-to-all-start.3 = ((f32[32,8,128]{2,1,0:T(8,128)}), f32[32,8,128]{2,1,0:T(8,128)S(1)}, u32[]{:S(2)}, u32[]{:S(2)}) async-start(f32[32,8,128]{2,1,0:T(8,128)} %get-tuple-element.11), calls=%async_computation.3 | async-start | bytes 262144 | tf_op jit(solution)/shard_map/all_to_all | solution.py:317
  66.0 5.6 %shard_map.80.inverse_ref = f32[128,128]{1,0:T(8,128)S(1)} custom-call(f32[32,8,128]{2,1,0:T(8,128)S(1)} %all_to_all.47.third_ref), custom_call_target="tpu_custom_call" | custom-call | tf_op jit(solution)/shard_map/pallas_call | solution.py:365
  71.6 3.6 %all-to-all-done.3.part_ref = f32[32,8,128]{2,1,0:T(8,128)S(1)} async-done(((f32[32,8,128]{2,1,0:T(8,128)}), f32[32,8,128]{2,1,0:T(8,128)S(1)}, u32[]{:S(2)}, u32[]{:S(2)}) %all-to-all-start.3) | async-done | bytes 131104 | tf_op jit(solution)/shard_map/all_to_all | solution.py:317
  75.2 0.6 shard_map.81
  75.7 17.6 %all_to_all.48.solved_ref = f32[32,32,128]{2,1,0:T(8,128)S(1)} all-to-all(f32[32,32,128]{2,1,0:T(8,128)S(1)} %shard_map.81), channel_id=1, replica_groups=mesh['slab'=32,'rows'=8] {'slab'}, dimensions={0} | all-to-all | bytes 1048576 | tf_op jit(solution)/shard_map/all_to_all | solution.py:317
  93.3 1.4 shard_map.82
  94.7 8.8 %all-to-all-start.5 = ((f32[8,32,128]{2,1,0:T(8,128)}), f32[8,32,128]{2,1,0:T(8,128)S(1)}, u32[]{:S(2)}, u32[]{:S(2)}) async-start(f32[8,32,128]{2,1,0:T(8,128)} %shard_map.82), calls=%async_computation.5 | async-start | bytes 262144 | tf_op jit(solution)/shard_map/all_to_all | solution.py:317
  103.5 5.7 %shard_map.85 = f32[32,8,128]{2,1,0:T(8,128)} custom-call(s32[6,3]{1,0:T(8,128)S(1)} %copy.9.place_ref, s32[1]{0:T(128)S(6)} %copy.11.count_ref, f32[6,32,64,128]{3,2,1,0:T(8,128)} %get-tuple-element.15.folded_ref, f32[1024,128]{1,0:T(8,128)S(1)} %bitcast.6), custom_call_target="tpu_custom_call" | custom-call | tf_op jit(solution)/shard_map/pallas_call | solution.py:369
  109.2 0.0 all-to-all-done.5.square_ref
  109.2 6.2 %all-to-all-start.6 = ((f32[32,8,128]{2,1,0:T(8,128)}), f32[32,8,128]{2,1,0:T(8,128)S(1)}, u32[]{:S(2)}, u32[]{:S(2)}) async-start(f32[32,8,128]{2,1,0:T(8,128)} %shard_map.85), calls=%async_computation.6 | async-start | bytes 262144 | tf_op jit(solution)/shard_map/all_to_all | solution.py:317
  115.4 5.7 %shard_map.83 = (f32[128,128]{1,0:T(8,128)S(1)}, f32[1,128]{1,0:T(1,128)S(1)}) custom-call(f32[8,32,128]{2,1,0:T(8,128)S(1)} %all-to-all-done.5.square_ref, f32[32,8,128]{2,1,0:T(8,128)S(1)} %all_to_all.47.third_ref), custom_call_target="tpu_custom_call" | custom-call | tf_op jit(solution)/shard_map/pallas_call | solution.py:388
  121.1 1.3 shard_map.84
  122.4 2.2 %all-to-all-done.6.part_ref = f32[32,8,128]{2,1,0:T(8,128)S(1)} async-done(((f32[32,8,128]{2,1,0:T(8,128)}), f32[32,8,128]{2,1,0:T(8,128)S(1)}, u32[]{:S(2)}, u32[]{:S(2)}) %all-to-all-start.6) | async-done | bytes 131104 | tf_op jit(solution)/shard_map/all_to_all | solution.py:317
  124.6 0.6 shard_map.86
  125.2 21.0 %all_to_all.49.solved_ref = f32[32,32,128]{2,1,0:T(8,128)S(1)} all-to-all(f32[32,32,128]{2,1,0:T(8,128)S(1)} %shard_map.86), channel_id=1, replica_groups=mesh['slab'=32,'rows'=8] {'slab'}, dimensions={0} | all-to-all | bytes 1048576 | tf_op jit(solution)/shard_map/all_to_all | solution.py:317
  146.1 0.1 shard_map.87
  146.3 12.6 %all_to_all.50.square_ref = f32[8,8,128]{2,1,0:T(8,128)S(1)} all-to-all(f32[8,8,128]{2,1,0:T(8,128)S(1)} %shard_map.87), channel_id=1, replica_groups=mesh['slab'=32,'rows'=8] {'rows'}, dimensions={0} | all-to-all | bytes 65536 | tf_op jit(solution)/shard_map/all_to_all | solution.py:317
  158.9 1.3 shard_map.88
  (1 shorter events, 0.0 us)
Async XLA Ops:
  2.0 1.0 copy-start
  3.1 0.8 copy-start.2
  53.5 1.0 copy-start.1
  58.6 16.6 %all-to-all-start.3 = ((f32[32,8,128]{2,1,0:T(8,128)}), f32[32,8,128]{2,1,0:T(8,128)S(1)}, u32[]{:S(2)}, u32[]{:S(2)}) async-start(f32[32,8,128]{2,1,0:T(8,128)} %get-tuple-element.11), calls=%async_computation.3 | async-start | bytes 262144 | tf_op jit(solution)/shard_map/all_to_all | solution.py:317
  94.7 14.5 %all-to-all-start.5 = ((f32[8,32,128]{2,1,0:T(8,128)}), f32[8,32,128]{2,1,0:T(8,128)S(1)}, u32[]{:S(2)}, u32[]{:S(2)}) async-start(f32[8,32,128]{2,1,0:T(8,128)} %shard_map.82), calls=%async_computation.5 | async-start | bytes 262144 | tf_op jit(solution)/shard_map/all_to_all | solution.py:317
  109.2 15.4 %all-to-all-start.6 = ((f32[32,8,128]{2,1,0:T(8,128)}), f32[32,8,128]{2,1,0:T(8,128)S(1)}, u32[]{:S(2)}, u32[]{:S(2)}) async-start(f32[32,8,128]{2,1,0:T(8,128)} %shard_map.85), calls=%async_computation.6 | async-start | bytes 262144 | tf_op jit(solution)/shard_map/all_to_all | solution.py:317

commit v3 on v2

v3 whole, which is shorter than its diff:
```python
import jax
import jax.numpy as jnp
from jax import lax
from jax.experimental import pallas as pl
from jax.experimental.pallas import tpu as pltpu
from jax.sharding import Mesh
from jax.sharding import PartitionSpec as P

SIDE = 64
HALF = 32
WIDE = 128
STEP = 8
TILE = 8
SLOTS = 6
LEAD = 2
TURNS = 4
PEERS = 8
OWNERS = 32
GROUP = 2048
ROWS = 16384
HIGH = lax.Precision.HIGHEST
SLAB = ("x", "z")
LIMIT = pltpu.CompilerParams(vmem_limit_bytes=24 * 1024 * 1024)
LARGE = pltpu.CompilerParams(vmem_limit_bytes=48 * 1024 * 1024)


def low(shape):
    return lax.broadcasted_iota(jnp.int32, shape, len(shape) - 1) < SIDE


def swap(x):
    return pltpu.roll(x, SIDE, 1)


def unfold_halves(packed):
    mask, other = low(packed.shape), swap(packed)
    return jnp.concatenate([jnp.where(mask, packed, other), jnp.where(mask, other, packed)], axis=0)


def fold_halves(rows):
    return jnp.where(low((HALF, WIDE)), rows[:HALF], rows[HALF:])


def product(left, right, left_dim=1, right_dim=0):
    return lax.dot_general(
        left,
        right,
        (((left_dim,), (right_dim,)), ((), ())),
        precision=HIGH,
        preferred_element_type=jnp.float32,
    )


def gram_packed(packed):
    both = product(packed, packed, 0, 0)
    total = both[:SIDE] + swap(both[SIDE:])
    return fold_halves(jnp.where(low(total.shape), total, swap(total)))


def inverse(gram):
    shape = gram.shape
    row = lax.broadcasted_iota(jnp.int32, shape, 0)
    lane = lax.broadcasted_iota(jnp.int32, shape, 1)
    work = jnp.where(lane < SIDE, gram, jnp.where(lane - SIDE == row, 1.0, 0.0))
    for k in range(SIDE):
        line = work[k : k + 1, :] / work[k : k + 1, k : k + 1]
        column = work[:, k : k + 1]
        work = jnp.where(row == k, line, work - column * line)
    zero = jnp.zeros_like(work)
    mask = lane < SIDE
    return jnp.concatenate([jnp.where(mask, swap(work), zero), jnp.where(mask, zero, work)], axis=0)


def held(shape):
    return lax.broadcasted_iota(jnp.int32, shape, 0) % TILE >= LEAD


def pick(meta, at):
    lane = lax.broadcasted_iota(jnp.int32, meta.shape, 1)
    hit = (meta == (lane - at).astype(jnp.float32)) & (lane >= at) & (lane < at + OWNERS) & held(meta.shape)
    return jnp.where(hit, 1.0, 0.0)


def lines(ref):
    return ref[...].reshape(OWNERS * TILE, WIDE)


def prepare(given_ref, out_ref, place_ref):
    third = given_ref[:SIDE, :]
    twice = jnp.concatenate([third, third], axis=1)
    piece, gram = fold_halves(twice), fold_halves(product(third, twice, 0, 0))
    given = given_ref[SIDE:, :].astype(jnp.int32)
    place_ref[...] = given
    row = lax.broadcasted_iota(jnp.int32, given.shape, 0)
    lane = lax.broadcasted_iota(jnp.int32, given.shape, 1)
    first, second, third = (
        jnp.sum(jnp.where(lane == row - LEAD, given[n : n + 1, :], 0), axis=1, keepdims=True) for n in range(3)
    )
    row = lax.broadcasted_iota(jnp.int32, (TILE, WIDE), 0)
    lane = lax.broadcasted_iota(jnp.int32, (TILE, WIDE), 1)
    meta = jnp.where(
        lane < OWNERS,
        first % OWNERS,
        jnp.where(lane < 2 * OWNERS, second % OWNERS, third % PEERS * OWNERS + third // PEERS),
    )
    meta = jnp.where((row >= LEAD) & (row - LEAD < given[3:4, 0:1]), meta, -1)
    out_ref[...] = jnp.broadcast_to(meta.astype(jnp.float32)[None], out_ref.shape)
    out_ref[:, 0, :] = piece
    out_ref[:, 1, :] = gram


def arrange(second_ref, gram_ref, pairs_ref, turned):
    second = second_ref[...]
    gram_ref[...] = fold_halves(product(second, jnp.concatenate([second, second], axis=0), 1, 1))
    mask = low((HALF, WIDE))
    for pair in range(OWNERS // 2):
        tile = second[:, pair * WIDE : (pair + 1) * WIDE]
        turned[pair % 2] = jnp.concatenate([tile, tile], axis=0).T
        for n in range(2):
            even = turned[pair % 2, pl.ds(n * SIDE, HALF, stride=2), :]
            odd = turned[pair % 2, pl.ds(n * SIDE + 1, HALF, stride=2), :]
            pairs_ref[2 * pair + n] = jnp.where(mask, even, odd)


def relay(first_ref, gram_ref, out_ref):
    out_ref[:, :HALF, :] = jnp.broadcast_to(first_ref[:, 0, :][None], (PEERS, HALF, WIDE))
    second = gram_ref[pl.ds(lax.axis_index(SLAB), 1), :]
    third = jnp.sum(first_ref[:, 1, :], axis=0, keepdims=True)
    row = lax.broadcasted_iota(jnp.int32, (TILE, WIDE), 0)
    grams = jnp.where(row == 0, second, jnp.where(row == 1, third, 0.0))
    out_ref[:, HALF:, :] = jnp.broadcast_to(grams[None], (PEERS, TILE, WIDE))


def answer(meta_ref, held_ref, out_ref):
    wanted = lines(meta_ref)[:, 2 * OWNERS : 2 * OWNERS + 1]
    shape = (OWNERS * TILE, PEERS * OWNERS)
    lane = lax.broadcasted_iota(jnp.int32, shape, 1).astype(jnp.float32)
    stock = held_ref[:, :HALF, :].reshape(PEERS * OWNERS, WIDE)
    found = product(jnp.where((wanted == lane) & held(shape), 1.0, 0.0), stock)
    grams = jnp.sum(held_ref[:, HALF:, :], axis=0)
    out_ref[...] = found.reshape(OWNERS, TILE, WIDE)
    out_ref[:, 0, :] = jnp.broadcast_to(grams[0:1], (OWNERS, WIDE))
    out_ref[:, 1, :] = jnp.broadcast_to(grams[1:2], (OWNERS, WIDE))


def split(x):
    high = x.astype(jnp.bfloat16)
    return high, (x - high.astype(jnp.float32)).astype(jnp.bfloat16)


def fold(
    place_ref,
    blocks_ref,
    third_ref,
    pairs_ref,
    folded_ref,
    out_ref,
    held,
    made,
    weights,
    terms,
    held_sem,
    made_sem,
):
    count = place_ref[3, 0]

    def load(slot):
        return pltpu.make_async_copy(blocks_ref.at[slot], held.at[slot], held_sem.at[slot])

    def store(slot):
        return pltpu.make_async_copy(made.at[slot], folded_ref.at[slot], made_sem.at[slot])

    for slot in range(SLOTS):

        @pl.when(slot < count)
        def _():
            load(slot).start()

    for slot in range(SLOTS):
        packed = third_ref[:, slot + LEAD, :]
        mask, other = low(packed.shape), swap(packed)
        zero = jnp.zeros_like(packed)
        twin = jnp.concatenate(
            [
                jnp.where(mask, packed, zero),
                jnp.where(mask, other, zero),
                jnp.where(mask, zero, other),
                jnp.where(mask, zero, packed),
            ],
            axis=0,
        )
        high, rest = split(twin)
        twin = jnp.concatenate([high, rest], axis=1)
        weights[slot] = jnp.concatenate([twin, twin], axis=0)
    terms[...] = jnp.zeros_like(terms)

    @pl.loop(0, count)
    def _(slot):
        pairs = pairs_ref[place_ref[1, slot] % OWNERS]
        load(slot).wait()
        total = jnp.zeros((SIDE, WIDE), jnp.float32)
        for at in range(0, HALF, STEP):
            rows = jnp.concatenate(
                [held[slot, :, (at + n) * WIDE : (at + n + 1) * WIDE] for n in range(STEP)], axis=0
            )
            high, rest = split(rows)
            rows = jnp.concatenate([high, rest], axis=1)
            both = jnp.dot(rows, weights[slot], preferred_element_type=jnp.float32)
            both = both[:, :WIDE] + both[:, WIDE:]
            for n in range(STEP):
                piece = both[n * SIDE : (n + 1) * SIDE]
                made[slot, at + n] = piece
                total += piece * pairs[at + n : at + n + 1, :]
        store(slot).start()
        terms[slot + LEAD] = fold_halves(total + swap(total))

    for k in range(TILE):
        out_ref[:, k, :] = terms[k]

    for slot in range(SLOTS):

        @pl.when(slot < count)
        def _():
            store(slot).wait()


def invert_first(third_ref, out_ref):
    out_ref[...] = inverse(unfold_halves(third_ref[:, 0, :] * third_ref[:, 1, :]))


def solve_first(part_ref, meta_ref, inverse_ref, out_ref, solved_ref):
    chosen = pick(lines(meta_ref), 0)
    solved = product(product(chosen, lines(part_ref), 0, 0), inverse_ref[...])
    out_ref[...] = product(chosen, solved).reshape(OWNERS, TILE, WIDE)
    solved = solved[:OWNERS]
    out_ref[:, 0, :] = gram_packed(solved)
    solved_ref[...] = solved


def share_gram(first_ref, out_ref):
    total = jnp.sum(first_ref[:, 0, :], axis=0, keepdims=True)
    out_ref[...] = jnp.broadcast_to(total[None], out_ref.shape)


def contract(place_ref, folded_ref, first_ref, out_ref, held, first_rows, terms, spaced, held_sem):
    count = place_ref[3, 0]

    def load(slot):
        return pltpu.make_async_copy(folded_ref.at[slot], held.at[slot], held_sem.at[slot])

    for slot in range(SLOTS):

        @pl.when(slot < count)
        def _():
            load(slot).start()

    terms[...] = jnp.zeros_like(terms)
    for slot in range(SLOTS):
        first_rows[slot] = first_ref[:, slot + LEAD, :]

    @pl.loop(0, count)
    def _(slot):
        first = unfold_halves(first_rows[slot])
        load(slot).wait()
        term = jnp.sum(held[slot] * first[None], axis=1)
        spaced[pl.ds(0, HALF, stride=2), :] = term
        spaced[pl.ds(1, HALF, stride=2), :] = swap(term)
        terms[slot + LEAD] = jnp.where(low(term.shape), spaced[:HALF, :], swap(spaced[HALF:, :]))

    for k in range(TILE):
        out_ref[:, k, :] = terms[k]


def insert(part_ref, square_ref, out_ref):
    out_ref[...] = part_ref[...]
    total = jnp.sum(square_ref[:, 0, :], axis=0, keepdims=True)
    out_ref[:, 0, :] = jnp.broadcast_to(total, (OWNERS, WIDE))


def sum_second(part_ref, meta_ref, solved_ref, out_ref):
    total = product(pick(lines(meta_ref), OWNERS), lines(part_ref), 0, 0)[OWNERS : 2 * OWNERS]
    both = jnp.concatenate([total, solved_ref[...]], axis=0)
    out_ref[...] = jnp.broadcast_to(both[None], out_ref.shape)


def invert_second(part_ref, third_ref, out_ref, scale_ref):
    square = unfold_halves(part_ref[:, 0, :])
    shape = square.shape
    row = lax.broadcasted_iota(jnp.int32, shape, 0)
    lane = lax.broadcasted_iota(jnp.int32, shape, 1)
    means = jnp.where(row == lane % SIDE, square, 0.0) / ROWS
    along = jnp.sqrt(jnp.sum(means, axis=0, keepdims=True) + 1e-06)
    down = jnp.sqrt(jnp.sum(jnp.where(lane < SIDE, means, 0.0), axis=1, keepdims=True) + 1e-06)
    scale_ref[...] = along
    out_ref[...] = inverse(square / along / down * unfold_halves(third_ref[:, 1, :]))


def solve_second(near_ref, inverse_ref, scale_ref, out_ref, square_ref):
    near = near_ref[...] / scale_ref[...]
    solved = product(near[:, :HALF].reshape(PEERS * HALF, WIDE), inverse_ref[...])
    out_ref[:, :HALF, :] = solved.reshape(PEERS, HALF, WIDE)
    out_ref[:, HALF:, :] = near[:, HALF:]
    total = jnp.sum(solved * solved, axis=0, keepdims=True)
    square_ref[...] = jnp.broadcast_to(total[None], square_ref.shape)


def turn(solved_ref, out_ref):
    mask = low((HALF, WIDE))
    half = OWNERS // 2
    for pair in range(half // 2):
        parts = []
        for block in (2 * pair, 2 * pair + 1):
            left, right = solved_ref[:, block, :], solved_ref[:, block + half, :]
            parts += [jnp.where(mask, left, swap(right)), jnp.where(mask, swap(left), right)]
        both = jnp.concatenate(parts, axis=0).T
        out_ref[:, pair * WIDE : (pair + 1) * WIDE] = both[:SIDE]
        out_ref[:, GROUP // 2 + pair * WIDE : GROUP // 2 + (pair + 1) * WIDE] = both[SIDE:]


def collect(parts, which, scale, out_ref):
    own = lax.axis_index("x")
    for step, part in enumerate(parts):
        rows = part[:, which * HALF : (which + 1) * HALF, :]
        out_ref[pl.ds((own + TURNS - step) % TURNS * PEERS, PEERS)] = rows if scale is None else rows / scale


def finish_first(own_ref, one_ref, two_ref, three_ref, new_ref, solved):
    collect((own_ref, one_ref, two_ref, three_ref), 1, None, solved)
    turn(solved, new_ref)


def finish_second(own_ref, one_ref, two_ref, three_ref, square_ref, new_ref, scale_ref, solved):
    total = jnp.sum(square_ref[:, 0, :], axis=0, keepdims=True)
    scale = jnp.sqrt((total + swap(total)) / ROWS + 1e-06)
    scale_ref[...] = scale[:, :SIDE]
    collect((own_ref, one_ref, two_ref, three_ref), 0, scale, solved)
    turn(solved, new_ref)


def struct(*shape):
    return jax.ShapeDtypeStruct(shape, jnp.float32)


def exchange(x, axis):
    return lax.all_to_all(x, axis, 0, 0, tiled=True)


def call(body, *outs):
    return pl.pallas_call(body, out_shape=outs if len(outs) > 1 else outs[0], compiler_params=LIMIT)


def shards(blocks, coords, counts, factor_b, factor_c):
    scalars = pl.BlockSpec(memory_space=pltpu.SMEM)
    local = pl.BlockSpec(memory_space=pltpu.VMEM)
    apart = pl.BlockSpec(memory_space=pltpu.HBM)
    small = (OWNERS, TILE, WIDE)
    full = (OWNERS, HALF, WIDE)
    given = jnp.pad(coords, ((0, SIDE - SLOTS), (SIDE, TILE - 3))).T.astype(jnp.float32)
    row = lax.broadcasted_iota(jnp.int32, given.shape, 0)
    given = jnp.where(row < SIDE, jnp.pad(factor_c, ((0, TILE), (0, 0))), given)
    given = jnp.where(row < SIDE + 3, given, counts.astype(jnp.float32)[:, None])
    opening, place = pl.pallas_call(
        prepare,
        out_shape=(struct(*small), jax.ShapeDtypeStruct((TILE, SIDE), jnp.int32)),
        compiler_params=LIMIT,
    )(given)
    meta = exchange(opening, SLAB)
    gram_b, pairs = pl.pallas_call(
        arrange,
        out_shape=(struct(HALF, WIDE), struct(*full)),
        scratch_shapes=[pltpu.VMEM((2, WIDE, WIDE), jnp.float32)],
        compiler_params=LIMIT,
    )(factor_b.T)
    held = exchange(call(relay, struct(PEERS, HALF + TILE, WIDE))(meta, gram_b), "rows")
    third = exchange(call(answer, struct(*small))(meta, held), SLAB)
    folded, part_a = pl.pallas_call(
        fold,
        in_specs=[scalars, apart, local, local],
        out_specs=[apart, local],
        out_shape=(struct(SLOTS, HALF, SIDE, WIDE), struct(*small)),
        scratch_shapes=[
            pltpu.VMEM((SLOTS, SIDE, SIDE * SIDE), jnp.float32),
            pltpu.VMEM((SLOTS, HALF, SIDE, WIDE), jnp.float32),
            pltpu.VMEM((SLOTS, 2 * WIDE, 2 * WIDE), jnp.bfloat16),
            pltpu.VMEM((TILE, HALF, WIDE), jnp.float32),
            pltpu.SemaphoreType.DMA((SLOTS,)),
            pltpu.SemaphoreType.DMA((SLOTS,)),
        ],
        compiler_params=LARGE,
    )(place, blocks, third, pairs)
    part_a = exchange(part_a, SLAB)
    inverse_a = call(invert_first, struct(WIDE, WIDE))(third)
    answer_a, solved_a = call(solve_first, struct(*small), struct(HALF, WIDE))(part_a, meta, inverse_a)
    first = exchange(answer_a, SLAB)
    square_a = exchange(call(share_gram, struct(PEERS, TILE, WIDE))(first), "rows")
    part_b = pl.pallas_call(
        contract,
        in_specs=[scalars, apart, local],
        out_specs=local,
        out_shape=struct(*small),
        scratch_shapes=[
            pltpu.VMEM((SLOTS, HALF, SIDE, WIDE), jnp.float32),
            pltpu.VMEM((SLOTS, HALF, WIDE), jnp.float32),
            pltpu.VMEM((TILE, HALF, WIDE), jnp.float32),
            pltpu.VMEM((SIDE, WIDE), jnp.float32),
            pltpu.SemaphoreType.DMA((SLOTS,)),
        ],
        compiler_params=LARGE,
    )(place, folded, first)
    part_b = exchange(call(insert, struct(*small))(part_b, square_a), SLAB)
    near = exchange(call(sum_second, struct(PEERS, SIDE, WIDE))(part_b, meta, solved_a), "z")
    inverse_b, scale_a = call(invert_second, struct(WIDE, WIDE), struct(1, WIDE))(part_b, third)
    near, square_b = call(solve_second, struct(PEERS, SIDE, WIDE), struct(*small))(near, inverse_b, scale_a)
    parts = [near] + [
        lax.ppermute(near, "x", [(n, (n + step) % TURNS) for n in range(TURNS)]) for step in range(1, TURNS)
    ]
    square_b = exchange(square_b, ("x", "rows"))
    scratch = [pltpu.VMEM(full, jnp.float32)]
    new_a = pl.pallas_call(
        finish_first, out_shape=struct(SIDE, GROUP), scratch_shapes=scratch, compiler_params=LIMIT
    )(*parts)
    new_b, scale_b = pl.pallas_call(
        finish_second,
        out_shape=(struct(SIDE, GROUP), struct(1, SIDE)),
        scratch_shapes=scratch,
        compiler_params=LIMIT,
    )(*parts, square_b)
    return (new_a.T, new_b.T, scale_b.reshape(SIDE))


def solution(mesh):
    mesh = Mesh(mesh.devices.reshape(TURNS, PEERS, PEERS), ("x", "z", "rows"))
    split = ("x", "z", "rows")
    in_specs = (P(split, None, None), P(split, None), P(split), P("rows", None), P(split, None))
    out_specs = (P("rows", None), P("rows", None), P())
    return jax.shard_map(shards, mesh=mesh, in_specs=in_specs, out_specs=out_specs, check_vma=False)
```

time: 161 us -> 147 us (0.913)
  blocking collectives: 99.1 us -> 51.3 us
  starting transfers between devices: 22.3 us -> 39.3 us
  waiting for transfers between devices: 5.83 us -> 21.3 us
  Pallas kernels: 28 us -> 30.8 us
  local copies, waits for them, and re-layouts: 3.61 us -> 1.04 us
    all_to_all x6 -> x4, blocking collectives: 99.1 us -> 51.3 us  [exchange(): return lax.all_to_all(x, axis, 0, 0, tiled=True)]
    all_to_all x3 -> x5, waiting for transfers between devices: 5.83 us -> 21.3 us  [exchange(): return lax.all_to_all(x, axis, 0, 0, tiled=True)]
    all_to_all x3 -> x5, starting transfers between devices: 22.3 us -> 36 us  [exchange(): return lax.all_to_all(x, axis, 0, 0, tiled=True)]
    ppermute x0 -> x3, starting transfers between devices: none -> 3.22 us  [shards(): lax.ppermute(near, 'x', [(n, (n + step) % TURNS) for n in range(TURNS)])]
    pallas_call x12 -> x14, Pallas kernels: 22.4 us -> 25.2 us  [the longest x1 6.79 us: shards(): pl.pallas_call(fold, in_specs=[scalars, apart, local, local], out_specs=[...]
    unnamed x7 -> x2, local copies, waits for them, and re-layouts: 3.61 us -> 1.04 us
  transfers between devices with their start and end apart: 3 -> 8, of which waited for: 2 -> 5; matrix products, arithmetic and copies ran while one was open for 0% -> 0% of each run, Pallas kernels for 11% -> 12%
where the time goes in v3:
time: 147 us; the launch traced here: 146 us
  blocking collectives  51.3 us (35%)
  starting transfers between devices  39.3 us (27%)
  Pallas kernels  30.8 us (21%)
  waiting for transfers between devices  21.3 us (14%)
    all_to_all x4, blocking collectives, exchange(): return lax.all_to_all(x, axis, 0, 0, tiled=True)  51.3 us
    all_to_all x5, starting transfers between devices, exchange(): return lax.all_to_all(x, axis, 0, 0, tiled=True)  36 us
    all_to_all x5, waiting for transfers between devices, exchange(): return lax.all_to_all(x, axis, 0, 0, tiled=True)  21.3 us
    pallas_call x1, Pallas kernels, shards(): pl.pallas_call(fold, in_specs=[scalars, apart, local, local], out_specs=[...  6.79 us
    pallas_call x1, Pallas kernels, shards(): call(invert_second, struct(WIDE, WIDE), struct(1, WIDE))(part_b, third)  5.69 us
    pallas_call x1, Pallas kernels, shards(): inverse_a = call(invert_first, struct(WIDE, WIDE))(third)  5.56 us
    pallas_call x1, Pallas kernels, shards(): pl.pallas_call(contract, in_specs=[scalars, apart, local], out_specs=loca...  3.73 us
    ppermute x3, starting transfers between devices, shards(): lax.ppermute(near, 'x', [(n, (n + step) % TURNS) for n in range(TURNS)])  3.22 us
  transfers between devices with their start and end apart: 8, of which 5 were waited for; matrix products, arithmetic and copies ran while one was open for 0% of the time, Pallas kernels for 12%

profile of v3, /device:TPU:1, one launch (start us, length us, event | category | flops | bytes accessed | tf_op | source)
XLA Modules:
  0.0 146.0 jit_solution(937806284811182034)
XLA Ops:
  1.3 0.9 fusion.given_ref
  2.2 0.9 shard_map.76
  3.1 11.9 %all-to-all-start = ((f32[32,8,128]{2,1,0:T(8,128)}), f32[32,8,128]{2,1,0:T(8,128)S(1)}, u32[]{:S(2)}, u32[]{:S(2)}) async-start(f32[32,8,128]{2,1,0:T(8,128)} %get-tuple-element.18), calls=%async_computation | async-start | bytes 262144 | tf_op jit(solution)/shard_map/all_to_all | solution.py:345
  15.0 0.0 copy-start
  15.0 1.0 copy-done
  16.0 1.3 shard_map.77
  17.3 6.8 %all-to-all-done.first_ref.meta_ref = f32[32,8,128]{2,1,0:T(8,128)S(1)} async-done(((f32[32,8,128]{2,1,0:T(8,128)}), f32[32,8,128]{2,1,0:T(8,128)S(1)}, u32[]{:S(2)}, u32[]{:S(2)}) %all-to-all-start) | async-done | bytes 131104 | tf_op jit(solution)/shard_map/all_to_all | solution.py:345
  24.1 11.9 %all_to_all.45.held_ref = f32[8,40,128]{2,1,0:T(8,128)S(1)} all-to-all(f32[8,40,128]{2,1,0:T(8,128)S(1)} %shard_map.78), channel_id=1, replica_groups=mesh['x'=4,'z'=8,'rows'=8] {'rows'}, dimensions={0} | all-to-all | bytes 327680 | tf_op jit(solution)/shard_map/all_to_all | solution.py:345
  36.1 0.4 shard_map.79
  36.5 12.5 %all_to_all.46.third_ref = f32[32,8,128]{2,1,0:T(8,128)S(1)} all-to-all(f32[32,8,128]{2,1,0:T(8,128)S(1)} %shard_map.79), channel_id=1, replica_groups=mesh['x'=4,'z'=8,'rows'=8] {'x','z'}, dimensions={0} | all-to-all | bytes 262144 | tf_op jit(solution)/shard_map/all_to_all | solution.py:345
  48.9 6.8 %shard_map.80 = (f32[6,32,64,128]{3,2,1,0:T(8,128)}, f32[32,8,128]{2,1,0:T(8,128)}) custom-call(s32[8,64]{1,0:T(8,128)S(1)} %get-tuple-element.17.place_ref, f32[6,64,4096]{2,1,0:T(8,128)} %blocks_ref.1, f32[32,8,128]{2,1,0:T(8,128)S(1)} %all_to_all.46.third_ref, f32[32,32,128]{2,1,0:T(8,128)S(1)} %get-tuple-element.20.pairs_ref), custom_call_target="tpu_custom_call" | custom-call | tf_op jit(solution)/shard_map/pallas_call | solution.py:376
  55.7 3.9 %all-to-all-start.3 = ((f32[32,8,128]{2,1,0:T(8,128)}), f32[32,8,128]{2,1,0:T(8,128)S(1)}, u32[]{:S(2)}, u32[]{:S(2)}) async-start(f32[32,8,128]{2,1,0:T(8,128)} %get-tuple-element.22), calls=%async_computation.3 | async-start | bytes 262144 | tf_op jit(solution)/shard_map/all_to_all | solution.py:345
  59.6 5.6 %shard_map.81.inverse_ref = f32[128,128]{1,0:T(8,128)S(1)} custom-call(f32[32,8,128]{2,1,0:T(8,128)S(1)} %all_to_all.46.third_ref), custom_call_target="tpu_custom_call" | custom-call | tf_op jit(solution)/shard_map/pallas_call | solution.py:392
  65.2 3.6 %all-to-all-done.3.part_ref = f32[32,8,128]{2,1,0:T(8,128)S(1)} async-done(((f32[32,8,128]{2,1,0:T(8,128)}), f32[32,8,128]{2,1,0:T(8,128)S(1)}, u32[]{:S(2)}, u32[]{:S(2)}) %all-to-all-start.3) | async-done | bytes 131104 | tf_op jit(solution)/shard_map/all_to_all | solution.py:345
  68.8 1.0 shard_map.82
  69.7 14.6 %all_to_all.47.first_ref = f32[32,8,128]{2,1,0:T(8,128)S(1)} all-to-all(f32[32,8,128]{2,1,0:T(8,128)S(1)} %get-tuple-element.23), channel_id=1, replica_groups=mesh['x'=4,'z'=8,'rows'=8] {'x','z'}, dimensions={0} | all-to-all | bytes 262144 | tf_op jit(solution)/shard_map/all_to_all | solution.py:345
  84.3 0.6 shard_map.84
  85.0 7.4 %all-to-all-start.5 = ((f32[8,8,128]{2,1,0:T(8,128)}), f32[8,8,128]{2,1,0:T(8,128)S(1)}, u32[]{:S(2)}, u32[]{:S(2)}) async-start(f32[8,8,128]{2,1,0:T(8,128)} %shard_map.84), calls=%async_computation.5 | async-start | bytes 65536 | tf_op jit(solution)/shard_map/all_to_all | solution.py:345
  92.3 3.7 %shard_map.83.part_ref = f32[32,8,128]{2,1,0:T(8,128)S(1)} custom-call(s32[8,64]{1,0:T(8,128)S(1)} %get-tuple-element.17.place_ref, f32[6,32,64,128]{3,2,1,0:T(8,128)} %get-tuple-element.21.folded_ref, f32[32,8,128]{2,1,0:T(8,128)S(1)} %all_to_all.47.first_ref), custom_call_target="tpu_custom_call" | custom-call | tf_op jit(solution)/shard_map/pallas_call | solution.py:396
  96.1 1.0 all-to-all-done.5.square_ref
  97.1 12.4 %all_to_all.48.part_ref = f32[32,8,128]{2,1,0:T(8,128)S(1)} all-to-all(f32[32,8,128]{2,1,0:T(8,128)S(1)} %shard_map.85), channel_id=1, replica_groups=mesh['x'=4,'z'=8,'rows'=8] {'x','z'}, dimensions={0} | all-to-all | bytes 262144 | tf_op jit(solution)/shard_map/all_to_all | solution.py:345
  109.5 1.0 shard_map.86
  110.5 3.4 %all-to-all-start.7 = ((f32[8,64,128]{2,1,0:T(8,128)}), f32[8,64,128]{2,1,0:T(8,128)S(1)}, u32[]{:S(2)}, u32[]{:S(2)}) async-start(f32[8,64,128]{2,1,0:T(8,128)} %shard_map.86), calls=%async_computation.7 | async-start | bytes 524288 | tf_op jit(solution)/shard_map/all_to_all | solution.py:345
  113.9 5.7 %shard_map.87 = (f32[128,128]{1,0:T(8,128)S(1)}, f32[1,128]{1,0:T(1,128)S(1)}) custom-call(f32[32,8,128]{2,1,0:T(8,128)S(1)} %all_to_all.48.part_ref, f32[32,8,128]{2,1,0:T(8,128)S(1)} %all_to_all.46.third_ref), custom_call_target="tpu_custom_call" | custom-call | tf_op jit(solution)/shard_map/pallas_call | solution.py:412
  119.6 3.5 %all-to-all-done.7.near_ref = f32[8,64,128]{2,1,0:T(8,128)S(1)} async-done(((f32[8,64,128]{2,1,0:T(8,128)}), f32[8,64,128]{2,1,0:T(8,128)S(1)}, u32[]{:S(2)}, u32[]{:S(2)}) %all-to-all-start.7) | async-done | bytes 262176 | tf_op jit(solution)/shard_map/all_to_all | solution.py:345
  123.1 0.9 shard_map.88
  124.0 0.3 collective-permute-start
  124.4 1.7 %collective-permute-start.1 = (f32[8,64,128]{2,1,0:T(8,128)S(1)}, f32[8,64,128]{2,1,0:T(8,128)S(1)}, u32[]{:S(2)}, u32[]{:S(2)}) collective-permute-start(f32[8,64,128]{2,1,0:T(8,128)S(1)} %get-tuple-element.27.own_ref), channel_id=1, source_target_pairs={{0,128},{64,192},{128,0},{192,64},{1,129},{65,193},{129,1},{193,65... | collective-permute-start | bytes 786440 | tf_op jit(solution)/shard_map/ppermute | solution.py:415
  126.1 1.2 collective-permute-start.2
  127.3 9.5 %all-to-all-start.8 = ((f32[32,8,128]{2,1,0:T(8,128)}), f32[32,8,128]{2,1,0:T(8,128)S(1)}, u32[]{:S(2)}, u32[]{:S(2)}) async-start(f32[32,8,128]{2,1,0:T(8,128)} %get-tuple-element.28), calls=%async_computation.8 | async-start | bytes 262144 | tf_op jit(solution)/shard_map/all_to_all | solution.py:345
  136.8 0.0 collective-permute-done.one_ref
  136.8 0.0 collective-permute-done.1.two_ref
  136.8 0.0 collective-permute-done.2.three_ref
  136.8 1.4 shard_map.89
  138.2 6.3 %all-to-all-done.8.square_ref = f32[32,8,128]{2,1,0:T(8,128)S(1)} async-done(((f32[32,8,128]{2,1,0:T(8,128)}), f32[32,8,128]{2,1,0:T(8,128)S(1)}, u32[]{:S(2)}, u32[]{:S(2)}) %all-to-all-start.8) | async-done | bytes 131104 | tf_op jit(solution)/shard_map/all_to_all | solution.py:345
  144.5 1.4 shard_map.90
  (3 shorter events, 0.1 us)
Async XLA Ops:
  3.1 21.0 %all-to-all-start = ((f32[32,8,128]{2,1,0:T(8,128)}), f32[32,8,128]{2,1,0:T(8,128)S(1)}, u32[]{:S(2)}, u32[]{:S(2)}) async-start(f32[32,8,128]{2,1,0:T(8,128)} %get-tuple-element.18), calls=%async_computation | async-start | bytes 262144 | tf_op jit(solution)/shard_map/all_to_all | solution.py:345
  15.0 1.0 copy-start
  55.7 13.0 %all-to-all-start.3 = ((f32[32,8,128]{2,1,0:T(8,128)}), f32[32,8,128]{2,1,0:T(8,128)S(1)}, u32[]{:S(2)}, u32[]{:S(2)}) async-start(f32[32,8,128]{2,1,0:T(8,128)} %get-tuple-element.22), calls=%async_computation.3 | async-start | bytes 262144 | tf_op jit(solution)/shard_map/all_to_all | solution.py:345
  85.0 12.1 %all-to-all-start.5 = ((f32[8,8,128]{2,1,0:T(8,128)}), f32[8,8,128]{2,1,0:T(8,128)S(1)}, u32[]{:S(2)}, u32[]{:S(2)}) async-start(f32[8,8,128]{2,1,0:T(8,128)} %shard_map.84), calls=%async_computation.5 | async-start | bytes 65536 | tf_op jit(solution)/shard_map/all_to_all | solution.py:345
  110.5 12.6 %all-to-all-start.7 = ((f32[8,64,128]{2,1,0:T(8,128)}), f32[8,64,128]{2,1,0:T(8,128)S(1)}, u32[]{:S(2)}, u32[]{:S(2)}) async-start(f32[8,64,128]{2,1,0:T(8,128)} %shard_map.86), calls=%async_computation.7 | async-start | bytes 524288 | tf_op jit(solution)/shard_map/all_to_all | solution.py:345
  124.0 12.8 %collective-permute-start = (f32[8,64,128]{2,1,0:T(8,128)S(1)}, f32[8,64,128]{2,1,0:T(8,128)S(1)}, u32[]{:S(2)}, u32[]{:S(2)}) collective-permute-start(f32[8,64,128]{2,1,0:T(8,128)S(1)} %get-tuple-element.27.own_ref), channel_id=1, source_target_pairs={{0,64},{64,128},{128,192},{192,0},{1,65},{65,129},{129,193},{193,1... | collective-permute-start | bytes 786440 | tf_op jit(solution)/shard_map/ppermute | solution.py:415
  124.4 12.5 %collective-permute-start.1 = (f32[8,64,128]{2,1,0:T(8,128)S(1)}, f32[8,64,128]{2,1,0:T(8,128)S(1)}, u32[]{:S(2)}, u32[]{:S(2)}) collective-permute-start(f32[8,64,128]{2,1,0:T(8,128)S(1)} %get-tuple-element.27.own_ref), channel_id=1, source_target_pairs={{0,128},{64,192},{128,0},{192,64},{1,129},{65,193},{129,1},{193,65... | collective-permute-start | bytes 786440 | tf_op jit(solution)/shard_map/ppermute | solution.py:415
  126.1 10.7 %collective-permute-start.2 = (f32[8,64,128]{2,1,0:T(8,128)S(1)}, f32[8,64,128]{2,1,0:T(8,128)S(1)}, u32[]{:S(2)}, u32[]{:S(2)}) collective-permute-start(f32[8,64,128]{2,1,0:T(8,128)S(1)} %get-tuple-element.27.own_ref), channel_id=1, source_target_pairs={{0,192},{64,0},{128,64},{192,128},{1,193},{65,1},{129,65},{193,129... | collective-permute-start | bytes 786440 | tf_op jit(solution)/shard_map/ppermute | solution.py:415
  127.3 17.3 %all-to-all-start.8 = ((f32[32,8,128]{2,1,0:T(8,128)}), f32[32,8,128]{2,1,0:T(8,128)S(1)}, u32[]{:S(2)}, u32[]{:S(2)}) async-start(f32[32,8,128]{2,1,0:T(8,128)} %get-tuple-element.28), calls=%async_computation.8 | async-start | bytes 262144 | tf_op jit(solution)/shard_map/all_to_all | solution.py:345

commit v4 on v3

--- a/solution.py
+++ b/solution.py
@@ -10,6 +10,8 @@
 HALF = 32
 WIDE = 128
 STEP = 8
+BEFORE = 10
+AFTER = 8
 TILE = 8
 SLOTS = 6
 LEAD = 2
@@ -57,18 +59,29 @@
     return fold_halves(jnp.where(low(total.shape), total, swap(total)))
 
 
-def inverse(gram):
-    shape = gram.shape
-    row = lax.broadcasted_iota(jnp.int32, shape, 0)
-    lane = lax.broadcasted_iota(jnp.int32, shape, 1)
-    work = jnp.where(lane < SIDE, gram, jnp.where(lane - SIDE == row, 1.0, 0.0))
-    for k in range(SIDE):
+def begin_inverse(gram):
+    row = lax.broadcasted_iota(jnp.int32, gram.shape, 0)
+    lane = lax.broadcasted_iota(jnp.int32, gram.shape, 1)
+    return jnp.where(lane < SIDE, gram, jnp.where(lane - SIDE == row, 1.0, 0.0))
+
+
+def eliminate(work, first, last):
+    row = lax.broadcasted_iota(jnp.int32, work.shape, 0)
+    for k in range(first, last):
         line = work[k : k + 1, :] / work[k : k + 1, k : k + 1]
         column = work[:, k : k + 1]
         work = jnp.where(row == k, line, work - column * line)
+    return work
+
+
+def end_inverse(work):
     zero = jnp.zeros_like(work)
-    mask = lane < SIDE
+    mask = low(work.shape)
     return jnp.concatenate([jnp.where(mask, swap(work), zero), jnp.where(mask, zero, work)], axis=0)
+
+
+def inverse(gram):
+    return end_inverse(eliminate(begin_inverse(gram), 0, SIDE))
 
 
 def held(shape):
@@ -155,15 +168,13 @@
     pairs_ref,
     folded_ref,
     out_ref,
+    inverse_ref,
     held,
     made,
     weights,
-    terms,
     held_sem,
     made_sem,
 ):
-    count = place_ref[3, 0]
-
     def load(slot):
         return pltpu.make_async_copy(blocks_ref.at[slot], held.at[slot], held_sem.at[slot])
 
@@ -171,11 +182,7 @@
         return pltpu.make_async_copy(made.at[slot], folded_ref.at[slot], made_sem.at[slot])
 
     for slot in range(SLOTS):
-
-        @pl.when(slot < count)
-        def _():
-            load(slot).start()
-
+        load(slot).start()
     for slot in range(SLOTS):
         packed = third_ref[:, slot + LEAD, :]
         mask, other = low(packed.shape), swap(packed)
@@ -192,10 +199,12 @@
         high, rest = split(twin)
         twin = jnp.concatenate([high, rest], axis=1)
         weights[slot] = jnp.concatenate([twin, twin], axis=0)
-    terms[...] = jnp.zeros_like(terms)
-
-    @pl.loop(0, count)
-    def _(slot):
+    out_ref[:, :LEAD, :] = jnp.zeros((OWNERS, LEAD, WIDE), jnp.float32)
+    work = begin_inverse(unfold_halves(third_ref[:, 0, :] * third_ref[:, 1, :]))
+    work = eliminate(work, 0, BEFORE)
+    groups, inner = SLOTS * HALF // STEP, SIDE - BEFORE - AFTER
+    group = 0
+    for slot in range(SLOTS):
         pairs = pairs_ref[place_ref[1, slot] % OWNERS]
         load(slot).wait()
         total = jnp.zeros((SIDE, WIDE), jnp.float32)
@@ -211,21 +220,13 @@
                 piece = both[n * SIDE : (n + 1) * SIDE]
                 made[slot, at + n] = piece
                 total += piece * pairs[at + n : at + n + 1, :]
+            work = eliminate(work, BEFORE + group * inner // groups, BEFORE + (group + 1) * inner // groups)
+            group += 1
         store(slot).start()
-        terms[slot + LEAD] = fold_halves(total + swap(total))
-
-    for k in range(TILE):
-        out_ref[:, k, :] = terms[k]
-
-    for slot in range(SLOTS):
-
-        @pl.when(slot < count)
-        def _():
-            store(slot).wait()
-
-
-def invert_first(third_ref, out_ref):
-    out_ref[...] = inverse(unfold_halves(third_ref[:, 0, :] * third_ref[:, 1, :]))
+        out_ref[:, slot + LEAD, :] = fold_halves(total + swap(total))
+    inverse_ref[...] = end_inverse(eliminate(work, SIDE - AFTER, SIDE))
+    for slot in range(SLOTS):
+        store(slot).wait()
 
 
 def solve_first(part_ref, meta_ref, inverse_ref, out_ref, solved_ref):
@@ -242,33 +243,20 @@
     out_ref[...] = jnp.broadcast_to(total[None], out_ref.shape)
 
 
-def contract(place_ref, folded_ref, first_ref, out_ref, held, first_rows, terms, spaced, held_sem):
-    count = place_ref[3, 0]
-
+def contract(folded_ref, first_ref, out_ref, held, spaced, held_sem):
     def load(slot):
         return pltpu.make_async_copy(folded_ref.at[slot], held.at[slot], held_sem.at[slot])
 
     for slot in range(SLOTS):
-
-        @pl.when(slot < count)
-        def _():
-            load(slot).start()
-
-    terms[...] = jnp.zeros_like(terms)
-    for slot in range(SLOTS):
-        first_rows[slot] = first_ref[:, slot + LEAD, :]
-
-    @pl.loop(0, count)
-    def _(slot):
-        first = unfold_halves(first_rows[slot])
+        load(slot).start()
+    out_ref[:, :LEAD, :] = jnp.zeros((OWNERS, LEAD, WIDE), jnp.float32)
+    for slot in range(SLOTS):
+        first = unfold_halves(first_ref[:, slot + LEAD, :])
         load(slot).wait()
         term = jnp.sum(held[slot] * first[None], axis=1)
-        spaced[pl.ds(0, HALF, stride=2), :] = term
-        spaced[pl.ds(1, HALF, stride=2), :] = swap(term)
-        terms[slot + LEAD] = jnp.where(low(term.shape), spaced[:HALF, :], swap(spaced[HALF:, :]))
-
-    for k in range(TILE):
-        out_ref[:, k, :] = terms[k]
+        spaced[slot, pl.ds(0, HALF, stride=2), :] = term
+        spaced[slot, pl.ds(1, HALF, stride=2), :] = swap(term)
+        out_ref[:, slot + LEAD, :] = jnp.where(low(term.shape), spaced[slot, :HALF, :], swap(spaced[slot, HALF:, :]))
 
 
 def insert(part_ref, square_ref, out_ref):
@@ -317,24 +305,30 @@
         out_ref[:, GROUP // 2 + pair * WIDE : GROUP // 2 + (pair + 1) * WIDE] = both[SIDE:]
 
 
-def collect(parts, which, scale, out_ref):
+def collect(which, own_ref, one_ref, two_ref, three_ref, out_ref, solved):
     own = lax.axis_index("x")
-    for step, part in enumerate(parts):
+    for step, part in enumerate((own_ref, one_ref, two_ref, three_ref)):
         rows = part[:, which * HALF : (which + 1) * HALF, :]
-        out_ref[pl.ds((own + TURNS - step) % TURNS * PEERS, PEERS)] = rows if scale is None else rows / scale
-
-
-def finish_first(own_ref, one_ref, two_ref, three_ref, new_ref, solved):
-    collect((own_ref, one_ref, two_ref, three_ref), 1, None, solved)
-    turn(solved, new_ref)
-
-
-def finish_second(own_ref, one_ref, two_ref, three_ref, square_ref, new_ref, scale_ref, solved):
+        solved[pl.ds((own + TURNS - step) % TURNS * PEERS, PEERS)] = rows
+    turn(solved, out_ref)
+
+
+def collect_first(*refs):
+    collect(1, *refs)
+
+
+def collect_second(*refs):
+    collect(0, *refs)
+
+
+def finish(turned_ref, square_ref, new_ref, scale_ref):
     total = jnp.sum(square_ref[:, 0, :], axis=0, keepdims=True)
     scale = jnp.sqrt((total + swap(total)) / ROWS + 1e-06)
     scale_ref[...] = scale[:, :SIDE]
-    collect((own_ref, one_ref, two_ref, three_ref), 0, scale, solved)
-    turn(solved, new_ref)
+    shape = (SIDE, WIDE)
+    row, lane = lax.broadcasted_iota(jnp.int32, shape, 0), lax.broadcasted_iota(jnp.int32, shape, 1)
+    down = jnp.sum(jnp.where(row == lane, scale, 0.0), axis=1, keepdims=True)
+    new_ref[...] = turned_ref[...] / down
 
 
 def struct(*shape):
@@ -373,40 +367,36 @@
     )(factor_b.T)
     held = exchange(call(relay, struct(PEERS, HALF + TILE, WIDE))(meta, gram_b), "rows")
     third = exchange(call(answer, struct(*small))(meta, held), SLAB)
-    folded, part_a = pl.pallas_call(
+    folded, part_a, inverse_a = pl.pallas_call(
         fold,
         in_specs=[scalars, apart, local, local],
-        out_specs=[apart, local],
-        out_shape=(struct(SLOTS, HALF, SIDE, WIDE), struct(*small)),
+        out_specs=[apart, local, local],
+        out_shape=(struct(SLOTS, HALF, SIDE, WIDE), struct(*small), struct(WIDE, WIDE)),
         scratch_shapes=[
             pltpu.VMEM((SLOTS, SIDE, SIDE * SIDE), jnp.float32),
             pltpu.VMEM((SLOTS, HALF, SIDE, WIDE), jnp.float32),
             pltpu.VMEM((SLOTS, 2 * WIDE, 2 * WIDE), jnp.bfloat16),
-            pltpu.VMEM((TILE, HALF, WIDE), jnp.float32),
             pltpu.SemaphoreType.DMA((SLOTS,)),
             pltpu.SemaphoreType.DMA((SLOTS,)),
         ],
         compiler_params=LARGE,
     )(place, blocks, third, pairs)
     part_a = exchange(part_a, SLAB)
-    inverse_a = call(invert_first, struct(WIDE, WIDE))(third)
     answer_a, solved_a = call(solve_first, struct(*small), struct(HALF, WIDE))(part_a, meta, inverse_a)
     first = exchange(answer_a, SLAB)
     square_a = exchange(call(share_gram, struct(PEERS, TILE, WIDE))(first), "rows")
     part_b = pl.pallas_call(
         contract,
-        in_specs=[scalars, apart, local],
+        in_specs=[apart, local],
         out_specs=local,
         out_shape=struct(*small),
         scratch_shapes=[
             pltpu.VMEM((SLOTS, HALF, SIDE, WIDE), jnp.float32),
-            pltpu.VMEM((SLOTS, HALF, WIDE), jnp.float32),
-            pltpu.VMEM((TILE, HALF, WIDE), jnp.float32),
-            pltpu.VMEM((SIDE, WIDE), jnp.float32),
+            pltpu.VMEM((SLOTS, SIDE, WIDE), jnp.float32),
             pltpu.SemaphoreType.DMA((SLOTS,)),
         ],
         compiler_params=LARGE,
-    )(place, folded, first)
+    )(folded, first)
     part_b = exchange(call(insert, struct(*small))(part_b, square_a), SLAB)
     near = exchange(call(sum_second, struct(PEERS, SIDE, WIDE))(part_b, meta, solved_a), "z")
     inverse_b, scale_a = call(invert_second, struct(WIDE, WIDE), struct(1, WIDE))(part_b, third)
@@ -416,15 +406,11 @@
     ]
     square_b = exchange(square_b, ("x", "rows"))
     scratch = [pltpu.VMEM(full, jnp.float32)]
-    new_a = pl.pallas_call(
-        finish_first, out_shape=struct(SIDE, GROUP), scratch_shapes=scratch, compiler_params=LIMIT
-    )(*parts)
-    new_b, scale_b = pl.pallas_call(
-        finish_second,
-        out_shape=(struct(SIDE, GROUP), struct(1, SIDE)),
-        scratch_shapes=scratch,
-        compiler_params=LIMIT,
-    )(*parts, square_b)
+    new_a, turned_b = (
+        pl.pallas_call(body, out_shape=struct(SIDE, GROUP), scratch_shapes=scratch, compiler_params=LIMIT)(*parts)
+        for body in (collect_first, collect_second)
+    )
+    new_b, scale_b = call(finish, struct(SIDE, GROUP), struct(1, SIDE))(turned_b, square_b)
     return (new_a.T, new_b.T, scale_b.reshape(SIDE))
 
 

time: 147 us -> 144 us (0.980)
  blocking collectives: 51.3 us -> 62.2 us
  Pallas kernels: 30.8 us -> 25.2 us
  starting transfers between devices: 39.3 us -> 35.3 us
  waiting for transfers between devices: 21.3 us -> 17.8 us
    all_to_all x4 -> x5, blocking collectives: 51.3 us -> 62.2 us  [exchange(): return lax.all_to_all(x, axis, 0, 0, tiled=True)]
    pallas_call x4, Pallas kernels: 12.1 us -> 5.98 us  [the longest x1 3.06 us: shards(): pl.pallas_call(contract, in_specs=[apart, local], out_specs=local, out_sh...]
    all_to_all x5 -> x4, waiting for transfers between devices: 21.3 us -> 15.7 us  [exchange(): return lax.all_to_all(x, axis, 0, 0, tiled=True)]
    all_to_all x5 -> x4, starting transfers between devices: 36 us -> 33.2 us  [exchange(): return lax.all_to_all(x, axis, 0, 0, tiled=True)]
    ppermute x3, waiting for transfers between devices: 0.01 us -> 2.05 us  [shards(): lax.ppermute(near, 'x', [(n, (n + step) % TURNS) for n in range(TURNS)])]
  transfers between devices with their start and end apart: 8 -> 7, of which waited for: 5 -> 5; matrix products, arithmetic and copies ran while one was open for 0% -> 0% of each run, Pallas kernels for 12% -> 8%
where the time goes in v4:
time: 144 us
  blocking collectives  62.2 us (43%)
  starting transfers between devices  35.3 us (25%)
  Pallas kernels  25.2 us (18%)
  waiting for transfers between devices  17.8 us (12%)
    all_to_all x5, blocking collectives, exchange(): return lax.all_to_all(x, axis, 0, 0, tiled=True)  62.2 us
    all_to_all x4, starting transfers between devices, exchange(): return lax.all_to_all(x, axis, 0, 0, tiled=True)  33.2 us
    all_to_all x4, waiting for transfers between devices, exchange(): return lax.all_to_all(x, axis, 0, 0, tiled=True)  15.7 us
    pallas_call x1, Pallas kernels, shards(): pl.pallas_call(fold, in_specs=[scalars, apart, local, local], out_specs=[...  7.31 us
    pallas_call x1, Pallas kernels, shards(): call(invert_second, struct(WIDE, WIDE), struct(1, WIDE))(part_b, third)  5.69 us
    pallas_call x1, Pallas kernels, shards(): pl.pallas_call(contract, in_specs=[apart, local], out_specs=local, out_sh...  3.06 us
  transfers between devices with their start and end apart: 7, of which 5 were waited for; matrix products, arithmetic and copies ran while one was open for 0% of the time, Pallas kernels for 8%

profile of v4, /device:TPU:1, one launch (start us, length us, event | category | flops | bytes accessed | tf_op | source)
XLA Modules:
  0.0 143.7 jit_solution(11516592421129666605)
XLA Ops:
  1.3 0.9 fusion.given_ref
  2.2 0.9 shard_map.76
  3.1 11.9 %all-to-all-start = ((f32[32,8,128]{2,1,0:T(8,128)}), f32[32,8,128]{2,1,0:T(8,128)S(1)}, u32[]{:S(2)}, u32[]{:S(2)}) async-start(f32[32,8,128]{2,1,0:T(8,128)} %get-tuple-element.19), calls=%async_computation | async-start | bytes 262144 | tf_op jit(solution)/shard_map/all_to_all | solution.py:339
  15.0 0.0 copy-start
  15.0 1.0 copy-done
  16.0 1.3 shard_map.77
  17.3 6.8 %all-to-all-done.first_ref.meta_ref = f32[32,8,128]{2,1,0:T(8,128)S(1)} async-done(((f32[32,8,128]{2,1,0:T(8,128)}), f32[32,8,128]{2,1,0:T(8,128)S(1)}, u32[]{:S(2)}, u32[]{:S(2)}) %all-to-all-start) | async-done | bytes 131104 | tf_op jit(solution)/shard_map/all_to_all | solution.py:339
  24.1 11.9 %all_to_all.45.held_ref = f32[8,40,128]{2,1,0:T(8,128)S(1)} all-to-all(f32[8,40,128]{2,1,0:T(8,128)S(1)} %shard_map.78), channel_id=1, replica_groups=mesh['x'=4,'z'=8,'rows'=8] {'rows'}, dimensions={0} | all-to-all | bytes 327680 | tf_op jit(solution)/shard_map/all_to_all | solution.py:339
  36.1 0.4 shard_map.79
  36.5 12.5 %all_to_all.46.third_ref = f32[32,8,128]{2,1,0:T(8,128)S(1)} all-to-all(f32[32,8,128]{2,1,0:T(8,128)S(1)} %shard_map.79), channel_id=1, replica_groups=mesh['x'=4,'z'=8,'rows'=8] {'x','z'}, dimensions={0} | all-to-all | bytes 262144 | tf_op jit(solution)/shard_map/all_to_all | solution.py:339
  48.9 7.3 %shard_map.80 = (f32[6,32,64,128]{3,2,1,0:T(8,128)}, f32[32,8,128]{2,1,0:T(8,128)S(1)}, f32[128,128]{1,0:T(8,128)S(1)}) custom-call(s32[8,64]{1,0:T(8,128)S(1)} %get-tuple-element.18.place_ref, f32[6,64,4096]{2,1,0:T(8,128)} %blocks_ref.1, f32[32,8,128]{2,1,0:T(8,128)S(1)} %all_to_all.46.third_ref, f32[32,32,128]{2,1,0:T(8,128)S(1)} %get-tuple-element.21.pairs_ref), custom_call_target="tpu_custom_call" | custom-call | tf_op jit(solution)/shard_map/pallas_call | solution.py:370
  56.3 12.7 %all_to_all.47.part_ref = f32[32,8,128]{2,1,0:T(8,128)S(1)} all-to-all(f32[32,8,128]{2,1,0:T(8,128)S(1)} %get-tuple-element.23), channel_id=1, replica_groups=mesh['x'=4,'z'=8,'rows'=8] {'x','z'}, dimensions={0} | all-to-all | bytes 262144 | tf_op jit(solution)/shard_map/all_to_all | solution.py:339
  69.0 1.0 shard_map.81
  69.9 12.6 %all_to_all.48.first_ref = f32[32,8,128]{2,1,0:T(8,128)S(1)} all-to-all(f32[32,8,128]{2,1,0:T(8,128)S(1)} %get-tuple-element.25), channel_id=1, replica_groups=mesh['x'=4,'z'=8,'rows'=8] {'x','z'}, dimensions={0} | all-to-all | bytes 262144 | tf_op jit(solution)/shard_map/all_to_all | solution.py:339
  82.6 0.6 shard_map.83
  83.2 7.9 %all-to-all-start.5 = ((f32[8,8,128]{2,1,0:T(8,128)}), f32[8,8,128]{2,1,0:T(8,128)S(1)}, u32[]{:S(2)}, u32[]{:S(2)}) async-start(f32[8,8,128]{2,1,0:T(8,128)} %shard_map.83), calls=%async_computation.5 | async-start | bytes 65536 | tf_op jit(solution)/shard_map/all_to_all | solution.py:339
  91.1 3.1 %shard_map.82.part_ref = f32[32,8,128]{2,1,0:T(8,128)S(1)} custom-call(f32[6,32,64,128]{3,2,1,0:T(8,128)} %get-tuple-element.22.folded_ref, f32[32,8,128]{2,1,0:T(8,128)S(1)} %all_to_all.48.first_ref), custom_call_target="tpu_custom_call" | custom-call | tf_op jit(solution)/shard_map/pallas_call | solution.py:388
  94.2 1.7 %all-to-all-done.5.square_ref = f32[8,8,128]{2,1,0:T(8,128)S(1)} async-done(((f32[8,8,128]{2,1,0:T(8,128)}), f32[8,8,128]{2,1,0:T(8,128)S(1)}, u32[]{:S(2)}, u32[]{:S(2)}) %all-to-all-start.5) | async-done | bytes 32800 | tf_op jit(solution)/shard_map/all_to_all | solution.py:339
  95.9 12.4 %all_to_all.49.part_ref = f32[32,8,128]{2,1,0:T(8,128)S(1)} all-to-all(f32[32,8,128]{2,1,0:T(8,128)S(1)} %shard_map.84), channel_id=1, replica_groups=mesh['x'=4,'z'=8,'rows'=8] {'x','z'}, dimensions={0} | all-to-all | bytes 262144 | tf_op jit(solution)/shard_map/all_to_all | solution.py:339
  108.3 1.0 shard_map.85
  109.3 3.4 %all-to-all-start.7 = ((f32[8,64,128]{2,1,0:T(8,128)}), f32[8,64,128]{2,1,0:T(8,128)S(1)}, u32[]{:S(2)}, u32[]{:S(2)}) async-start(f32[8,64,128]{2,1,0:T(8,128)} %shard_map.85), calls=%async_computation.7 | async-start | bytes 524288 | tf_op jit(solution)/shard_map/all_to_all | solution.py:339
  112.8 5.7 %shard_map.86 = (f32[128,128]{1,0:T(8,128)S(1)}, f32[1,128]{1,0:T(1,128)S(1)}) custom-call(f32[32,8,128]{2,1,0:T(8,128)S(1)} %all_to_all.49.part_ref, f32[32,8,128]{2,1,0:T(8,128)S(1)} %all_to_all.46.third_ref), custom_call_target="tpu_custom_call" | custom-call | tf_op jit(solution)/shard_map/pallas_call | solution.py:402
  118.5 3.5 %all-to-all-done.7.near_ref = f32[8,64,128]{2,1,0:T(8,128)S(1)} async-done(((f32[8,64,128]{2,1,0:T(8,128)}), f32[8,64,128]{2,1,0:T(8,128)S(1)}, u32[]{:S(2)}, u32[]{:S(2)}) %all-to-all-start.7) | async-done | bytes 262176 | tf_op jit(solution)/shard_map/all_to_all | solution.py:339
  122.0 0.9 shard_map.87
  122.9 0.9 collective-permute-start.2
  123.8 1.2 collective-permute-start.1
  125.0 0.0 collective-permute-start
  125.0 10.0 %all-to-all-start.8 = ((f32[32,8,128]{2,1,0:T(8,128)}), f32[32,8,128]{2,1,0:T(8,128)S(1)}, u32[]{:S(2)}, u32[]{:S(2)}) async-start(f32[32,8,128]{2,1,0:T(8,128)} %get-tuple-element.30), calls=%async_computation.8 | async-start | bytes 262144 | tf_op jit(solution)/shard_map/all_to_all | solution.py:339
  135.0 0.0 collective-permute-done.2.refs_3_
  135.0 0.0 collective-permute-done.1.refs_2_
  135.0 2.0 %collective-permute-done.refs_1_ = f32[8,64,128]{2,1,0:T(8,128)S(1)} collective-permute-done((f32[8,64,128]{2,1,0:T(8,128)S(1)}, f32[8,64,128]{2,1,0:T(8,128)S(1)}, u32[]{:S(2)}, u32[]{:S(2)}) %collective-permute-start) | collective-permute-done | bytes 262176 | tf_op jit(solution)/shard_map/ppermute | solution.py:405
  137.1 0.6 shard_map.89.turned_ref
  137.6 1.4 shard_map.88
  139.0 3.7 %all-to-all-done.8.square_ref = f32[32,8,128]{2,1,0:T(8,128)S(1)} async-done(((f32[32,8,128]{2,1,0:T(8,128)}), f32[32,8,128]{2,1,0:T(8,128)S(1)}, u32[]{:S(2)}, u32[]{:S(2)}) %all-to-all-start.8) | async-done | bytes 131104 | tf_op jit(solution)/shard_map/all_to_all | solution.py:339
  142.7 1.0 shard_map.90
  (3 shorter events, 0.1 us)
Async XLA Ops:
  3.1 21.0 %all-to-all-start = ((f32[32,8,128]{2,1,0:T(8,128)}), f32[32,8,128]{2,1,0:T(8,128)S(1)}, u32[]{:S(2)}, u32[]{:S(2)}) async-start(f32[32,8,128]{2,1,0:T(8,128)} %get-tuple-element.19), calls=%async_computation | async-start | bytes 262144 | tf_op jit(solution)/shard_map/all_to_all | solution.py:339
  15.0 1.0 copy-start
  83.2 12.7 %all-to-all-start.5 = ((f32[8,8,128]{2,1,0:T(8,128)}), f32[8,8,128]{2,1,0:T(8,128)S(1)}, u32[]{:S(2)}, u32[]{:S(2)}) async-start(f32[8,8,128]{2,1,0:T(8,128)} %shard_map.83), calls=%async_computation.5 | async-start | bytes 65536 | tf_op jit(solution)/shard_map/all_to_all | solution.py:339
  109.3 12.6 %all-to-all-start.7 = ((f32[8,64,128]{2,1,0:T(8,128)}), f32[8,64,128]{2,1,0:T(8,128)S(1)}, u32[]{:S(2)}, u32[]{:S(2)}) async-start(f32[8,64,128]{2,1,0:T(8,128)} %shard_map.85), calls=%async_computation.7 | async-start | bytes 524288 | tf_op jit(solution)/shard_map/all_to_all | solution.py:339
  122.9 12.1 %collective-permute-start.2 = (f32[8,64,128]{2,1,0:T(8,128)S(1)}, f32[8,64,128]{2,1,0:T(8,128)S(1)}, u32[]{:S(2)}, u32[]{:S(2)}) collective-permute-start(f32[8,64,128]{2,1,0:T(8,128)S(1)} %get-tuple-element.29.refs_0_), channel_id=1, source_target_pairs={{0,192},{64,0},{128,64},{192,128},{1,193},{65,1},{129,65},{193,129... | collective-permute-start | bytes 786440 | tf_op jit(solution)/shard_map/ppermute | solution.py:405
  123.8 11.2 %collective-permute-start.1 = (f32[8,64,128]{2,1,0:T(8,128)S(1)}, f32[8,64,128]{2,1,0:T(8,128)S(1)}, u32[]{:S(2)}, u32[]{:S(2)}) collective-permute-start(f32[8,64,128]{2,1,0:T(8,128)S(1)} %get-tuple-element.29.refs_0_), channel_id=1, source_target_pairs={{0,128},{64,192},{128,0},{192,64},{1,129},{65,193},{129,1},{193,65... | collective-permute-start | bytes 786440 | tf_op jit(solution)/shard_map/ppermute | solution.py:405
  125.0 12.0 %collective-permute-start = (f32[8,64,128]{2,1,0:T(8,128)S(1)}, f32[8,64,128]{2,1,0:T(8,128)S(1)}, u32[]{:S(2)}, u32[]{:S(2)}) collective-permute-start(f32[8,64,128]{2,1,0:T(8,128)S(1)} %get-tuple-element.29.refs_0_), channel_id=1, source_target_pairs={{0,64},{64,128},{128,192},{192,0},{1,65},{65,129},{129,193},{193,1... | collective-permute-start | bytes 786440 | tf_op jit(solution)/shard_map/ppermute | solution.py:405
  125.0 17.7 %all-to-all-start.8 = ((f32[32,8,128]{2,1,0:T(8,128)}), f32[32,8,128]{2,1,0:T(8,128)S(1)}, u32[]{:S(2)}, u32[]{:S(2)}) async-start(f32[32,8,128]{2,1,0:T(8,128)} %get-tuple-element.30), calls=%async_computation.8 | async-start | bytes 262144 | tf_op jit(solution)/shard_map/all_to_all | solution.py:339

commit v5 on v4

--- a/solution.py
+++ b/solution.py
@@ -88,10 +88,24 @@
     return lax.broadcasted_iota(jnp.int32, shape, 0) % TILE >= LEAD
 
 
-def pick(meta, at):
+def pick(meta):
     lane = lax.broadcasted_iota(jnp.int32, meta.shape, 1)
-    hit = (meta == (lane - at).astype(jnp.float32)) & (lane >= at) & (lane < at + OWNERS) & held(meta.shape)
+    hit = (meta == (lane % OWNERS).astype(jnp.float32)) & (lane < 2 * OWNERS) & held(meta.shape)
     return jnp.where(hit, 1.0, 0.0)
+
+
+def choose(chosen, values, chosen_dim=0):
+    high = values.astype(jnp.bfloat16)
+    rest = values - high.astype(jnp.float32)
+    middle = rest.astype(jnp.bfloat16)
+    last = (rest - middle.astype(jnp.float32)).astype(jnp.bfloat16)
+    parts = lax.dot_general(
+        chosen,
+        jnp.concatenate([high, middle, last], axis=1),
+        (((1 - chosen_dim,), (0,)), ((), ())),
+        preferred_element_type=jnp.float32,
+    )
+    return parts[:, :WIDE] + (parts[:, WIDE : 2 * WIDE] + parts[:, 2 * WIDE :])
 
 
 def lines(ref):
@@ -149,7 +163,7 @@
     shape = (OWNERS * TILE, PEERS * OWNERS)
     lane = lax.broadcasted_iota(jnp.int32, shape, 1).astype(jnp.float32)
     stock = held_ref[:, :HALF, :].reshape(PEERS * OWNERS, WIDE)
-    found = product(jnp.where((wanted == lane) & held(shape), 1.0, 0.0), stock)
+    found = choose(jnp.where((wanted == lane) & held(shape), 1.0, 0.0).astype(jnp.bfloat16), stock)
     grams = jnp.sum(held_ref[:, HALF:, :], axis=0)
     out_ref[...] = found.reshape(OWNERS, TILE, WIDE)
     out_ref[:, 0, :] = jnp.broadcast_to(grams[0:1], (OWNERS, WIDE))
@@ -230,26 +244,27 @@
 
 
 def solve_first(part_ref, meta_ref, inverse_ref, out_ref, solved_ref):
-    chosen = pick(lines(meta_ref), 0)
-    solved = product(product(chosen, lines(part_ref), 0, 0), inverse_ref[...])
-    out_ref[...] = product(chosen, solved).reshape(OWNERS, TILE, WIDE)
-    solved = solved[:OWNERS]
+    chosen = pick(lines(meta_ref)).astype(jnp.bfloat16)
+    solved = product(choose(chosen, lines(part_ref), 1)[:OWNERS], inverse_ref[...])
+    solved_ref[...] = solved
+    blank = jnp.zeros((WIDE - OWNERS, WIDE), jnp.float32)
+    out_ref[...] = choose(chosen, jnp.concatenate([solved, blank], axis=0)).reshape(OWNERS, TILE, WIDE)
     out_ref[:, 0, :] = gram_packed(solved)
-    solved_ref[...] = solved
 
 
 def share_gram(first_ref, out_ref):
     total = jnp.sum(first_ref[:, 0, :], axis=0, keepdims=True)
-    out_ref[...] = jnp.broadcast_to(total[None], out_ref.shape)
-
-
-def contract(folded_ref, first_ref, out_ref, held, spaced, held_sem):
+    out_ref[...] = jnp.broadcast_to(total, out_ref.shape)
+
+
+def contract(folded_ref, first_ref, meta_ref, out_ref, turned_ref, held, spaced, held_sem):
     def load(slot):
         return pltpu.make_async_copy(folded_ref.at[slot], held.at[slot], held_sem.at[slot])
 
     for slot in range(SLOTS):
         load(slot).start()
     out_ref[:, :LEAD, :] = jnp.zeros((OWNERS, LEAD, WIDE), jnp.float32)
+    turned_ref[...] = pick(lines(meta_ref)).T.astype(jnp.bfloat16)
     for slot in range(SLOTS):
         first = unfold_halves(first_ref[:, slot + LEAD, :])
         load(slot).wait()
@@ -259,32 +274,32 @@
         out_ref[:, slot + LEAD, :] = jnp.where(low(term.shape), spaced[slot, :HALF, :], swap(spaced[slot, HALF:, :]))
 
 
-def insert(part_ref, square_ref, out_ref):
+def insert(part_ref, square_ref, other_ref, out_ref):
     out_ref[...] = part_ref[...]
-    total = jnp.sum(square_ref[:, 0, :], axis=0, keepdims=True)
-    out_ref[:, 0, :] = jnp.broadcast_to(total, (OWNERS, WIDE))
-
-
-def sum_second(part_ref, meta_ref, solved_ref, out_ref):
-    total = product(pick(lines(meta_ref), OWNERS), lines(part_ref), 0, 0)[OWNERS : 2 * OWNERS]
+    out_ref[:, 0, :] = jnp.broadcast_to(square_ref[0:1, :] + other_ref[0:1, :], (OWNERS, WIDE))
+
+
+def sum_second(part_ref, turned_ref, solved_ref, out_ref, square_ref):
+    total = choose(turned_ref[OWNERS : 2 * OWNERS, :], lines(part_ref))
     both = jnp.concatenate([total, solved_ref[...]], axis=0)
     out_ref[...] = jnp.broadcast_to(both[None], out_ref.shape)
-
-
-def invert_second(part_ref, third_ref, out_ref, scale_ref):
-    square = unfold_halves(part_ref[:, 0, :])
+    square_ref[...] = part_ref[:, 0, :]
+
+
+def invert_second(own_ref, one_ref, two_ref, three_ref, third_ref, out_ref, scale_ref):
+    square = unfold_halves(own_ref[...] + one_ref[...] + two_ref[...] + three_ref[...])
     shape = square.shape
     row = lax.broadcasted_iota(jnp.int32, shape, 0)
     lane = lax.broadcasted_iota(jnp.int32, shape, 1)
     means = jnp.where(row == lane % SIDE, square, 0.0) / ROWS
     along = jnp.sqrt(jnp.sum(means, axis=0, keepdims=True) + 1e-06)
     down = jnp.sqrt(jnp.sum(jnp.where(lane < SIDE, means, 0.0), axis=1, keepdims=True) + 1e-06)
-    scale_ref[...] = along
+    scale_ref[...] = 1.0 / along
     out_ref[...] = inverse(square / along / down * unfold_halves(third_ref[:, 1, :]))
 
 
 def solve_second(near_ref, inverse_ref, scale_ref, out_ref, square_ref):
-    near = near_ref[...] / scale_ref[...]
+    near = near_ref[...] * scale_ref[...]
     solved = product(near[:, :HALF].reshape(PEERS * HALF, WIDE), inverse_ref[...])
     out_ref[:, :HALF, :] = solved.reshape(PEERS, HALF, WIDE)
     out_ref[:, HALF:, :] = near[:, HALF:]
@@ -328,7 +343,7 @@
     shape = (SIDE, WIDE)
     row, lane = lax.broadcasted_iota(jnp.int32, shape, 0), lax.broadcasted_iota(jnp.int32, shape, 1)
     down = jnp.sum(jnp.where(row == lane, scale, 0.0), axis=1, keepdims=True)
-    new_ref[...] = turned_ref[...] / down
+    new_ref[...] = turned_ref[...] * (1.0 / down)
 
 
 def struct(*shape):
@@ -384,22 +399,28 @@
     part_a = exchange(part_a, SLAB)
     answer_a, solved_a = call(solve_first, struct(*small), struct(HALF, WIDE))(part_a, meta, inverse_a)
     first = exchange(answer_a, SLAB)
-    square_a = exchange(call(share_gram, struct(PEERS, TILE, WIDE))(first), "rows")
-    part_b = pl.pallas_call(
+    first, square_a = lax.optimization_barrier((first, call(share_gram, struct(TILE, WIDE))(first)))
+    other_a = lax.ppermute(square_a, "rows", [(n, n ^ 1) for n in range(PEERS)])
+    part_b, turned = pl.pallas_call(
         contract,
-        in_specs=[apart, local],
-        out_specs=local,
-        out_shape=struct(*small),
+        in_specs=[apart, local, local],
+        out_specs=[local, local],
+        out_shape=(struct(*small), jax.ShapeDtypeStruct((WIDE, OWNERS * TILE), jnp.bfloat16)),
         scratch_shapes=[
             pltpu.VMEM((SLOTS, HALF, SIDE, WIDE), jnp.float32),
             pltpu.VMEM((SLOTS, SIDE, WIDE), jnp.float32),
             pltpu.SemaphoreType.DMA((SLOTS,)),
         ],
         compiler_params=LARGE,
-    )(folded, first)
-    part_b = exchange(call(insert, struct(*small))(part_b, square_a), SLAB)
-    near = exchange(call(sum_second, struct(PEERS, SIDE, WIDE))(part_b, meta, solved_a), "z")
-    inverse_b, scale_a = call(invert_second, struct(WIDE, WIDE), struct(1, WIDE))(part_b, third)
+    )(folded, first, meta)
+    part_b = exchange(call(insert, struct(*small))(part_b, square_a, other_a), SLAB)
+    near, square_a = call(sum_second, struct(PEERS, SIDE, WIDE), struct(HALF, WIDE))(part_b, turned, solved_a)
+    squares_a = [square_a] + [
+        lax.ppermute(square_a, "rows", [(n, (n + 2 * step) % PEERS) for n in range(PEERS)])
+        for step in range(1, TURNS)
+    ]
+    near = exchange(near, "z")
+    inverse_b, scale_a = call(invert_second, struct(WIDE, WIDE), struct(1, WIDE))(*squares_a, third)
     near, square_b = call(solve_second, struct(PEERS, SIDE, WIDE), struct(*small))(near, inverse_b, scale_a)
     parts = [near] + [
         lax.ppermute(near, "x", [(n, (n + step) % TURNS) for n in range(TURNS)]) for step in range(1, TURNS)

time: 144 us -> 141 us (0.979)
  starting transfers between devices: 35.3 us -> 33.8 us
    all_to_all x4 -> x3, starting transfers between devices: 33.2 us -> 24.8 us  [exchange(): return lax.all_to_all(x, axis, 0, 0, tiled=True)]
    ppermute x0 -> x4, starting transfers between devices: none -> 6.91 us  [the longest x1 4.76 us: shards(): other_a = lax.ppermute(square_a, 'rows', [(n, n ^ 1) for n in range(PEERS)])]
    all_to_all x4 -> x3, waiting for transfers between devices: 15.7 us -> 10.4 us  [exchange(): return lax.all_to_all(x, axis, 0, 0, tiled=True)]
    ppermute x0 -> x4, waiting for transfers between devices: none -> 3.8 us  [the longest x3 3.8 us: shards(): lax.ppermute(square_a, 'rows', [(n, (n + 2 * step) % PEERS) for n in rang...]
  transfers between devices with their start and end apart: 7 -> 10, of which waited for: 5 -> 6; matrix products, arithmetic and copies ran while one was open for 0% -> 0% of each run, Pallas kernels for 8% -> 9%
where the time goes in v5:
time: 141 us; the launch traced here: 140 us
  blocking collectives  62.2 us (44%)
  starting transfers between devices  33.8 us (24%)
  Pallas kernels  24.2 us (17%)
  waiting for transfers between devices  16.4 us (12%)
  between operations  1.42 us (1%)
    all_to_all x5, blocking collectives, exchange(): return lax.all_to_all(x, axis, 0, 0, tiled=True)  62.2 us
    all_to_all x3, starting transfers between devices, exchange(): return lax.all_to_all(x, axis, 0, 0, tiled=True)  24.8 us
    all_to_all x3, waiting for transfers between devices, exchange(): return lax.all_to_all(x, axis, 0, 0, tiled=True)  10.4 us
    pallas_call x1, Pallas kernels, shards(): pl.pallas_call(fold, in_specs=[scalars, apart, local, local], out_specs=[...  7.29 us
    pallas_call x1, Pallas kernels, shards(): call(invert_second, struct(WIDE, WIDE), struct(1, WIDE))(*squares_a, third)  5.68 us
    ppermute x1, starting transfers between devices, shards(): other_a = lax.ppermute(square_a, 'rows', [(n, n ^ 1) for n in range(PEERS)])  4.76 us
    ppermute x3, waiting for transfers between devices, shards(): lax.ppermute(square_a, 'rows', [(n, (n + 2 * step) % PEERS) for n in rang...  3.8 us
    pallas_call x1, Pallas kernels, shards(): pl.pallas_call(contract, in_specs=[apart, local, local], out_specs=[local...  3.09 us
  transfers between devices with their start and end apart: 10, of which 6 were waited for; matrix products, arithmetic and copies ran while one was open for 0% of the time, Pallas kernels for 9%

profile of v5, /device:TPU:1, one launch (start us, length us, event | category | flops | bytes accessed | tf_op | source)
XLA Modules:
  0.0 139.9 jit_solution(11303184302451676833)
XLA Ops:
  1.3 0.9 fusion.given_ref
  2.2 0.9 shard_map.76
  3.1 11.9 %all-to-all-start = ((f32[32,8,128]{2,1,0:T(8,128)}), f32[32,8,128]{2,1,0:T(8,128)S(1)}, u32[]{:S(2)}, u32[]{:S(2)}) async-start(f32[32,8,128]{2,1,0:T(8,128)} %get-tuple-element.25), calls=%async_computation | async-start | bytes 262144 | tf_op jit(solution)/shard_map/all_to_all | solution.py:354
  15.0 0.0 copy-start
  15.0 1.0 copy-done
  16.0 1.3 shard_map.77
  17.3 6.8 %all-to-all-done.first_ref.meta_ref = f32[32,8,128]{2,1,0:T(8,128)S(1)} async-done(((f32[32,8,128]{2,1,0:T(8,128)}), f32[32,8,128]{2,1,0:T(8,128)S(1)}, u32[]{:S(2)}, u32[]{:S(2)}) %all-to-all-start) | async-done | bytes 131104 | tf_op jit(solution)/shard_map/all_to_all | solution.py:354
  24.1 11.9 %all_to_all.40.held_ref = f32[8,40,128]{2,1,0:T(8,128)S(1)} all-to-all(f32[8,40,128]{2,1,0:T(8,128)S(1)} %shard_map.78), channel_id=1, replica_groups=mesh['x'=4,'z'=8,'rows'=8] {'rows'}, dimensions={0} | all-to-all | bytes 327680 | tf_op jit(solution)/shard_map/all_to_all | solution.py:354
  36.1 0.3 shard_map.79
  36.3 12.5 %all_to_all.41.third_ref = f32[32,8,128]{2,1,0:T(8,128)S(1)} all-to-all(f32[32,8,128]{2,1,0:T(8,128)S(1)} %shard_map.79), channel_id=1, replica_groups=mesh['x'=4,'z'=8,'rows'=8] {'x','z'}, dimensions={0} | all-to-all | bytes 262144 | tf_op jit(solution)/shard_map/all_to_all | solution.py:354
  48.8 7.3 %shard_map.80 = (f32[6,32,64,128]{3,2,1,0:T(8,128)}, f32[32,8,128]{2,1,0:T(8,128)S(1)}, f32[128,128]{1,0:T(8,128)S(1)}) custom-call(s32[8,64]{1,0:T(8,128)S(1)} %get-tuple-element.24.place_ref, f32[6,64,4096]{2,1,0:T(8,128)} %blocks_ref.1, f32[32,8,128]{2,1,0:T(8,128)S(1)} %all_to_all.41.third_ref, f32[32,32,128]{2,1,0:T(8,128)S(1)} %get-tuple-element.27.pairs_ref), custom_call_target="tpu_custom_call" | custom-call | tf_op jit(solution)/shard_map/pallas_call | solution.py:385
  56.1 12.7 %all_to_all.42.part_ref = f32[32,8,128]{2,1,0:T(8,128)S(1)} all-to-all(f32[32,8,128]{2,1,0:T(8,128)S(1)} %get-tuple-element.29), channel_id=1, replica_groups=mesh['x'=4,'z'=8,'rows'=8] {'x','z'}, dimensions={0} | all-to-all | bytes 262144 | tf_op jit(solution)/shard_map/all_to_all | solution.py:354
  68.8 0.9 shard_map.81
  69.7 12.6 %all_to_all.43.first_ref = f32[32,8,128]{2,1,0:T(8,128)S(1)} all-to-all(f32[32,8,128]{2,1,0:T(8,128)S(1)} %get-tuple-element.31), channel_id=1, replica_groups=mesh['x'=4,'z'=8,'rows'=8] {'x','z'}, dimensions={0} | all-to-all | bytes 262144 | tf_op jit(solution)/shard_map/all_to_all | solution.py:354
  82.4 4.8 %collective-permute-start = (f32[8,128]{1,0:T(8,128)S(1)}, f32[8,128]{1,0:T(8,128)S(1)}, u32[]{:S(2)}, u32[]{:S(2)}) collective-permute-start(f32[8,128]{1,0:T(8,128)S(1)} %shard_map.82.square_ref), channel_id=1, source_target_pairs={{0,1},{1,0},{2,3},{3,2},{4,5},{5,4},{6,7},{7,6},{8,9},{9,8},{10,11... | collective-permute-start | bytes 12296 | tf_op jit(solution)/shard_map/ppermute | solution.py:403
  87.1 3.1 %shard_map.83 = (f32[32,8,128]{2,1,0:T(8,128)S(1)}, bf16[128,256]{1,0:T(8,128)(2,1)S(1)}) custom-call(f32[6,32,64,128]{3,2,1,0:T(8,128)} %get-tuple-element.28.folded_ref, f32[32,8,128]{2,1,0:T(8,128)S(1)} %all_to_all.43.first_ref, f32[32,8,128]{2,1,0:T(8,128)S(1)} %all-to-all-done.first_ref.meta_ref), custom_call_target="tpu_custom_call" | custom-call | tf_op jit(solution)/shard_map/pallas_call | solution.py:404
  90.2 0.0 collective-permute-done.other_ref
  90.3 12.4 %all_to_all.44.part_ref = f32[32,8,128]{2,1,0:T(8,128)S(1)} all-to-all(f32[32,8,128]{2,1,0:T(8,128)S(1)} %shard_map.84), channel_id=1, replica_groups=mesh['x'=4,'z'=8,'rows'=8] {'x','z'}, dimensions={0} | all-to-all | bytes 262144 | tf_op jit(solution)/shard_map/all_to_all | solution.py:354
  102.7 0.9 shard_map.85
  103.5 3.4 %all-to-all-start.6 = ((f32[8,64,128]{2,1,0:T(8,128)}), f32[8,64,128]{2,1,0:T(8,128)S(1)}, u32[]{:S(2)}, u32[]{:S(2)}) async-start(f32[8,64,128]{2,1,0:T(8,128)} %get-tuple-element.37), calls=%async_computation.6 | async-start | bytes 524288 | tf_op jit(solution)/shard_map/all_to_all | solution.py:354
  107.0 1.0 collective-permute-start.3
  107.9 1.2 collective-permute-start.2
  109.1 0.0 collective-permute-start.1
  109.1 0.5 collective-permute-done.3.three_ref
  109.6 2.4 %collective-permute-done.2.two_ref = f32[32,128]{1,0:T(8,128)S(1)} collective-permute-done((f32[32,128]{1,0:T(8,128)S(1)}, f32[32,128]{1,0:T(8,128)S(1)}, u32[]{:S(2)}, u32[]{:S(2)}) %collective-permute-start.2) | collective-permute-done | bytes 16416 | tf_op jit(solution)/shard_map/ppermute | solution.py:419
  112.0 0.9 collective-permute-done.1.one_ref
  112.9 5.7 %shard_map.86 = (f32[128,128]{1,0:T(8,128)S(1)}, f32[1,128]{1,0:T(1,128)S(1)}) custom-call(f32[32,128]{1,0:T(8,128)S(1)} %get-tuple-element.38.own_ref, f32[32,128]{1,0:T(8,128)S(1)} %collective-permute-done.1.one_ref, f32[32,128]{1,0:T(8,128)S(1)} %collective-permute-done.2.two_ref, f32[32,128]{1,0:T(8,128)S(1)} %collective-permute-done.3.three_ref, ...), custom_call_target="tpu_custom_call" | custom-call | tf_op jit(solution)/shard_map/pallas_call | solution.py:423
  118.6 0.0 all-to-all-done.6.near_ref
  118.6 0.9 shard_map.87
  119.6 0.9 collective-permute-start.6
  120.4 1.2 collective-permute-start.5
  121.7 0.0 collective-permute-start.4
  121.7 9.5 %all-to-all-start.7 = ((f32[32,8,128]{2,1,0:T(8,128)}), f32[32,8,128]{2,1,0:T(8,128)S(1)}, u32[]{:S(2)}, u32[]{:S(2)}) async-start(f32[32,8,128]{2,1,0:T(8,128)} %get-tuple-element.42), calls=%async_computation.7 | async-start | bytes 262144 | tf_op jit(solution)/shard_map/all_to_all | solution.py:354
  131.2 0.0 collective-permute-done.6.refs_3_
  131.2 0.0 collective-permute-done.5.refs_2_
  131.2 2.2 %collective-permute-done.4.refs_1_ = f32[8,64,128]{2,1,0:T(8,128)S(1)} collective-permute-done((f32[8,64,128]{2,1,0:T(8,128)S(1)}, f32[8,64,128]{2,1,0:T(8,128)S(1)}, u32[]{:S(2)}, u32[]{:S(2)}) %collective-permute-start.4) | collective-permute-done | bytes 262176 | tf_op jit(solution)/shard_map/ppermute | solution.py:426
  133.5 0.6 shard_map.89.turned_ref
  134.0 1.4 shard_map.88
  135.4 3.6 %all-to-all-done.7.square_ref = f32[32,8,128]{2,1,0:T(8,128)S(1)} async-done(((f32[32,8,128]{2,1,0:T(8,128)}), f32[32,8,128]{2,1,0:T(8,128)S(1)}, u32[]{:S(2)}, u32[]{:S(2)}) %all-to-all-start.7) | async-done | bytes 131104 | tf_op jit(solution)/shard_map/all_to_all | solution.py:354
  138.9 1.0 shard_map.90
  (4 shorter events, 0.1 us)
Async XLA Ops:
  3.1 21.0 %all-to-all-start = ((f32[32,8,128]{2,1,0:T(8,128)}), f32[32,8,128]{2,1,0:T(8,128)S(1)}, u32[]{:S(2)}, u32[]{:S(2)}) async-start(f32[32,8,128]{2,1,0:T(8,128)} %get-tuple-element.25), calls=%async_computation | async-start | bytes 262144 | tf_op jit(solution)/shard_map/all_to_all | solution.py:354
  15.0 1.0 copy-start
  82.4 7.9 %collective-permute-start = (f32[8,128]{1,0:T(8,128)S(1)}, f32[8,128]{1,0:T(8,128)S(1)}, u32[]{:S(2)}, u32[]{:S(2)}) collective-permute-start(f32[8,128]{1,0:T(8,128)S(1)} %shard_map.82.square_ref), channel_id=1, source_target_pairs={{0,1},{1,0},{2,3},{3,2},{4,5},{5,4},{6,7},{7,6},{8,9},{9,8},{10,11... | collective-permute-start | bytes 12296 | tf_op jit(solution)/shard_map/ppermute | solution.py:403
  103.5 15.1 %all-to-all-start.6 = ((f32[8,64,128]{2,1,0:T(8,128)}), f32[8,64,128]{2,1,0:T(8,128)S(1)}, u32[]{:S(2)}, u32[]{:S(2)}) async-start(f32[8,64,128]{2,1,0:T(8,128)} %get-tuple-element.37), calls=%async_computation.6 | async-start | bytes 524288 | tf_op jit(solution)/shard_map/all_to_all | solution.py:354
  107.0 2.7 %collective-permute-start.3 = (f32[32,128]{1,0:T(8,128)S(1)}, f32[32,128]{1,0:T(8,128)S(1)}, u32[]{:S(2)}, u32[]{:S(2)}) collective-permute-start(f32[32,128]{1,0:T(8,128)S(1)} %get-tuple-element.38.own_ref), channel_id=1, source_target_pairs={{0,6},{1,7},{2,0},{3,1},{4,2},{5,3},{6,4},{7,5},{8,14},{9,15},{10,... | collective-permute-start | bytes 49160 | tf_op jit(solution)/shard_map/ppermute | solution.py:419
  107.9 4.1 %collective-permute-start.2 = (f32[32,128]{1,0:T(8,128)S(1)}, f32[32,128]{1,0:T(8,128)S(1)}, u32[]{:S(2)}, u32[]{:S(2)}) collective-permute-start(f32[32,128]{1,0:T(8,128)S(1)} %get-tuple-element.38.own_ref), channel_id=1, source_target_pairs={{0,4},{1,5},{2,6},{3,7},{4,0},{5,1},{6,2},{7,3},{8,12},{9,13},{10,... | collective-permute-start | bytes 49160 | tf_op jit(solution)/shard_map/ppermute | solution.py:419
  109.1 3.8 %collective-permute-start.1 = (f32[32,128]{1,0:T(8,128)S(1)}, f32[32,128]{1,0:T(8,128)S(1)}, u32[]{:S(2)}, u32[]{:S(2)}) collective-permute-start(f32[32,128]{1,0:T(8,128)S(1)} %get-tuple-element.38.own_ref), channel_id=1, source_target_pairs={{0,2},{1,3},{2,4},{3,5},{4,6},{5,7},{6,0},{7,1},{8,10},{9,11},{10,... | collective-permute-start | bytes 49160 | tf_op jit(solution)/shard_map/ppermute | solution.py:419
  119.6 11.7 %collective-permute-start.6 = (f32[8,64,128]{2,1,0:T(8,128)S(1)}, f32[8,64,128]{2,1,0:T(8,128)S(1)}, u32[]{:S(2)}, u32[]{:S(2)}) collective-permute-start(f32[8,64,128]{2,1,0:T(8,128)S(1)} %get-tuple-element.41.refs_0_), channel_id=1, source_target_pairs={{0,192},{64,0},{128,64},{192,128},{1,193},{65,1},{129,65},{193,129... | collective-permute-start | bytes 786440 | tf_op jit(solution)/shard_map/ppermute | solution.py:426
  120.4 10.8 %collective-permute-start.5 = (f32[8,64,128]{2,1,0:T(8,128)S(1)}, f32[8,64,128]{2,1,0:T(8,128)S(1)}, u32[]{:S(2)}, u32[]{:S(2)}) collective-permute-start(f32[8,64,128]{2,1,0:T(8,128)S(1)} %get-tuple-element.41.refs_0_), channel_id=1, source_target_pairs={{0,128},{64,192},{128,0},{192,64},{1,129},{65,193},{129,1},{193,65... | collective-permute-start | bytes 786440 | tf_op jit(solution)/shard_map/ppermute | solution.py:426
  121.7 11.8 %collective-permute-start.4 = (f32[8,64,128]{2,1,0:T(8,128)S(1)}, f32[8,64,128]{2,1,0:T(8,128)S(1)}, u32[]{:S(2)}, u32[]{:S(2)}) collective-permute-start(f32[8,64,128]{2,1,0:T(8,128)S(1)} %get-tuple-element.41.refs_0_), channel_id=1, source_target_pairs={{0,64},{64,128},{128,192},{192,0},{1,65},{65,129},{129,193},{193,1... | collective-permute-start | bytes 786440 | tf_op jit(solution)/shard_map/ppermute | solution.py:426
  121.7 17.3 %all-to-all-start.7 = ((f32[32,8,128]{2,1,0:T(8,128)}), f32[32,8,128]{2,1,0:T(8,128)S(1)}, u32[]{:S(2)}, u32[]{:S(2)}) async-start(f32[32,8,128]{2,1,0:T(8,128)} %get-tuple-element.42), calls=%async_computation.7 | async-start | bytes 262144 | tf_op jit(solution)/shard_map/all_to_all | solution.py:354

commit v6 on v5

--- a/solution.py
+++ b/solution.py
@@ -10,8 +10,8 @@
 HALF = 32
 WIDE = 128
 STEP = 8
-BEFORE = 10
-AFTER = 8
+BEFORE = 14
+AFTER = 12
 TILE = 8
 SLOTS = 6
 LEAD = 2
@@ -59,6 +59,10 @@
     return fold_halves(jnp.where(low(total.shape), total, swap(total)))
 
 
+def spot(work, row, lane):
+    return jnp.broadcast_to(work[row : row + 1, lane : lane + 1], (TILE, WIDE))
+
+
 def begin_inverse(gram):
     row = lax.broadcasted_iota(jnp.int32, gram.shape, 0)
     lane = lax.broadcasted_iota(jnp.int32, gram.shape, 1)
@@ -74,6 +78,18 @@
     return work
 
 
+def eliminate_all(work):
+    row = lax.broadcasted_iota(jnp.int32, work.shape, 0)
+    ratio = 1.0 / spot(work, 0, 0)
+    for k in range(SIDE):
+        line = jnp.broadcast_to(work[k : k + 1, :], (TILE, WIDE)) * ratio
+        if k + 1 < SIDE:
+            ratio = 1.0 / (spot(work, k + 1, k + 1) - spot(work, k + 1, k) * (spot(work, k, k + 1) * ratio))
+        line = jnp.broadcast_to(line[None], (TILE, TILE, WIDE)).reshape(work.shape)
+        work = jnp.where(row == k, line, work - work[:, k : k + 1] * line)
+    return work
+
+
 def end_inverse(work):
     zero = jnp.zeros_like(work)
     mask = low(work.shape)
@@ -81,7 +97,7 @@
 
 
 def inverse(gram):
-    return end_inverse(eliminate(begin_inverse(gram), 0, SIDE))
+    return end_inverse(eliminate_all(begin_inverse(gram)))
 
 
 def held(shape):

time: 141 us -> 140 us (level)
  transfers between devices with their start and end apart: 10 -> 10, of which waited for: 6 -> 6; matrix products, arithmetic and copies ran while one was open for 0% -> 0% of each run, Pallas kernels for 9% -> 8%
where the time goes in v6:
time: 140 us; the launch traced here: 139 us
  blocking collectives  62.2 us (44%)
  starting transfers between devices  33.8 us (24%)
  Pallas kernels  23.1 us (16%)
  waiting for transfers between devices  16.4 us (12%)
  between operations  1.42 us (1%)
    all_to_all x5, blocking collectives, exchange(): return lax.all_to_all(x, axis, 0, 0, tiled=True)  62.2 us
    all_to_all x3, starting transfers between devices, exchange(): return lax.all_to_all(x, axis, 0, 0, tiled=True)  24.8 us
    all_to_all x3, waiting for transfers between devices, exchange(): return lax.all_to_all(x, axis, 0, 0, tiled=True)  10.4 us
    pallas_call x1, Pallas kernels, shards(): pl.pallas_call(fold, in_specs=[scalars, apart, local, local], out_specs=[...  7.03 us
    pallas_call x1, Pallas kernels, shards(): call(invert_second, struct(WIDE, WIDE), struct(1, WIDE))(*squares_a, third)  4.89 us
    ppermute x1, starting transfers between devices, shards(): other_a = lax.ppermute(square_a, 'rows', [(n, n ^ 1) for n in range(PEERS)])  4.76 us
    ppermute x3, waiting for transfers between devices, shards(): lax.ppermute(square_a, 'rows', [(n, (n + 2 * step) % PEERS) for n in rang...  3.8 us
    pallas_call x1, Pallas kernels, shards(): pl.pallas_call(contract, in_specs=[apart, local, local], out_specs=[local...  3.09 us
  transfers between devices with their start and end apart: 10, of which 6 were waited for; matrix products, arithmetic and copies ran while one was open for 0% of the time, Pallas kernels for 8%

profile of v6, /device:TPU:1, one launch (start us, length us, event | category | flops | bytes accessed | tf_op | source)
XLA Modules:
  0.0 138.9 jit_solution(16976262934799634197)
XLA Ops:
  1.3 0.9 fusion.given_ref
  2.2 0.9 shard_map.76
  3.1 11.9 %all-to-all-start = ((f32[32,8,128]{2,1,0:T(8,128)}), f32[32,8,128]{2,1,0:T(8,128)S(1)}, u32[]{:S(2)}, u32[]{:S(2)}) async-start(f32[32,8,128]{2,1,0:T(8,128)} %get-tuple-element.25), calls=%async_computation | async-start | bytes 262144 | tf_op jit(solution)/shard_map/all_to_all | solution.py:370
  15.0 0.0 copy-start
  15.0 1.0 copy-done
  16.0 1.3 shard_map.77
  17.3 6.8 %all-to-all-done.first_ref.meta_ref = f32[32,8,128]{2,1,0:T(8,128)S(1)} async-done(((f32[32,8,128]{2,1,0:T(8,128)}), f32[32,8,128]{2,1,0:T(8,128)S(1)}, u32[]{:S(2)}, u32[]{:S(2)}) %all-to-all-start) | async-done | bytes 131104 | tf_op jit(solution)/shard_map/all_to_all | solution.py:370
  24.1 11.9 %all_to_all.40.held_ref = f32[8,40,128]{2,1,0:T(8,128)S(1)} all-to-all(f32[8,40,128]{2,1,0:T(8,128)S(1)} %shard_map.78), channel_id=1, replica_groups=mesh['x'=4,'z'=8,'rows'=8] {'rows'}, dimensions={0} | all-to-all | bytes 327680 | tf_op jit(solution)/shard_map/all_to_all | solution.py:370
  36.1 0.3 shard_map.79
  36.3 12.5 %all_to_all.41.third_ref = f32[32,8,128]{2,1,0:T(8,128)S(1)} all-to-all(f32[32,8,128]{2,1,0:T(8,128)S(1)} %shard_map.79), channel_id=1, replica_groups=mesh['x'=4,'z'=8,'rows'=8] {'x','z'}, dimensions={0} | all-to-all | bytes 262144 | tf_op jit(solution)/shard_map/all_to_all | solution.py:370
  48.8 7.0 %shard_map.80 = (f32[6,32,64,128]{3,2,1,0:T(8,128)}, f32[32,8,128]{2,1,0:T(8,128)S(1)}, f32[128,128]{1,0:T(8,128)S(1)}) custom-call(s32[8,64]{1,0:T(8,128)S(1)} %get-tuple-element.24.place_ref, f32[6,64,4096]{2,1,0:T(8,128)} %blocks_ref.1, f32[32,8,128]{2,1,0:T(8,128)S(1)} %all_to_all.41.third_ref, f32[32,32,128]{2,1,0:T(8,128)S(1)} %get-tuple-element.27.pairs_ref), custom_call_target="tpu_custom_call" | custom-call | tf_op jit(solution)/shard_map/pallas_call | solution.py:401
  55.8 12.7 %all_to_all.42.part_ref = f32[32,8,128]{2,1,0:T(8,128)S(1)} all-to-all(f32[32,8,128]{2,1,0:T(8,128)S(1)} %get-tuple-element.29), channel_id=1, replica_groups=mesh['x'=4,'z'=8,'rows'=8] {'x','z'}, dimensions={0} | all-to-all | bytes 262144 | tf_op jit(solution)/shard_map/all_to_all | solution.py:370
  68.6 0.9 shard_map.81
  69.5 12.6 %all_to_all.43.first_ref = f32[32,8,128]{2,1,0:T(8,128)S(1)} all-to-all(f32[32,8,128]{2,1,0:T(8,128)S(1)} %get-tuple-element.31), channel_id=1, replica_groups=mesh['x'=4,'z'=8,'rows'=8] {'x','z'}, dimensions={0} | all-to-all | bytes 262144 | tf_op jit(solution)/shard_map/all_to_all | solution.py:370
  82.1 4.8 %collective-permute-start = (f32[8,128]{1,0:T(8,128)S(1)}, f32[8,128]{1,0:T(8,128)S(1)}, u32[]{:S(2)}, u32[]{:S(2)}) collective-permute-start(f32[8,128]{1,0:T(8,128)S(1)} %shard_map.82.square_ref), channel_id=1, source_target_pairs={{0,1},{1,0},{2,3},{3,2},{4,5},{5,4},{6,7},{7,6},{8,9},{9,8},{10,11... | collective-permute-start | bytes 12296 | tf_op jit(solution)/shard_map/ppermute | solution.py:419
  86.9 3.1 %shard_map.83 = (f32[32,8,128]{2,1,0:T(8,128)S(1)}, bf16[128,256]{1,0:T(8,128)(2,1)S(1)}) custom-call(f32[6,32,64,128]{3,2,1,0:T(8,128)} %get-tuple-element.28.folded_ref, f32[32,8,128]{2,1,0:T(8,128)S(1)} %all_to_all.43.first_ref, f32[32,8,128]{2,1,0:T(8,128)S(1)} %all-to-all-done.first_ref.meta_ref), custom_call_target="tpu_custom_call" | custom-call | tf_op jit(solution)/shard_map/pallas_call | solution.py:420
  90.0 0.0 collective-permute-done.other_ref
  90.0 12.4 %all_to_all.44.part_ref = f32[32,8,128]{2,1,0:T(8,128)S(1)} all-to-all(f32[32,8,128]{2,1,0:T(8,128)S(1)} %shard_map.84), channel_id=1, replica_groups=mesh['x'=4,'z'=8,'rows'=8] {'x','z'}, dimensions={0} | all-to-all | bytes 262144 | tf_op jit(solution)/shard_map/all_to_all | solution.py:370
  102.4 0.9 shard_map.85
  103.3 3.4 %all-to-all-start.6 = ((f32[8,64,128]{2,1,0:T(8,128)}), f32[8,64,128]{2,1,0:T(8,128)S(1)}, u32[]{:S(2)}, u32[]{:S(2)}) async-start(f32[8,64,128]{2,1,0:T(8,128)} %get-tuple-element.37), calls=%async_computation.6 | async-start | bytes 524288 | tf_op jit(solution)/shard_map/all_to_all | solution.py:370
  106.7 1.0 collective-permute-start.3
  107.7 1.2 collective-permute-start.2
  108.9 0.0 collective-permute-start.1
  108.9 0.5 collective-permute-done.3.three_ref
  109.4 2.4 %collective-permute-done.2.two_ref = f32[32,128]{1,0:T(8,128)S(1)} collective-permute-done((f32[32,128]{1,0:T(8,128)S(1)}, f32[32,128]{1,0:T(8,128)S(1)}, u32[]{:S(2)}, u32[]{:S(2)}) %collective-permute-start.2) | collective-permute-done | bytes 16416 | tf_op jit(solution)/shard_map/ppermute | solution.py:435
  111.8 0.9 collective-permute-done.1.one_ref
  112.7 4.9 %shard_map.86 = (f32[128,128]{1,0:T(8,128)S(1)}, f32[1,128]{1,0:T(1,128)S(1)}) custom-call(f32[32,128]{1,0:T(8,128)S(1)} %get-tuple-element.38.own_ref, f32[32,128]{1,0:T(8,128)S(1)} %collective-permute-done.1.one_ref, f32[32,128]{1,0:T(8,128)S(1)} %collective-permute-done.2.two_ref, f32[32,128]{1,0:T(8,128)S(1)} %collective-permute-done.3.three_ref, ...), custom_call_target="tpu_custom_call" | custom-call | tf_op jit(solution)/shard_map/pallas_call | solution.py:439
  117.6 0.0 all-to-all-done.6.near_ref
  117.6 0.9 shard_map.87
  118.5 0.9 collective-permute-start.6
  119.4 1.2 collective-permute-start.5
  120.6 0.0 collective-permute-start.4
  120.6 9.5 %all-to-all-start.7 = ((f32[32,8,128]{2,1,0:T(8,128)}), f32[32,8,128]{2,1,0:T(8,128)S(1)}, u32[]{:S(2)}, u32[]{:S(2)}) async-start(f32[32,8,128]{2,1,0:T(8,128)} %get-tuple-element.42), calls=%async_computation.7 | async-start | bytes 262144 | tf_op jit(solution)/shard_map/all_to_all | solution.py:370
  130.2 0.0 collective-permute-done.6.refs_3_
  130.2 0.0 collective-permute-done.5.refs_2_
  130.2 2.2 %collective-permute-done.4.refs_1_ = f32[8,64,128]{2,1,0:T(8,128)S(1)} collective-permute-done((f32[8,64,128]{2,1,0:T(8,128)S(1)}, f32[8,64,128]{2,1,0:T(8,128)S(1)}, u32[]{:S(2)}, u32[]{:S(2)}) %collective-permute-start.4) | collective-permute-done | bytes 262176 | tf_op jit(solution)/shard_map/ppermute | solution.py:442
  132.4 0.6 shard_map.89.turned_ref
  133.0 1.4 shard_map.88
  134.3 3.6 %all-to-all-done.7.square_ref = f32[32,8,128]{2,1,0:T(8,128)S(1)} async-done(((f32[32,8,128]{2,1,0:T(8,128)}), f32[32,8,128]{2,1,0:T(8,128)S(1)}, u32[]{:S(2)}, u32[]{:S(2)}) %all-to-all-start.7) | async-done | bytes 131104 | tf_op jit(solution)/shard_map/all_to_all | solution.py:370
  137.9 1.0 shard_map.90
  (4 shorter events, 0.1 us)
Async XLA Ops:
  3.1 21.0 %all-to-all-start = ((f32[32,8,128]{2,1,0:T(8,128)}), f32[32,8,128]{2,1,0:T(8,128)S(1)}, u32[]{:S(2)}, u32[]{:S(2)}) async-start(f32[32,8,128]{2,1,0:T(8,128)} %get-tuple-element.25), calls=%async_computation | async-start | bytes 262144 | tf_op jit(solution)/shard_map/all_to_all | solution.py:370
  15.0 1.0 copy-start
  82.1 7.9 %collective-permute-start = (f32[8,128]{1,0:T(8,128)S(1)}, f32[8,128]{1,0:T(8,128)S(1)}, u32[]{:S(2)}, u32[]{:S(2)}) collective-permute-start(f32[8,128]{1,0:T(8,128)S(1)} %shard_map.82.square_ref), channel_id=1, source_target_pairs={{0,1},{1,0},{2,3},{3,2},{4,5},{5,4},{6,7},{7,6},{8,9},{9,8},{10,11... | collective-permute-start | bytes 12296 | tf_op jit(solution)/shard_map/ppermute | solution.py:419
  103.3 14.3 %all-to-all-start.6 = ((f32[8,64,128]{2,1,0:T(8,128)}), f32[8,64,128]{2,1,0:T(8,128)S(1)}, u32[]{:S(2)}, u32[]{:S(2)}) async-start(f32[8,64,128]{2,1,0:T(8,128)} %get-tuple-element.37), calls=%async_computation.6 | async-start | bytes 524288 | tf_op jit(solution)/shard_map/all_to_all | solution.py:370
  106.7 2.7 %collective-permute-start.3 = (f32[32,128]{1,0:T(8,128)S(1)}, f32[32,128]{1,0:T(8,128)S(1)}, u32[]{:S(2)}, u32[]{:S(2)}) collective-permute-start(f32[32,128]{1,0:T(8,128)S(1)} %get-tuple-element.38.own_ref), channel_id=1, source_target_pairs={{0,6},{1,7},{2,0},{3,1},{4,2},{5,3},{6,4},{7,5},{8,14},{9,15},{10,... | collective-permute-start | bytes 49160 | tf_op jit(solution)/shard_map/ppermute | solution.py:435
  107.7 4.1 %collective-permute-start.2 = (f32[32,128]{1,0:T(8,128)S(1)}, f32[32,128]{1,0:T(8,128)S(1)}, u32[]{:S(2)}, u32[]{:S(2)}) collective-permute-start(f32[32,128]{1,0:T(8,128)S(1)} %get-tuple-element.38.own_ref), channel_id=1, source_target_pairs={{0,4},{1,5},{2,6},{3,7},{4,0},{5,1},{6,2},{7,3},{8,12},{9,13},{10,... | collective-permute-start | bytes 49160 | tf_op jit(solution)/shard_map/ppermute | solution.py:435
  108.9 3.8 %collective-permute-start.1 = (f32[32,128]{1,0:T(8,128)S(1)}, f32[32,128]{1,0:T(8,128)S(1)}, u32[]{:S(2)}, u32[]{:S(2)}) collective-permute-start(f32[32,128]{1,0:T(8,128)S(1)} %get-tuple-element.38.own_ref), channel_id=1, source_target_pairs={{0,2},{1,3},{2,4},{3,5},{4,6},{5,7},{6,0},{7,1},{8,10},{9,11},{10,... | collective-permute-start | bytes 49160 | tf_op jit(solution)/shard_map/ppermute | solution.py:435
  118.5 11.7 %collective-permute-start.6 = (f32[8,64,128]{2,1,0:T(8,128)S(1)}, f32[8,64,128]{2,1,0:T(8,128)S(1)}, u32[]{:S(2)}, u32[]{:S(2)}) collective-permute-start(f32[8,64,128]{2,1,0:T(8,128)S(1)} %get-tuple-element.41.refs_0_), channel_id=1, source_target_pairs={{0,192},{64,0},{128,64},{192,128},{1,193},{65,1},{129,65},{193,129... | collective-permute-start | bytes 786440 | tf_op jit(solution)/shard_map/ppermute | solution.py:442
  119.4 10.8 %collective-permute-start.5 = (f32[8,64,128]{2,1,0:T(8,128)S(1)}, f32[8,64,128]{2,1,0:T(8,128)S(1)}, u32[]{:S(2)}, u32[]{:S(2)}) collective-permute-start(f32[8,64,128]{2,1,0:T(8,128)S(1)} %get-tuple-element.41.refs_0_), channel_id=1, source_target_pairs={{0,128},{64,192},{128,0},{192,64},{1,129},{65,193},{129,1},{193,65... | collective-permute-start | bytes 786440 | tf_op jit(solution)/shard_map/ppermute | solution.py:442
  120.6 11.8 %collective-permute-start.4 = (f32[8,64,128]{2,1,0:T(8,128)S(1)}, f32[8,64,128]{2,1,0:T(8,128)S(1)}, u32[]{:S(2)}, u32[]{:S(2)}) collective-permute-start(f32[8,64,128]{2,1,0:T(8,128)S(1)} %get-tuple-element.41.refs_0_), channel_id=1, source_target_pairs={{0,64},{64,128},{128,192},{192,0},{1,65},{65,129},{129,193},{193,1... | collective-permute-start | bytes 786440 | tf_op jit(solution)/shard_map/ppermute | solution.py:442
  120.6 17.3 %all-to-all-start.7 = ((f32[32,8,128]{2,1,0:T(8,128)}), f32[32,8,128]{2,1,0:T(8,128)S(1)}, u32[]{:S(2)}, u32[]{:S(2)}) async-start(f32[32,8,128]{2,1,0:T(8,128)} %get-tuple-element.42), calls=%async_computation.7 | async-start | bytes 262144 | tf_op jit(solution)/shard_map/all_to_all | solution.py:370

commit v7 on v6

--- a/solution.py
+++ b/solution.py
@@ -437,7 +437,7 @@
     ]
     near = exchange(near, "z")
     inverse_b, scale_a = call(invert_second, struct(WIDE, WIDE), struct(1, WIDE))(*squares_a, third)
-    near, square_b = call(solve_second, struct(PEERS, SIDE, WIDE), struct(*small))(near, inverse_b, scale_a)
+    near, square_b = call(solve_second, struct(PEERS, SIDE, WIDE), struct(OWNERS, 1, WIDE))(near, inverse_b, scale_a)
     parts = [near] + [
         lax.ppermute(near, "x", [(n, (n + step) % TURNS) for n in range(TURNS)]) for step in range(1, TURNS)
     ]

time: 140 us -> 139 us (level)
  no operation moved by 1% of the time
where the time goes in v7:
time: 139 us; the launch traced here: 138 us
  blocking collectives  62.2 us (45%)
  starting transfers between devices  33.8 us (24%)
  Pallas kernels  23.1 us (17%)
  waiting for transfers between devices  15.6 us (11%)
  between operations  1.42 us (1%)
    all_to_all x5, blocking collectives, exchange(): return lax.all_to_all(x, axis, 0, 0, tiled=True)  62.2 us
    all_to_all x3, starting transfers between devices, exchange(): return lax.all_to_all(x, axis, 0, 0, tiled=True)  24.8 us
    all_to_all x3, waiting for transfers between devices, exchange(): return lax.all_to_all(x, axis, 0, 0, tiled=True)  9.56 us
    pallas_call x1, Pallas kernels, shards(): pl.pallas_call(fold, in_specs=[scalars, apart, local, local], out_specs=[...  7.03 us
    pallas_call x1, Pallas kernels, shards(): call(invert_second, struct(WIDE, WIDE), struct(1, WIDE))(*squares_a, third)  4.89 us
    ppermute x1, starting transfers between devices, shards(): other_a = lax.ppermute(square_a, 'rows', [(n, n ^ 1) for n in range(PEERS)])  4.76 us
    ppermute x3, waiting for transfers between devices, shards(): lax.ppermute(square_a, 'rows', [(n, (n + 2 * step) % PEERS) for n in rang...  3.8 us
    pallas_call x1, Pallas kernels, shards(): pl.pallas_call(contract, in_specs=[apart, local, local], out_specs=[local...  3.09 us
  transfers between devices with their start and end apart: 10, of which 6 were waited for; matrix products, arithmetic and copies ran while one was open for 0% of the time, Pallas kernels for 8%

profile of v7, /device:TPU:1, one launch (start us, length us, event | category | flops | bytes accessed | tf_op | source)
XLA Modules:
  0.0 138.0 jit_solution(15792883683614376924)
XLA Ops:
  1.3 0.9 fusion.given_ref
  2.2 0.9 shard_map.76
  3.1 11.9 %all-to-all-start = ((f32[32,8,128]{2,1,0:T(8,128)}), f32[32,8,128]{2,1,0:T(8,128)S(1)}, u32[]{:S(2)}, u32[]{:S(2)}) async-start(f32[32,8,128]{2,1,0:T(8,128)} %get-tuple-element.25), calls=%async_computation | async-start | bytes 262144 | tf_op jit(solution)/shard_map/all_to_all | solution.py:370
  15.0 0.0 copy-start
  15.0 1.0 copy-done
  16.0 1.3 shard_map.77
  17.3 6.8 %all-to-all-done.first_ref.meta_ref = f32[32,8,128]{2,1,0:T(8,128)S(1)} async-done(((f32[32,8,128]{2,1,0:T(8,128)}), f32[32,8,128]{2,1,0:T(8,128)S(1)}, u32[]{:S(2)}, u32[]{:S(2)}) %all-to-all-start) | async-done | bytes 131104 | tf_op jit(solution)/shard_map/all_to_all | solution.py:370
  24.1 11.9 %all_to_all.40.held_ref = f32[8,40,128]{2,1,0:T(8,128)S(1)} all-to-all(f32[8,40,128]{2,1,0:T(8,128)S(1)} %shard_map.78), channel_id=1, replica_groups=mesh['x'=4,'z'=8,'rows'=8] {'rows'}, dimensions={0} | all-to-all | bytes 327680 | tf_op jit(solution)/shard_map/all_to_all | solution.py:370
  36.1 0.3 shard_map.79
  36.3 12.5 %all_to_all.41.third_ref = f32[32,8,128]{2,1,0:T(8,128)S(1)} all-to-all(f32[32,8,128]{2,1,0:T(8,128)S(1)} %shard_map.79), channel_id=1, replica_groups=mesh['x'=4,'z'=8,'rows'=8] {'x','z'}, dimensions={0} | all-to-all | bytes 262144 | tf_op jit(solution)/shard_map/all_to_all | solution.py:370
  48.8 7.0 %shard_map.80 = (f32[6,32,64,128]{3,2,1,0:T(8,128)}, f32[32,8,128]{2,1,0:T(8,128)S(1)}, f32[128,128]{1,0:T(8,128)S(1)}) custom-call(s32[8,64]{1,0:T(8,128)S(1)} %get-tuple-element.24.place_ref, f32[6,64,4096]{2,1,0:T(8,128)} %blocks_ref.1, f32[32,8,128]{2,1,0:T(8,128)S(1)} %all_to_all.41.third_ref, f32[32,32,128]{2,1,0:T(8,128)S(1)} %get-tuple-element.27.pairs_ref), custom_call_target="tpu_custom_call" | custom-call | tf_op jit(solution)/shard_map/pallas_call | solution.py:401
  55.8 12.7 %all_to_all.42.part_ref = f32[32,8,128]{2,1,0:T(8,128)S(1)} all-to-all(f32[32,8,128]{2,1,0:T(8,128)S(1)} %get-tuple-element.29), channel_id=1, replica_groups=mesh['x'=4,'z'=8,'rows'=8] {'x','z'}, dimensions={0} | all-to-all | bytes 262144 | tf_op jit(solution)/shard_map/all_to_all | solution.py:370
  68.6 0.9 shard_map.81
  69.5 12.6 %all_to_all.43.first_ref = f32[32,8,128]{2,1,0:T(8,128)S(1)} all-to-all(f32[32,8,128]{2,1,0:T(8,128)S(1)} %get-tuple-element.31), channel_id=1, replica_groups=mesh['x'=4,'z'=8,'rows'=8] {'x','z'}, dimensions={0} | all-to-all | bytes 262144 | tf_op jit(solution)/shard_map/all_to_all | solution.py:370
  82.1 4.8 %collective-permute-start = (f32[8,128]{1,0:T(8,128)S(1)}, f32[8,128]{1,0:T(8,128)S(1)}, u32[]{:S(2)}, u32[]{:S(2)}) collective-permute-start(f32[8,128]{1,0:T(8,128)S(1)} %shard_map.82.square_ref), channel_id=1, source_target_pairs={{0,1},{1,0},{2,3},{3,2},{4,5},{5,4},{6,7},{7,6},{8,9},{9,8},{10,11... | collective-permute-start | bytes 12296 | tf_op jit(solution)/shard_map/ppermute | solution.py:419
  86.9 3.1 %shard_map.83 = (f32[32,8,128]{2,1,0:T(8,128)S(1)}, bf16[128,256]{1,0:T(8,128)(2,1)S(1)}) custom-call(f32[6,32,64,128]{3,2,1,0:T(8,128)} %get-tuple-element.28.folded_ref, f32[32,8,128]{2,1,0:T(8,128)S(1)} %all_to_all.43.first_ref, f32[32,8,128]{2,1,0:T(8,128)S(1)} %all-to-all-done.first_ref.meta_ref), custom_call_target="tpu_custom_call" | custom-call | tf_op jit(solution)/shard_map/pallas_call | solution.py:420
  90.0 0.0 collective-permute-done.other_ref
  90.0 12.4 %all_to_all.44.part_ref = f32[32,8,128]{2,1,0:T(8,128)S(1)} all-to-all(f32[32,8,128]{2,1,0:T(8,128)S(1)} %shard_map.84), channel_id=1, replica_groups=mesh['x'=4,'z'=8,'rows'=8] {'x','z'}, dimensions={0} | all-to-all | bytes 262144 | tf_op jit(solution)/shard_map/all_to_all | solution.py:370
  102.4 0.9 shard_map.85
  103.3 3.4 %all-to-all-start.6 = ((f32[8,64,128]{2,1,0:T(8,128)}), f32[8,64,128]{2,1,0:T(8,128)S(1)}, u32[]{:S(2)}, u32[]{:S(2)}) async-start(f32[8,64,128]{2,1,0:T(8,128)} %get-tuple-element.37), calls=%async_computation.6 | async-start | bytes 524288 | tf_op jit(solution)/shard_map/all_to_all | solution.py:370
  106.7 1.0 collective-permute-start.3
  107.7 1.2 collective-permute-start.2
  108.9 0.0 collective-permute-start.1
  108.9 0.5 collective-permute-done.3.three_ref
  109.4 2.4 %collective-permute-done.2.two_ref = f32[32,128]{1,0:T(8,128)S(1)} collective-permute-done((f32[32,128]{1,0:T(8,128)S(1)}, f32[32,128]{1,0:T(8,128)S(1)}, u32[]{:S(2)}, u32[]{:S(2)}) %collective-permute-start.2) | collective-permute-done | bytes 16416 | tf_op jit(solution)/shard_map/ppermute | solution.py:435
  111.8 0.9 collective-permute-done.1.one_ref
  112.7 4.9 %shard_map.86 = (f32[128,128]{1,0:T(8,128)S(1)}, f32[1,128]{1,0:T(1,128)S(1)}) custom-call(f32[32,128]{1,0:T(8,128)S(1)} %get-tuple-element.38.own_ref, f32[32,128]{1,0:T(8,128)S(1)} %collective-permute-done.1.one_ref, f32[32,128]{1,0:T(8,128)S(1)} %collective-permute-done.2.two_ref, f32[32,128]{1,0:T(8,128)S(1)} %collective-permute-done.3.three_ref, ...), custom_call_target="tpu_custom_call" | custom-call | tf_op jit(solution)/shard_map/pallas_call | solution.py:439
  117.6 0.0 all-to-all-done.6.near_ref
  117.6 0.9 shard_map.87
  118.5 0.9 collective-permute-start.6
  119.3 1.2 collective-permute-start.5
  120.6 0.0 collective-permute-start.4
  120.6 9.5 %all-to-all-start.7 = ((f32[32,1,128]{2,1,0:T(1,128)}), f32[32,1,128]{2,1,0:T(1,128)S(1)}, u32[]{:S(2)}, u32[]{:S(2)}) async-start(f32[32,1,128]{2,1,0:T(1,128)} %get-tuple-element.42), calls=%async_computation.7 | async-start | bytes 32768 | tf_op jit(solution)/shard_map/all_to_all | solution.py:370
  130.1 0.0 collective-permute-done.6.refs_3_
  130.1 0.0 collective-permute-done.5.refs_2_
  130.1 2.2 %collective-permute-done.4.refs_1_ = f32[8,64,128]{2,1,0:T(8,128)S(1)} collective-permute-done((f32[8,64,128]{2,1,0:T(8,128)S(1)}, f32[8,64,128]{2,1,0:T(8,128)S(1)}, u32[]{:S(2)}, u32[]{:S(2)}) %collective-permute-start.4) | collective-permute-done | bytes 262176 | tf_op jit(solution)/shard_map/ppermute | solution.py:442
  132.4 0.6 shard_map.89.turned_ref
  132.9 1.4 shard_map.88
  134.3 2.7 %all-to-all-done.7.square_ref = f32[32,1,128]{2,1,0:T(1,128)S(1)} async-done(((f32[32,1,128]{2,1,0:T(1,128)}), f32[32,1,128]{2,1,0:T(1,128)S(1)}, u32[]{:S(2)}, u32[]{:S(2)}) %all-to-all-start.7) | async-done | bytes 16416 | tf_op jit(solution)/shard_map/all_to_all | solution.py:370
  137.0 1.0 shard_map.90
  (4 shorter events, 0.1 us)
Async XLA Ops:
  3.1 21.0 %all-to-all-start = ((f32[32,8,128]{2,1,0:T(8,128)}), f32[32,8,128]{2,1,0:T(8,128)S(1)}, u32[]{:S(2)}, u32[]{:S(2)}) async-start(f32[32,8,128]{2,1,0:T(8,128)} %get-tuple-element.25), calls=%async_computation | async-start | bytes 262144 | tf_op jit(solution)/shard_map/all_to_all | solution.py:370
  15.0 1.0 copy-start
  82.1 7.9 %collective-permute-start = (f32[8,128]{1,0:T(8,128)S(1)}, f32[8,128]{1,0:T(8,128)S(1)}, u32[]{:S(2)}, u32[]{:S(2)}) collective-permute-start(f32[8,128]{1,0:T(8,128)S(1)} %shard_map.82.square_ref), channel_id=1, source_target_pairs={{0,1},{1,0},{2,3},{3,2},{4,5},{5,4},{6,7},{7,6},{8,9},{9,8},{10,11... | collective-permute-start | bytes 12296 | tf_op jit(solution)/shard_map/ppermute | solution.py:419
  103.3 14.3 %all-to-all-start.6 = ((f32[8,64,128]{2,1,0:T(8,128)}), f32[8,64,128]{2,1,0:T(8,128)S(1)}, u32[]{:S(2)}, u32[]{:S(2)}) async-start(f32[8,64,128]{2,1,0:T(8,128)} %get-tuple-element.37), calls=%async_computation.6 | async-start | bytes 524288 | tf_op jit(solution)/shard_map/all_to_all | solution.py:370
  106.7 2.7 %collective-permute-start.3 = (f32[32,128]{1,0:T(8,128)S(1)}, f32[32,128]{1,0:T(8,128)S(1)}, u32[]{:S(2)}, u32[]{:S(2)}) collective-permute-start(f32[32,128]{1,0:T(8,128)S(1)} %get-tuple-element.38.own_ref), channel_id=1, source_target_pairs={{0,6},{1,7},{2,0},{3,1},{4,2},{5,3},{6,4},{7,5},{8,14},{9,15},{10,... | collective-permute-start | bytes 49160 | tf_op jit(solution)/shard_map/ppermute | solution.py:435
  107.7 4.1 %collective-permute-start.2 = (f32[32,128]{1,0:T(8,128)S(1)}, f32[32,128]{1,0:T(8,128)S(1)}, u32[]{:S(2)}, u32[]{:S(2)}) collective-permute-start(f32[32,128]{1,0:T(8,128)S(1)} %get-tuple-element.38.own_ref), channel_id=1, source_target_pairs={{0,4},{1,5},{2,6},{3,7},{4,0},{5,1},{6,2},{7,3},{8,12},{9,13},{10,... | collective-permute-start | bytes 49160 | tf_op jit(solution)/shard_map/ppermute | solution.py:435
  108.9 3.8 %collective-permute-start.1 = (f32[32,128]{1,0:T(8,128)S(1)}, f32[32,128]{1,0:T(8,128)S(1)}, u32[]{:S(2)}, u32[]{:S(2)}) collective-permute-start(f32[32,128]{1,0:T(8,128)S(1)} %get-tuple-element.38.own_ref), channel_id=1, source_target_pairs={{0,2},{1,3},{2,4},{3,5},{4,6},{5,7},{6,0},{7,1},{8,10},{9,11},{10,... | collective-permute-start | bytes 49160 | tf_op jit(solution)/shard_map/ppermute | solution.py:435
  118.5 11.7 %collective-permute-start.6 = (f32[8,64,128]{2,1,0:T(8,128)S(1)}, f32[8,64,128]{2,1,0:T(8,128)S(1)}, u32[]{:S(2)}, u32[]{:S(2)}) collective-permute-start(f32[8,64,128]{2,1,0:T(8,128)S(1)} %get-tuple-element.41.refs_0_), channel_id=1, source_target_pairs={{0,192},{64,0},{128,64},{192,128},{1,193},{65,1},{129,65},{193,129... | collective-permute-start | bytes 786440 | tf_op jit(solution)/shard_map/ppermute | solution.py:442
  119.3 10.8 %collective-permute-start.5 = (f32[8,64,128]{2,1,0:T(8,128)S(1)}, f32[8,64,128]{2,1,0:T(8,128)S(1)}, u32[]{:S(2)}, u32[]{:S(2)}) collective-permute-start(f32[8,64,128]{2,1,0:T(8,128)S(1)} %get-tuple-element.41.refs_0_), channel_id=1, source_target_pairs={{0,128},{64,192},{128,0},{192,64},{1,129},{65,193},{129,1},{193,65... | collective-permute-start | bytes 786440 | tf_op jit(solution)/shard_map/ppermute | solution.py:442
  120.6 11.8 %collective-permute-start.4 = (f32[8,64,128]{2,1,0:T(8,128)S(1)}, f32[8,64,128]{2,1,0:T(8,128)S(1)}, u32[]{:S(2)}, u32[]{:S(2)}) collective-permute-start(f32[8,64,128]{2,1,0:T(8,128)S(1)} %get-tuple-element.41.refs_0_), channel_id=1, source_target_pairs={{0,64},{64,128},{128,192},{192,0},{1,65},{65,129},{129,193},{193,1... | collective-permute-start | bytes 786440 | tf_op jit(solution)/shard_map/ppermute | solution.py:442
  120.6 16.4 %all-to-all-start.7 = ((f32[32,1,128]{2,1,0:T(1,128)}), f32[32,1,128]{2,1,0:T(1,128)S(1)}, u32[]{:S(2)}, u32[]{:S(2)}) async-start(f32[32,1,128]{2,1,0:T(1,128)} %get-tuple-element.42), calls=%async_computation.7 | async-start | bytes 32768 | tf_op jit(solution)/shard_map/all_to_all | solution.py:370

commit v8 on v7

--- a/solution.py
+++ b/solution.py
@@ -79,15 +79,18 @@
 
 
 def eliminate_all(work):
-    row = lax.broadcasted_iota(jnp.int32, work.shape, 0)
-    ratio = 1.0 / spot(work, 0, 0)
+    row = lax.broadcasted_iota(jnp.int32, (TILE, WIDE), 0)
+    tiles = [work[n * TILE : (n + 1) * TILE] for n in range(SIDE // TILE)]
+    ratio = 1.0 / spot(tiles[0], 0, 0)
     for k in range(SIDE):
-        line = jnp.broadcast_to(work[k : k + 1, :], (TILE, WIDE)) * ratio
+        at, inner = divmod(k, TILE)
+        line = jnp.broadcast_to(tiles[at][inner : inner + 1, :], (TILE, WIDE)) * ratio
         if k + 1 < SIDE:
-            ratio = 1.0 / (spot(work, k + 1, k + 1) - spot(work, k + 1, k) * (spot(work, k, k + 1) * ratio))
-        line = jnp.broadcast_to(line[None], (TILE, TILE, WIDE)).reshape(work.shape)
-        work = jnp.where(row == k, line, work - work[:, k : k + 1] * line)
-    return work
+            beside, later = spot(tiles[at], inner, k + 1), divmod(k + 1, TILE)
+            ratio = 1.0 / (spot(tiles[later[0]], later[1], k + 1) - beside * (beside * ratio))
+        tiles = [tile - tile[:, k : k + 1] * line for tile in tiles]
+        tiles[at] = jnp.where(row == inner, line, tiles[at])
+    return jnp.concatenate(tiles, axis=0)
 
 
 def end_inverse(work):
@@ -415,7 +418,7 @@
     part_a = exchange(part_a, SLAB)
     answer_a, solved_a = call(solve_first, struct(*small), struct(HALF, WIDE))(part_a, meta, inverse_a)
     first = exchange(answer_a, SLAB)
-    first, square_a = lax.optimization_barrier((first, call(share_gram, struct(TILE, WIDE))(first)))
+    first, square_a = lax.optimization_barrier((first, call(share_gram, struct(1, WIDE))(first)))
     other_a = lax.ppermute(square_a, "rows", [(n, n ^ 1) for n in range(PEERS)])
     part_b, turned = pl.pallas_call(
         contract,

time: 139 us -> 139 us (level)
  no operation moved by 1% of the time
where the time goes in v8:
time: 139 us; the launch traced here: 138 us
  blocking collectives  62.2 us (45%)
  starting transfers between devices  33.9 us (24%)
  Pallas kernels  23 us (17%)
  waiting for transfers between devices  15.6 us (11%)
  between operations  1.42 us (1%)
    all_to_all x5, blocking collectives, exchange(): return lax.all_to_all(x, axis, 0, 0, tiled=True)  62.2 us
    all_to_all x3, starting transfers between devices, exchange(): return lax.all_to_all(x, axis, 0, 0, tiled=True)  24.8 us
    all_to_all x3, waiting for transfers between devices, exchange(): return lax.all_to_all(x, axis, 0, 0, tiled=True)  9.56 us
    pallas_call x1, Pallas kernels, shards(): pl.pallas_call(fold, in_specs=[scalars, apart, local, local], out_specs=[...  7.03 us
    pallas_call x1, Pallas kernels, shards(): call(invert_second, struct(WIDE, WIDE), struct(1, WIDE))(*squares_a, third)  4.84 us
    ppermute x1, starting transfers between devices, shards(): other_a = lax.ppermute(square_a, 'rows', [(n, n ^ 1) for n in range(PEERS)])  4.76 us
    ppermute x3, waiting for transfers between devices, shards(): lax.ppermute(square_a, 'rows', [(n, (n + 2 * step) % PEERS) for n in rang...  3.8 us
    pallas_call x1, Pallas kernels, shards(): pl.pallas_call(contract, in_specs=[apart, local, local], out_specs=[local...  3.09 us
  transfers between devices with their start and end apart: 10, of which 6 were waited for; matrix products, arithmetic and copies ran while one was open for 0% of the time, Pallas kernels for 8%

profile of v8, /device:TPU:1, one launch (start us, length us, event | category | flops | bytes accessed | tf_op | source)
XLA Modules:
  0.0 138.0 jit_solution(6131562827712371435)
XLA Ops:
  1.3 0.9 fusion.given_ref
  2.2 0.9 shard_map.76
  3.1 11.9 %all-to-all-start = ((f32[32,8,128]{2,1,0:T(8,128)}), f32[32,8,128]{2,1,0:T(8,128)S(1)}, u32[]{:S(2)}, u32[]{:S(2)}) async-start(f32[32,8,128]{2,1,0:T(8,128)} %get-tuple-element.25), calls=%async_computation | async-start | bytes 262144 | tf_op jit(solution)/shard_map/all_to_all | solution.py:373
  15.0 0.0 copy-start
  15.0 1.0 copy-done
  16.0 1.3 shard_map.77
  17.3 6.8 %all-to-all-done.first_ref.meta_ref = f32[32,8,128]{2,1,0:T(8,128)S(1)} async-done(((f32[32,8,128]{2,1,0:T(8,128)}), f32[32,8,128]{2,1,0:T(8,128)S(1)}, u32[]{:S(2)}, u32[]{:S(2)}) %all-to-all-start) | async-done | bytes 131104 | tf_op jit(solution)/shard_map/all_to_all | solution.py:373
  24.1 11.9 %all_to_all.40.held_ref = f32[8,40,128]{2,1,0:T(8,128)S(1)} all-to-all(f32[8,40,128]{2,1,0:T(8,128)S(1)} %shard_map.78), channel_id=1, replica_groups=mesh['x'=4,'z'=8,'rows'=8] {'rows'}, dimensions={0} | all-to-all | bytes 327680 | tf_op jit(solution)/shard_map/all_to_all | solution.py:373
  36.1 0.3 shard_map.79
  36.3 12.5 %all_to_all.41.third_ref = f32[32,8,128]{2,1,0:T(8,128)S(1)} all-to-all(f32[32,8,128]{2,1,0:T(8,128)S(1)} %shard_map.79), channel_id=1, replica_groups=mesh['x'=4,'z'=8,'rows'=8] {'x','z'}, dimensions={0} | all-to-all | bytes 262144 | tf_op jit(solution)/shard_map/all_to_all | solution.py:373
  48.8 7.0 %shard_map.80 = (f32[6,32,64,128]{3,2,1,0:T(8,128)}, f32[32,8,128]{2,1,0:T(8,128)S(1)}, f32[128,128]{1,0:T(8,128)S(1)}) custom-call(s32[8,64]{1,0:T(8,128)S(1)} %get-tuple-element.24.place_ref, f32[6,64,4096]{2,1,0:T(8,128)} %blocks_ref.1, f32[32,8,128]{2,1,0:T(8,128)S(1)} %all_to_all.41.third_ref, f32[32,32,128]{2,1,0:T(8,128)S(1)} %get-tuple-element.27.pairs_ref), custom_call_target="tpu_custom_call" | custom-call | tf_op jit(solution)/shard_map/pallas_call | solution.py:404
  55.8 12.7 %all_to_all.42.part_ref = f32[32,8,128]{2,1,0:T(8,128)S(1)} all-to-all(f32[32,8,128]{2,1,0:T(8,128)S(1)} %get-tuple-element.29), channel_id=1, replica_groups=mesh['x'=4,'z'=8,'rows'=8] {'x','z'}, dimensions={0} | all-to-all | bytes 262144 | tf_op jit(solution)/shard_map/all_to_all | solution.py:373
  68.6 0.9 shard_map.81
  69.5 12.6 %all_to_all.43.first_ref = f32[32,8,128]{2,1,0:T(8,128)S(1)} all-to-all(f32[32,8,128]{2,1,0:T(8,128)S(1)} %get-tuple-element.31), channel_id=1, replica_groups=mesh['x'=4,'z'=8,'rows'=8] {'x','z'}, dimensions={0} | all-to-all | bytes 262144 | tf_op jit(solution)/shard_map/all_to_all | solution.py:373
  82.1 4.8 %collective-permute-start = (f32[1,128]{1,0:T(1,128)S(1)}, f32[1,128]{1,0:T(1,128)S(1)}, u32[]{:S(2)}, u32[]{:S(2)}) collective-permute-start(f32[1,128]{1,0:T(1,128)S(1)} %shard_map.82.square_ref), channel_id=1, source_target_pairs={{0,1},{1,0},{2,3},{3,2},{4,5},{5,4},{6,7},{7,6},{8,9},{9,8},{10,11... | collective-permute-start | bytes 1544 | tf_op jit(solution)/shard_map/ppermute | solution.py:422
  86.9 3.1 %shard_map.83 = (f32[32,8,128]{2,1,0:T(8,128)S(1)}, bf16[128,256]{1,0:T(8,128)(2,1)S(1)}) custom-call(f32[6,32,64,128]{3,2,1,0:T(8,128)} %get-tuple-element.28.folded_ref, f32[32,8,128]{2,1,0:T(8,128)S(1)} %all_to_all.43.first_ref, f32[32,8,128]{2,1,0:T(8,128)S(1)} %all-to-all-done.first_ref.meta_ref), custom_call_target="tpu_custom_call" | custom-call | tf_op jit(solution)/shard_map/pallas_call | solution.py:423
  90.0 0.0 collective-permute-done.other_ref
  90.0 12.4 %all_to_all.44.part_ref = f32[32,8,128]{2,1,0:T(8,128)S(1)} all-to-all(f32[32,8,128]{2,1,0:T(8,128)S(1)} %shard_map.84), channel_id=1, replica_groups=mesh['x'=4,'z'=8,'rows'=8] {'x','z'}, dimensions={0} | all-to-all | bytes 262144 | tf_op jit(solution)/shard_map/all_to_all | solution.py:373
  102.4 0.9 shard_map.85
  103.3 3.4 %all-to-all-start.6 = ((f32[8,64,128]{2,1,0:T(8,128)}), f32[8,64,128]{2,1,0:T(8,128)S(1)}, u32[]{:S(2)}, u32[]{:S(2)}) async-start(f32[8,64,128]{2,1,0:T(8,128)} %get-tuple-element.37), calls=%async_computation.6 | async-start | bytes 524288 | tf_op jit(solution)/shard_map/all_to_all | solution.py:373
  106.7 1.0 collective-permute-start.3
  107.7 1.2 collective-permute-start.2
  108.9 0.0 collective-permute-start.1
  108.9 0.5 collective-permute-done.3.three_ref
  109.4 2.4 %collective-permute-done.2.two_ref = f32[32,128]{1,0:T(8,128)S(1)} collective-permute-done((f32[32,128]{1,0:T(8,128)S(1)}, f32[32,128]{1,0:T(8,128)S(1)}, u32[]{:S(2)}, u32[]{:S(2)}) %collective-permute-start.2) | collective-permute-done | bytes 16416 | tf_op jit(solution)/shard_map/ppermute | solution.py:438
  111.8 0.9 collective-permute-done.1.one_ref
  112.7 4.8 %shard_map.86 = (f32[128,128]{1,0:T(8,128)S(1)}, f32[1,128]{1,0:T(1,128)S(1)}) custom-call(f32[32,128]{1,0:T(8,128)S(1)} %get-tuple-element.38.own_ref, f32[32,128]{1,0:T(8,128)S(1)} %collective-permute-done.1.one_ref, f32[32,128]{1,0:T(8,128)S(1)} %collective-permute-done.2.two_ref, f32[32,128]{1,0:T(8,128)S(1)} %collective-permute-done.3.three_ref, ...), custom_call_target="tpu_custom_call" | custom-call | tf_op jit(solution)/shard_map/pallas_call | solution.py:442
  117.5 0.0 all-to-all-done.6.near_ref
  117.5 0.9 shard_map.87
  118.4 0.9 collective-permute-start.6
  119.3 1.2 collective-permute-start.5
  120.5 0.0 collective-permute-start.4
  120.5 9.5 %all-to-all-start.7 = ((f32[32,1,128]{2,1,0:T(1,128)}), f32[32,1,128]{2,1,0:T(1,128)S(1)}, u32[]{:S(2)}, u32[]{:S(2)}) async-start(f32[32,1,128]{2,1,0:T(1,128)} %get-tuple-element.42), calls=%async_computation.7 | async-start | bytes 32768 | tf_op jit(solution)/shard_map/all_to_all | solution.py:373
  130.1 0.0 collective-permute-done.6.refs_3_
  130.1 0.0 collective-permute-done.5.refs_2_
  130.1 2.2 %collective-permute-done.4.refs_1_ = f32[8,64,128]{2,1,0:T(8,128)S(1)} collective-permute-done((f32[8,64,128]{2,1,0:T(8,128)S(1)}, f32[8,64,128]{2,1,0:T(8,128)S(1)}, u32[]{:S(2)}, u32[]{:S(2)}) %collective-permute-start.4) | collective-permute-done | bytes 262176 | tf_op jit(solution)/shard_map/ppermute | solution.py:445
  132.3 0.6 shard_map.89.turned_ref
  132.9 1.4 shard_map.88
  134.2 2.7 %all-to-all-done.7.square_ref = f32[32,1,128]{2,1,0:T(1,128)S(1)} async-done(((f32[32,1,128]{2,1,0:T(1,128)}), f32[32,1,128]{2,1,0:T(1,128)S(1)}, u32[]{:S(2)}, u32[]{:S(2)}) %all-to-all-start.7) | async-done | bytes 16416 | tf_op jit(solution)/shard_map/all_to_all | solution.py:373
  136.9 1.0 shard_map.90
  (4 shorter events, 0.1 us)
Async XLA Ops:
  3.1 21.0 %all-to-all-start = ((f32[32,8,128]{2,1,0:T(8,128)}), f32[32,8,128]{2,1,0:T(8,128)S(1)}, u32[]{:S(2)}, u32[]{:S(2)}) async-start(f32[32,8,128]{2,1,0:T(8,128)} %get-tuple-element.25), calls=%async_computation | async-start | bytes 262144 | tf_op jit(solution)/shard_map/all_to_all | solution.py:373
  15.0 1.0 copy-start
  82.1 7.9 %collective-permute-start = (f32[1,128]{1,0:T(1,128)S(1)}, f32[1,128]{1,0:T(1,128)S(1)}, u32[]{:S(2)}, u32[]{:S(2)}) collective-permute-start(f32[1,128]{1,0:T(1,128)S(1)} %shard_map.82.square_ref), channel_id=1, source_target_pairs={{0,1},{1,0},{2,3},{3,2},{4,5},{5,4},{6,7},{7,6},{8,9},{9,8},{10,11... | collective-permute-start | bytes 1544 | tf_op jit(solution)/shard_map/ppermute | solution.py:422
  103.3 14.2 %all-to-all-start.6 = ((f32[8,64,128]{2,1,0:T(8,128)}), f32[8,64,128]{2,1,0:T(8,128)S(1)}, u32[]{:S(2)}, u32[]{:S(2)}) async-start(f32[8,64,128]{2,1,0:T(8,128)} %get-tuple-element.37), calls=%async_computation.6 | async-start | bytes 524288 | tf_op jit(solution)/shard_map/all_to_all | solution.py:373
  106.7 2.7 %collective-permute-start.3 = (f32[32,128]{1,0:T(8,128)S(1)}, f32[32,128]{1,0:T(8,128)S(1)}, u32[]{:S(2)}, u32[]{:S(2)}) collective-permute-start(f32[32,128]{1,0:T(8,128)S(1)} %get-tuple-element.38.own_ref), channel_id=1, source_target_pairs={{0,6},{1,7},{2,0},{3,1},{4,2},{5,3},{6,4},{7,5},{8,14},{9,15},{10,... | collective-permute-start | bytes 49160 | tf_op jit(solution)/shard_map/ppermute | solution.py:438
  107.7 4.1 %collective-permute-start.2 = (f32[32,128]{1,0:T(8,128)S(1)}, f32[32,128]{1,0:T(8,128)S(1)}, u32[]{:S(2)}, u32[]{:S(2)}) collective-permute-start(f32[32,128]{1,0:T(8,128)S(1)} %get-tuple-element.38.own_ref), channel_id=1, source_target_pairs={{0,4},{1,5},{2,6},{3,7},{4,0},{5,1},{6,2},{7,3},{8,12},{9,13},{10,... | collective-permute-start | bytes 49160 | tf_op jit(solution)/shard_map/ppermute | solution.py:438
  108.9 3.8 %collective-permute-start.1 = (f32[32,128]{1,0:T(8,128)S(1)}, f32[32,128]{1,0:T(8,128)S(1)}, u32[]{:S(2)}, u32[]{:S(2)}) collective-permute-start(f32[32,128]{1,0:T(8,128)S(1)} %get-tuple-element.38.own_ref), channel_id=1, source_target_pairs={{0,2},{1,3},{2,4},{3,5},{4,6},{5,7},{6,0},{7,1},{8,10},{9,11},{10,... | collective-permute-start | bytes 49160 | tf_op jit(solution)/shard_map/ppermute | solution.py:438
  118.4 11.7 %collective-permute-start.6 = (f32[8,64,128]{2,1,0:T(8,128)S(1)}, f32[8,64,128]{2,1,0:T(8,128)S(1)}, u32[]{:S(2)}, u32[]{:S(2)}) collective-permute-start(f32[8,64,128]{2,1,0:T(8,128)S(1)} %get-tuple-element.41.refs_0_), channel_id=1, source_target_pairs={{0,192},{64,0},{128,64},{192,128},{1,193},{65,1},{129,65},{193,129... | collective-permute-start | bytes 786440 | tf_op jit(solution)/shard_map/ppermute | solution.py:445
  119.3 10.8 %collective-permute-start.5 = (f32[8,64,128]{2,1,0:T(8,128)S(1)}, f32[8,64,128]{2,1,0:T(8,128)S(1)}, u32[]{:S(2)}, u32[]{:S(2)}) collective-permute-start(f32[8,64,128]{2,1,0:T(8,128)S(1)} %get-tuple-element.41.refs_0_), channel_id=1, source_target_pairs={{0,128},{64,192},{128,0},{192,64},{1,129},{65,193},{129,1},{193,65... | collective-permute-start | bytes 786440 | tf_op jit(solution)/shard_map/ppermute | solution.py:445
  120.5 11.8 %collective-permute-start.4 = (f32[8,64,128]{2,1,0:T(8,128)S(1)}, f32[8,64,128]{2,1,0:T(8,128)S(1)}, u32[]{:S(2)}, u32[]{:S(2)}) collective-permute-start(f32[8,64,128]{2,1,0:T(8,128)S(1)} %get-tuple-element.41.refs_0_), channel_id=1, source_target_pairs={{0,64},{64,128},{128,192},{192,0},{1,65},{65,129},{129,193},{193,1... | collective-permute-start | bytes 786440 | tf_op jit(solution)/shard_map/ppermute | solution.py:445
  120.5 16.4 %all-to-all-start.7 = ((f32[32,1,128]{2,1,0:T(1,128)}), f32[32,1,128]{2,1,0:T(1,128)S(1)}, u32[]{:S(2)}, u32[]{:S(2)}) async-start(f32[32,1,128]{2,1,0:T(1,128)} %get-tuple-element.42), calls=%async_computation.7 | async-start | bytes 32768 | tf_op jit(solution)/shard_map/all_to_all | solution.py:373
